TPU v7x, 32 devices: a whole 2x2x4 slice. The times are simulated.
32 devices in a mesh: dp: 2 (over y), row: 4 (over x, core), col: 4 (over z).
Axes of the slice: x: 2, y: 2, z: 4, core: 2. Of those that a mesh axis runs over, the one named last changes fastest.
Arguments:
- layer_input: bfloat16 [4096, 2048], P(('dp', 'row'), 'col'), may hold values from -40 to 40
- segment_ids: int32 [4096], P('dp'), may hold values from 0 to 2, as said below
- positions: int32 [4096], P('dp'), may hold values from 0 to 2047, as said below
- norm_gain: float32 [2, 2048], P(None, 'col'), may hold values from 0.25 to 1.75
- norm_bias: float32 [2, 2048], P(None, 'col'), may hold values from -4 to 4
- qkv_weight: bfloat16 [2, 2048, 3, 2048], P(None, ('dp', 'row'), None, 'col'), may hold values from -0.125 to 0.125
- qkv_bias: float32 [2, 3, 2048], P(None, None, 'col'), may hold values from -4 to 4
- dense_weight: bfloat16 [2, 2048, 2048], P(None, 'col', ('dp', 'row')), may hold values from -1.75 to 1.75
- dense_bias: float32 [2, 2048], P(None, 'col'), may hold values from -4 to 4
- up_weight: bfloat16 [2, 2048, 8192], P(None, ('dp', 'row'), 'col'), may hold values from -0.125 to 0.125
- up_bias: float32 [2, 8192], P(None, 'col'), may hold values from -4 to 4
- down_weight: bfloat16 [2, 8192, 2048], P(None, 'col', ('dp', 'row')), may hold values from -0.0625 to 0.0625
- down_bias: float32 [2, 2048], P(None, 'col'), may hold values from -4 to 4
- output_cotangent: bfloat16 [4096, 2048], P(('dp', 'row'), 'col'), may hold values from -4 to 4
Outputs:
- layer_outputs: float32 [2, 4096, 2048], P(None, ('dp', 'row'), 'col')
- input_gradient: float32 [4096, 2048], P(('dp', 'row'), 'col')
- norm_gain_gradient: float32 [2, 2048], P(None, 'col')
- norm_bias_gradient: float32 [2, 2048], P(None, 'col')
- qkv_weight_gradient: float32 [2, 2048, 3, 2048], P(None, ('dp', 'row'), None, 'col')
- qkv_bias_gradient: float32 [2, 3, 2048], P(None, None, 'col')
- dense_weight_gradient: float32 [2, 2048, 2048], P(None, 'col', ('dp', 'row'))
- dense_bias_gradient: float32 [2, 2048], P(None, 'col')
- up_weight_gradient: float32 [2, 2048, 8192], P(None, ('dp', 'row'), 'col')
- up_bias_gradient: float32 [2, 8192], P(None, 'col')
- down_weight_gradient: float32 [2, 8192, 2048], P(None, 'col', ('dp', 'row'))
- down_bias_gradient: float32 [2, 2048], P(None, 'col')
Inputs may be any that keep to these rules, and one draw needn't show every extreme that they name: `segment_ids`: each index of dp holds one sequence of 2048 tokens in three documents numbered 0, 1, 2 in order; document 0 ends within the sequence's first 512 tokens and document 2 begins within its last 512 tokens. `positions`: within a document the position rises by one from token to token; document 1 starts at 0 and document 2 ends at 2047.
All inputs are finite; a program needn't handle non-finite values.
Results may differ from a plain program's by a relative error of at most 0.014.
Values may be sent and summed in bfloat16 or wider, within the bound.
No kernel may reach another device: no remote copies, remote signals or barrier semaphores. Data moves between devices by JAX's collectives and lax.ppermute only.
A program may use at most 256 MiB of HBM per device.

v0:
```python
import math

import jax
import jax.numpy as jnp
from jax import lax
from jax.sharding import PartitionSpec as P

HEAD_DIM = 64
ROT = 32


EPSILON = 1e-05
NEGATIVE = -1e30


def gelu_curve(values):
    return jax.nn.gelu(values, approximate=True)


def rotation_tables(place_values):
    half_width = ROT // 2
    freq_table = 1.0 / 10000.0 ** (jnp.arange(half_width, dtype=jnp.float32) * 2.0 / ROT)
    angles = place_values.astype(jnp.float32)[:, None] * freq_table
    return (jnp.cos(angles)[:, None, :], jnp.sin(angles)[:, None, :])


def rotate(tensor, cosine_table, sine_table):
    half_width = cosine_table.shape[-1]
    rotary = 2 * half_width
    first_half = tensor[..., :half_width]
    second_half = tensor[..., half_width:rotary]
    return jnp.concatenate(
        [
            first_half * cosine_table - second_half * sine_table,
            second_half * cosine_table + first_half * sine_table,
            tensor[..., rotary:],
        ],
        axis=-1,
    )


def rotate_back(tensor, cosine_table, sine_table):
    half_width = cosine_table.shape[-1]
    rotary = 2 * half_width
    first_half = tensor[..., :half_width]
    second_half = tensor[..., half_width:rotary]
    return jnp.concatenate(
        [
            first_half * cosine_table + second_half * sine_table,
            second_half * cosine_table - first_half * sine_table,
            tensor[..., rotary:],
        ],
        axis=-1,
    )


def key_slices(key_rows, value_rows, key_segments, key_begin, block_size):
    return (
        lax.dynamic_slice_in_dim(key_rows, key_begin, block_size, 0),
        lax.dynamic_slice_in_dim(value_rows, key_begin, block_size, 0),
        lax.dynamic_slice_in_dim(key_segments, key_begin, block_size, 0),
    )


def block_scores(queries, key_block, query_segments, segment_block, query_begin, key_begin):
    token_count, head_count, head_size = queries.shape
    block_size = key_block.shape[0]
    shaped_keys = key_block.reshape(block_size, head_count, head_size)
    scores = jnp.einsum(
        "qhe,khe->hqk", queries, shaped_keys, preferred_element_type=jnp.float32
    ) * head_size ** (-0.5)
    query_place = query_begin + jnp.arange(token_count, dtype=jnp.int32)
    key_place = key_begin + jnp.arange(block_size, dtype=jnp.int32)
    allowed = (key_place[None, :] <= query_place[:, None]) & (
        query_segments[:, None] == segment_block[None, :]
    )
    return (scores, allowed[None], shaped_keys)


def attend_forward(queries, key_rows, value_rows, query_segments, key_segments, query_begin):
    token_count, head_count, head_size = queries.shape
    block_size = math.gcd(key_rows.shape[0], 512)
    limit = (query_begin + token_count - 1) // block_size + 1

    def first_pass(index, running):
        running_top, running_total = running
        key_begin = index * block_size
        key_block, value_block, segment_block = key_slices(
            key_rows, value_rows, key_segments, key_begin, block_size
        )
        scores, allowed, unused = block_scores(
            queries, key_block, query_segments, segment_block, query_begin, key_begin
        )
        masked = jnp.where(allowed, scores, NEGATIVE)
        new_top = jnp.maximum(running_top, jnp.max(masked, axis=-1))
        exp_terms = jnp.where(allowed, jnp.exp(masked - new_top[..., None]), 0.0)
        running_total = running_total * jnp.exp(running_top - new_top) + jnp.sum(exp_terms, axis=-1)
        return (new_top, running_total)

    initial = (
        jnp.full((head_count, token_count), NEGATIVE, jnp.float32),
        jnp.zeros((head_count, token_count), jnp.float32),
    )
    running_top, running_total = lax.fori_loop(0, limit, first_pass, initial)
    log_total = running_top + jnp.log(running_total)

    def second_pass(index, accumulated):
        key_begin = index * block_size
        key_block, value_block, segment_block = key_slices(
            key_rows, value_rows, key_segments, key_begin, block_size
        )
        scores, allowed, unused = block_scores(
            queries, key_block, query_segments, segment_block, query_begin, key_begin
        )
        exact = jnp.where(allowed, jnp.exp(scores - log_total[..., None]), 0.0)
        shaped_values = value_block.reshape(block_size, head_count, head_size)
        return accumulated + jnp.einsum(
            "hqk,khe->qhe",
            exact.astype(jnp.bfloat16),
            shaped_values,
            preferred_element_type=jnp.float32,
        )

    mixed_sum = lax.fori_loop(
        0, limit, second_pass, jnp.zeros((token_count, head_count, head_size), jnp.float32)
    )
    return (mixed_sum, log_total)


def attend_backward(
    queries, key_rows, value_rows, query_segments, key_segments, query_begin, log_total, mixed_grad
):
    token_count, head_count, head_size = queries.shape
    total_keys = key_rows.shape[0]
    block_size = math.gcd(total_keys, 512)
    limit = (query_begin + token_count - 1) // block_size + 1
    score_scale = head_size ** (-0.5)

    def weights_at(key_begin):
        key_block, value_block, segment_block = key_slices(
            key_rows, value_rows, key_segments, key_begin, block_size
        )
        scores, allowed, shaped_keys = block_scores(
            queries, key_block, query_segments, segment_block, query_begin, key_begin
        )
        shaped_values = value_block.reshape(block_size, head_count, head_size)
        exact = jnp.where(allowed, jnp.exp(scores - log_total[..., None]), 0.0)
        weight_grad = jnp.einsum(
            "qhe,khe->hqk", mixed_grad, shaped_values, preferred_element_type=jnp.float32
        )
        return (exact, weight_grad, shaped_keys)

    def delta_pass(index, accumulated):
        exact, weight_grad, unused = weights_at(index * block_size)
        return accumulated + jnp.sum(exact * weight_grad, axis=-1)

    row_delta = lax.fori_loop(
        0, limit, delta_pass, jnp.zeros((head_count, token_count), jnp.float32)
    )

    def gradient_pass(index, carried):
        key_begin = index * block_size
        exact, weight_grad, shaped_keys = weights_at(key_begin)
        score_grad = (exact * (weight_grad - row_delta[..., None])).astype(jnp.bfloat16)
        query_grad = carried[0] + jnp.einsum(
            "hqk,khe->qhe", score_grad, shaped_keys, preferred_element_type=jnp.float32
        )
        key_grad = (
            jnp.einsum("hqk,qhe->khe", score_grad, queries, preferred_element_type=jnp.float32)
            * score_scale
        )
        value_grad = jnp.einsum(
            "hqk,qhe->khe",
            exact.astype(jnp.bfloat16),
            mixed_grad,
            preferred_element_type=jnp.float32,
        )
        return (
            query_grad,
            lax.dynamic_update_slice_in_dim(carried[1], key_grad, key_begin, 0),
            lax.dynamic_update_slice_in_dim(carried[2], value_grad, key_begin, 0),
        )

    query_zero = jnp.zeros((token_count, head_count, head_size), jnp.float32)
    key_zero = jnp.zeros((total_keys, head_count, head_size), jnp.float32)
    query_grad, key_grads, value_grads = lax.fori_loop(
        0, limit, gradient_pass, (query_zero, key_zero, key_zero)
    )
    return (
        query_grad * score_scale,
        row_delta,
        key_grads.reshape(total_keys, head_count * head_size),
        value_grads.reshape(total_keys, head_count * head_size),
    )


def per_device(
    layer_input,
    segment_ids,
    positions,
    norm_gain,
    norm_bias,
    qkv_weight,
    qkv_bias,
    dense_weight,
    dense_bias,
    up_weight,
    up_bias,
    down_weight,
    down_bias,
    output_cotangent,
):
    token_count = layer_input.shape[0]
    full_width = layer_input.shape[1] * lax.axis_size("col")
    layer_count = qkv_weight.shape[0]
    query_begin = lax.axis_index("row") * token_count
    query_segments = lax.dynamic_slice_in_dim(segment_ids, query_begin, token_count, 0)
    query_places = lax.dynamic_slice_in_dim(positions, query_begin, token_count, 0)
    cosine_table, sine_table = rotation_tables(query_places)
    residual = layer_input.astype(jnp.float32)
    outputs = []
    kept_values = []
    for layer_index in range(layer_count):
        gathered = (
            lax.all_gather(qkv_weight[layer_index], ("dp", "row"), axis=0, tiled=True),
            lax.all_gather(up_weight[layer_index], ("dp", "row"), axis=0, tiled=True),
            lax.all_gather(dense_weight[layer_index], ("dp", "row"), axis=1, tiled=True),
            lax.all_gather(down_weight[layer_index], ("dp", "row"), axis=1, tiled=True),
        )
        feature_sum, squares = lax.psum(
            (jnp.sum(residual, axis=1), jnp.sum(residual * residual, axis=1)), "col"
        )
        center = feature_sum / full_width
        inverse = lax.rsqrt(squares / full_width - center * center + EPSILON)
        centred = (residual - center[:, None]) * inverse[:, None]
        normed = (centred * norm_gain[layer_index] + norm_bias[layer_index]).astype(jnp.bfloat16)
        features = lax.all_gather(normed, "col", axis=1, tiled=True)
        gathered_qkv, gathered_up, gathered_dense, gathered_down = gathered
        column_width = gathered_qkv.shape[2]
        head_count = column_width // HEAD_DIM
        flat_qkv = gathered_qkv.reshape(gathered_qkv.shape[0], 3 * column_width)
        projected = jnp.dot(features, flat_qkv, preferred_element_type=jnp.float32) + qkv_bias[
            layer_index
        ].reshape(3 * column_width)
        expanded = (
            jnp.dot(features, gathered_up, preferred_element_type=jnp.float32)
            + up_bias[layer_index]
        )
        shaped = projected.reshape(token_count, 3, head_count, HEAD_DIM)
        queries = rotate(shaped[:, 0], cosine_table, sine_table).astype(jnp.bfloat16)
        key_local = (
            rotate(shaped[:, 1], cosine_table, sine_table)
            .astype(jnp.bfloat16)
            .reshape(token_count, column_width)
        )
        value_local = shaped[:, 2].astype(jnp.bfloat16).reshape(token_count, column_width)
        key_rows, value_rows = (
            lax.all_gather(key_local, "row", axis=0, tiled=True),
            lax.all_gather(value_local, "row", axis=0, tiled=True),
        )
        mixed_sum, log_total = attend_forward(
            queries, key_rows, value_rows, query_segments, segment_ids, query_begin
        )
        mixed_low = mixed_sum.reshape(token_count, column_width).astype(jnp.bfloat16)
        activated = gelu_curve(expanded).astype(jnp.bfloat16)
        partial_sum = jnp.dot(
            mixed_low, gathered_dense, preferred_element_type=jnp.float32
        ) + jnp.dot(activated, gathered_down, preferred_element_type=jnp.float32)
        branch = lax.psum_scatter(partial_sum, "col", scatter_dimension=1, tiled=True)
        residual = residual + branch + dense_bias[layer_index] + down_bias[layer_index]
        outputs.append(residual)
        kept_values.append(
            (
                centred,
                inverse,
                features,
                queries,
                key_local,
                value_local,
                key_rows,
                value_rows,
                log_total,
                mixed_low,
                expanded,
                activated,
                gathered,
            )
        )
    gradient = output_cotangent.astype(jnp.float32)
    small_terms = []
    weight_blocks = []
    for layer_index in reversed(range(layer_count)):
        (
            centred,
            inverse,
            features,
            queries,
            key_local,
            value_local,
            key_rows,
            value_rows,
            log_total,
            mixed_low,
            expanded,
            activated,
            gathered,
        ) = kept_values[layer_index]
        gathered_qkv, gathered_up, gathered_dense, gathered_down = gathered
        column_width = gathered_qkv.shape[2]
        head_count = column_width // HEAD_DIM
        flat_qkv = gathered_qkv.reshape(gathered_qkv.shape[0], 3 * column_width)
        out_bias_grad = jnp.sum(gradient, axis=0)
        grad_features = lax.all_gather(gradient.astype(jnp.bfloat16), "col", axis=1, tiled=True)
        mixed_grad = jnp.einsum(
            "td,cd->tc", grad_features, gathered_dense, preferred_element_type=jnp.float32
        ).astype(jnp.bfloat16)
        active_grad = jnp.einsum(
            "td,fd->tf", grad_features, gathered_down, preferred_element_type=jnp.float32
        )
        up_low = jax.vjp(gelu_curve, expanded)[1](active_grad)[0].astype(jnp.bfloat16)
        shaped_grad = mixed_grad.reshape(token_count, head_count, HEAD_DIM)
        query_grad, row_delta, key_grads, value_grads = attend_backward(
            queries,
            key_rows,
            value_rows,
            query_segments,
            segment_ids,
            query_begin,
            log_total,
            shaped_grad,
        )
        key_grad, value_grad = (
            lax.psum_scatter(key_grads, "row", scatter_dimension=0, tiled=True),
            lax.psum_scatter(value_grads, "row", scatter_dimension=0, tiled=True),
        )
        query_pre = rotate_back(query_grad, cosine_table, sine_table)
        key_pre = rotate_back(
            key_grad.reshape(token_count, head_count, HEAD_DIM), cosine_table, sine_table
        )
        qkv_low = (
            jnp.stack(
                [query_pre, key_pre, value_grad.reshape(token_count, head_count, HEAD_DIM)], axis=1
            )
            .reshape(token_count, 3 * column_width)
            .astype(jnp.bfloat16)
        )
        feature_grad = jnp.einsum(
            "tn,dn->td", qkv_low, flat_qkv, preferred_element_type=jnp.float32
        ) + jnp.einsum("tf,df->td", up_low, gathered_up, preferred_element_type=jnp.float32)
        normed_grad = lax.psum_scatter(feature_grad, "col", scatter_dimension=1, tiled=True)
        scaled_grad = normed_grad * norm_gain[layer_index]
        first_total, second_total = lax.psum(
            (jnp.sum(scaled_grad, axis=1), jnp.sum(scaled_grad * centred, axis=1)), "col"
        )
        qkv_term = jnp.einsum(
            "td,tn->dn", features, qkv_low, preferred_element_type=jnp.float32
        ).reshape(features.shape[1], 3, column_width)
        up_term = jnp.einsum("td,tf->df", features, up_low, preferred_element_type=jnp.float32)
        dense_term = jnp.einsum(
            "tc,td->cd", mixed_low, grad_features, preferred_element_type=jnp.float32
        )
        down_term = jnp.einsum(
            "tf,td->fd", activated, grad_features, preferred_element_type=jnp.float32
        )
        blocks = (
            lax.psum_scatter(
                qkv_term.astype(jnp.bfloat16), ("dp", "row"), scatter_dimension=0, tiled=True
            ).astype(jnp.float32),
            lax.psum_scatter(
                up_term.astype(jnp.bfloat16), ("dp", "row"), scatter_dimension=0, tiled=True
            ).astype(jnp.float32),
            lax.psum_scatter(
                dense_term.astype(jnp.bfloat16), ("dp", "row"), scatter_dimension=1, tiled=True
            ).astype(jnp.float32),
            lax.psum_scatter(
                down_term.astype(jnp.bfloat16), ("dp", "row"), scatter_dimension=1, tiled=True
            ).astype(jnp.float32),
        )
        weight_blocks.append(blocks)
        small_terms.append(
            (
                jnp.sum(normed_grad * centred, axis=0),
                jnp.sum(normed_grad, axis=0),
                jnp.sum(qkv_low, axis=0, dtype=jnp.float32).reshape(3, column_width),
                out_bias_grad,
                jnp.sum(up_low, axis=0, dtype=jnp.float32),
            )
        )
        gradient = gradient + inverse[:, None] * (
            scaled_grad
            - first_total[:, None] / full_width
            - centred * (second_total[:, None] / full_width)
        )
    ordered_small = small_terms[::-1]
    ordered_blocks = weight_blocks[::-1]
    gain_grads, shift_grads, qkv_bias_grads, out_bias_grads, up_bias_grads = lax.psum(
        (
            jnp.stack([entry[0] for entry in ordered_small]),
            jnp.stack([entry[1] for entry in ordered_small]),
            jnp.stack([entry[2] for entry in ordered_small]),
            jnp.stack([entry[3] for entry in ordered_small]),
            jnp.stack([entry[4] for entry in ordered_small]),
        ),
        ("dp", "row"),
    )
    return (
        jnp.stack(outputs),
        gradient,
        gain_grads,
        shift_grads,
        jnp.stack([entry[0] for entry in ordered_blocks]),
        qkv_bias_grads,
        jnp.stack([entry[2] for entry in ordered_blocks]),
        out_bias_grads,
        jnp.stack([entry[1] for entry in ordered_blocks]),
        up_bias_grads,
        jnp.stack([entry[3] for entry in ordered_blocks]),
        out_bias_grads,
    )


def solution(mesh):
    placed = (
        P(("dp", "row"), "col"),
        P("dp"),
        P("dp"),
        P(None, "col"),
        P(None, "col"),
        P(None, ("dp", "row"), None, "col"),
        P(None, None, "col"),
        P(None, "col", ("dp", "row")),
        P(None, "col"),
        P(None, ("dp", "row"), "col"),
        P(None, "col"),
        P(None, "col", ("dp", "row")),
        P(None, "col"),
        P(("dp", "row"), "col"),
    )
    return jax.shard_map(
        per_device,
        mesh=mesh,
        in_specs=placed,
        out_specs=(
            P(None, ("dp", "row"), "col"),
            P(("dp", "row"), "col"),
            P(None, "col"),
            P(None, "col"),
            P(None, ("dp", "row"), None, "col"),
            P(None, None, "col"),
            P(None, "col", ("dp", "row")),
            P(None, "col"),
            P(None, ("dp", "row"), "col"),
            P(None, "col"),
            P(None, "col", ("dp", "row")),
            P(None, "col"),
        ),
        check_vma=False,
    )
```

profile of v0, /device:TPU:0, one launch (start us, length us, event | category | flops | bytes accessed | tf_op | source)
XLA Modules:
  0.0 1846.7 jit_solution(7863110767343714918)
XLA Ops:
  31.0 39.5 %all-gather.25.cloned.1.call-done = bf16[512,2048]{1,0:T(8,128)(2,1)} async-done(((bf16[512,512]{1,0:T(8,128)(2,1)}), bf16[512,2048]{1,0:T(8,128)(2,1)}) %all-gather.25.cloned.1.call-update) | async-done | bytes 2097168 | tf_op jit(solution)/shard_map/all_gather | solution.py:237
  70.5 47.9 %all-gather.41.cloned.1.call-done = bf16[1,2048,3,512]{1,3,2,0:T(8,128)(2,1)} async-done(((bf16[1,256,3,512]{1,3,2,0:T(8,128)(2,1)}), bf16[1,2048,3,512]{1,3,2,0:T(8,128)(2,1)}) %all-gather.41.cloned.1.call-update) | async-done | bytes 6291472 | tf_op jit(solution)/shard_map/all_gather | solution.py:225
  159.3 19.5 %all-gather.27.cloned.1.call-done = bf16[2048,512]{0,1:T(8,128)(2,1)} async-done(((bf16[512,512]{0,1:T(8,128)(2,1)}), bf16[2048,512]{0,1:T(8,128)(2,1)}) %all-gather.27.cloned.1.call-update) | async-done | bytes 2097168 | tf_op jit(solution)/shard_map/all_gather | solution.py:259
  185.1 50.6 %all-gather.45.cloned.1.call-done = bf16[1,2048,2048]{2,1,0:T(8,128)(2,1)} async-done(((bf16[1,256,2048]{2,1,0:T(8,128)(2,1)}), bf16[1,2048,2048]{2,1,0:T(8,128)(2,1)}) %all-gather.45.cloned.1.call-update) | async-done | bytes 8388624 | tf_op jit(solution)/shard_map/all_gather | solution.py:226
  246.1 47.8 %all-gather.47.cloned.1.call-done = bf16[1,2048,2048]{2,1,0:T(8,128)(2,1)} async-done(((bf16[1,2048,256]{2,1,0:T(8,128)(2,1)}), bf16[1,2048,2048]{2,1,0:T(8,128)(2,1)}) %all-gather.47.cloned.1.call-update) | async-done | bytes 8388624 | tf_op jit(solution)/shard_map/all_gather | solution.py:228
  305.7 18.4 all-gather.43.cloned.1.call-done
  333.7 73.4 %reduce-scatter.17.cloned.1.call-done = f32[512,512]{1,0:T(8,128)} async-done(((f32[512,2048]{1,0:T(8,128)}), f32[512,512]{1,0:T(8,128)}) %reduce-scatter.17.cloned.1.call-update) | async-done | bytes 1048592 | tf_op jit(solution)/shard_map/reduce_scatter | solution.py:269
  422.5 34.5 %all-gather.49.cloned.1.call-done = bf16[1,2048,3,512]{1,3,2,0:T(8,128)(2,1)} async-done(((bf16[1,256,3,512]{1,3,2,0:T(8,128)(2,1)}), bf16[1,2048,3,512]{1,3,2,0:T(8,128)(2,1)}) %all-gather.49.cloned.1.call-update) | async-done | bytes 6291472 | tf_op jit(solution)/shard_map/all_gather | solution.py:225
  457.0 48.0 %all-gather.31.cloned.1.call-done = bf16[512,2048]{1,0:T(8,128)(2,1)} async-done(((bf16[512,512]{1,0:T(8,128)(2,1)}), bf16[512,2048]{1,0:T(8,128)(2,1)}) %all-gather.31.cloned.1.call-update) | async-done | bytes 2097168 | tf_op jit(solution)/shard_map/all_gather | solution.py:237
  523.5 27.9 %all-gather.37.cloned.1.call-done = bf16[512,2048]{1,0:T(8,128)(2,1)} async-done(((bf16[512,512]{1,0:T(8,128)(2,1)}), bf16[512,2048]{1,0:T(8,128)(2,1)}) %all-gather.37.cloned.1.call-update) | async-done | bytes 2097168 | tf_op jit(solution)/shard_map/all_gather | solution.py:313
  551.4 28.8 %all-gather.51.cloned.1.call-done = bf16[1,512,2048]{2,1,0:T(8,128)(2,1)} async-done(((bf16[1,512,256]{2,1,0:T(8,128)(2,1)}), bf16[1,512,2048]{2,1,0:T(8,128)(2,1)}) %all-gather.51.cloned.1.call-update) | async-done | bytes 2097168 | tf_op jit(solution)/shard_map/all_gather | solution.py:227
  583.8 21.2 %all-gather.35.cloned.1.call-done = bf16[2048,512]{0,1:T(8,128)(2,1)} async-done(((bf16[512,512]{0,1:T(8,128)(2,1)}), bf16[2048,512]{0,1:T(8,128)(2,1)}) %all-gather.35.cloned.1.call-update) | async-done | bytes 2097168 | tf_op jit(solution)/shard_map/all_gather | solution.py:258
  610.1 19.6 %all-gather.33.cloned.1.call-done = bf16[2048,512]{0,1:T(8,128)(2,1)} async-done(((bf16[512,512]{0,1:T(8,128)(2,1)}), bf16[2048,512]{0,1:T(8,128)(2,1)}) %all-gather.33.cloned.1.call-update) | async-done | bytes 2097168 | tf_op jit(solution)/shard_map/all_gather | solution.py:259
  654.6 31.4 %all-gather.53.cloned.1.call-done = bf16[1,2048,2048]{2,1,0:T(8,128)(2,1)} async-done(((bf16[1,256,2048]{2,1,0:T(8,128)(2,1)}), bf16[1,2048,2048]{2,1,0:T(8,128)(2,1)}) %all-gather.53.cloned.1.call-update) | async-done | bytes 8388624 | tf_op jit(solution)/shard_map/all_gather | solution.py:226
  696.5 48.0 %all-gather.55.cloned.1.call-done = bf16[1,2048,2048]{2,1,0:T(8,128)(2,1)} async-done(((bf16[1,2048,256]{2,1,0:T(8,128)(2,1)}), bf16[1,2048,2048]{2,1,0:T(8,128)(2,1)}) %all-gather.55.cloned.1.call-update) | async-done | bytes 8388624 | tf_op jit(solution)/shard_map/all_gather | solution.py:228
  744.5 14.1 convert_reduce_fusion
  759.7 32.4 %reduce-scatter.21.cloned.1.call-done = f32[512,512]{0,1:T(8,128)} async-done(((f32[2048,512]{0,1:T(8,128)}), f32[512,512]{0,1:T(8,128)}) %reduce-scatter.21.cloned.1.call-update) | async-done | bytes 1048592 | tf_op jit(solution)/shard_map/reduce_scatter | solution.py:333
  795.5 44.2 %reduce-scatter.23.cloned.1.call-done = f32[512,512]{0,1:T(8,128)} async-done(((f32[2048,512]{0,1:T(8,128)}), f32[512,512]{0,1:T(8,128)}) %reduce-scatter.23.cloned.1.call-update) | async-done | bytes 1048592 | tf_op jit(solution)/shard_map/reduce_scatter | solution.py:334
  884.2 47.8 %reduce-scatter.25.cloned.1.call-done = f32[512,512]{1,0:T(8,128)} async-done(((f32[512,2048]{1,0:T(8,128)}), f32[512,512]{1,0:T(8,128)}) %reduce-scatter.25.cloned.1.call-update) | async-done | bytes 1048592 | tf_op jit(solution)/shard_map/reduce_scatter | solution.py:350
  945.5 66.6 %reduce-scatter.19.cloned.1.call-done = f32[512,512]{1,0:T(8,128)} async-done(((f32[512,2048]{1,0:T(8,128)}), f32[512,512]{1,0:T(8,128)}) %reduce-scatter.19.cloned.1.call-update) | async-done | bytes 1048592 | tf_op jit(solution)/shard_map/reduce_scatter | solution.py:269
  1017.7 46.5 %all-gather.39.cloned.1.call-done = bf16[512,2048]{1,0:T(8,128)(2,1)} async-done(((bf16[512,512]{1,0:T(8,128)(2,1)}), bf16[512,2048]{1,0:T(8,128)(2,1)}) %all-gather.39.cloned.1.call-update) | async-done | bytes 2097168 | tf_op jit(solution)/shard_map/all_gather | solution.py:313
  1156.7 32.1 %reduce-scatter.27.cloned.1.call-done = f32[512,512]{0,1:T(8,128)} async-done(((f32[2048,512]{0,1:T(8,128)}), f32[512,512]{0,1:T(8,128)}) %reduce-scatter.27.cloned.1.call-update) | async-done | bytes 1048592 | tf_op jit(solution)/shard_map/reduce_scatter | solution.py:333
  1191.1 45.3 %reduce-scatter.29.cloned.1.call-done = f32[512,512]{0,1:T(8,128)} async-done(((f32[2048,512]{0,1:T(8,128)}), f32[512,512]{0,1:T(8,128)}) %reduce-scatter.29.cloned.1.call-update) | async-done | bytes 1048592 | tf_op jit(solution)/shard_map/reduce_scatter | solution.py:334
  1281.8 44.6 %reduce-scatter.37.cloned.1.call-done = bf16[512,256]{1,0:T(8,128)(2,1)} async-done(((bf16[512,2048]{1,0:T(8,128)(2,1)}), bf16[512,256]{1,0:T(8,128)(2,1)}) %reduce-scatter.37.cloned.1.call-update) | async-done | bytes 262160 | tf_op jit(solution)/shard_map/reduce_scatter | solution.py:372
  1328.5 72.9 %reduce-scatter.43.cloned.1.call-done = bf16[256,2048]{1,0:T(8,128)(2,1)} async-done(((bf16[2048,2048]{1,0:T(8,128)(2,1)}), bf16[256,2048]{1,0:T(8,128)(2,1)}) %reduce-scatter.43.cloned.1.call-update) | async-done | bytes 1048592 | tf_op jit(solution)/shard_map/reduce_scatter | solution.py:369
  1401.3 74.6 %reduce-scatter.41.cloned.1.call-done = bf16[256,2048]{1,0:T(8,128)(2,1)} async-done(((bf16[2048,2048]{1,0:T(8,128)(2,1)}), bf16[256,2048]{1,0:T(8,128)(2,1)}) %reduce-scatter.41.cloned.1.call-update) | async-done | bytes 1048592 | tf_op jit(solution)/shard_map/reduce_scatter | solution.py:369
  1479.8 71.3 %reduce-scatter.47.cloned.1.call-done = bf16[2048,256]{1,0:T(8,128)(2,1)} async-done(((bf16[2048,2048]{1,0:T(8,128)(2,1)}), bf16[2048,256]{1,0:T(8,128)(2,1)}) %reduce-scatter.47.cloned.1.call-update) | async-done | bytes 1048592 | tf_op jit(solution)/shard_map/reduce_scatter | solution.py:375
  1551.1 74.8 %reduce-scatter.45.cloned.1.call-done = bf16[2048,256]{1,0:T(8,128)(2,1)} async-done(((bf16[2048,2048]{1,0:T(8,128)(2,1)}), bf16[2048,256]{1,0:T(8,128)(2,1)}) %reduce-scatter.45.cloned.1.call-update) | async-done | bytes 1048592 | tf_op jit(solution)/shard_map/reduce_scatter | solution.py:375
  1629.7 75.2 %reduce-scatter.31.cloned.1.call-done = f32[512,512]{1,0:T(8,128)} async-done(((f32[512,2048]{1,0:T(8,128)}), f32[512,512]{1,0:T(8,128)}) %reduce-scatter.31.cloned.1.call-update) | async-done | bytes 1048592 | tf_op jit(solution)/shard_map/reduce_scatter | solution.py:350
  1706.8 25.1 %all-reduce = (f32[2,512]{1,0:T(2,128)}, f32[2,512]{1,0:T(2,128)}, f32[2,3,512]{2,1,0:T(4,128)S(1)}, f32[2,512]{1,0:T(2,128)S(1)}, f32[2,2048]{1,0:T(2,128)}) all-reduce(f32[2,512]{1,0:T(2,128)S(1)} %pad_maximum_fusion.7, f32[2,512]{1,0:T(2,128)S(1)} %pad_maximum_fusion.8, ...), channel_id=1, replica_groups=mesh['dp'=2,'row'=4,'col'=4] {'dp','row'}, use_global_device_ids=true, to_apply=%region_48.49 | all-reduce | flops 10240 | bytes 81920 | tf_op jit(solution)/shard_map/psum | solution.py:396
  1746.3 24.3 %reduce-scatter.35.cloned.1.call-done = bf16[256,3,512]{2,0,1:T(8,128)(2,1)} async-done(((bf16[2048,3,512]{2,0,1:T(8,128)(2,1)}), bf16[256,3,512]{2,0,1:T(8,128)(2,1)}) %reduce-scatter.35.cloned.1.call-update) | async-done | bytes 786448 | tf_op jit(solution)/shard_map/reduce_scatter | solution.py:366
  1770.6 65.6 %reduce-scatter.33.cloned.1.call-done = bf16[256,3,512]{2,0,1:T(8,128)(2,1)} async-done(((bf16[2048,3,512]{2,0,1:T(8,128)(2,1)}), bf16[256,3,512]{2,0,1:T(8,128)(2,1)}) %reduce-scatter.33.cloned.1.call-update) | async-done | bytes 786448 | tf_op jit(solution)/shard_map/reduce_scatter | solution.py:366
  (414 shorter events, 475.3 us)
Async XLA Ops:
  7.2 63.3 %all-gather.25.cloned.1.call-start = ((), (), s32[]{:S(2)}) async-start(), calls=%async_computation.16 | async-start | bytes 2621440 | tf_op jit(solution)/shard_map/all_gather | solution.py:237
  26.2 92.2 %all-gather.41.cloned.1.call-start = ((), (), s32[]{:S(2)}) async-start(), calls=%async_computation.40 | async-start | bytes 7077888 | tf_op jit(solution)/shard_map/all_gather | solution.py:225
  29.8 124.4 %all-gather.29.cloned.1.call-start = ((), (), s32[]{:S(2)}) async-start(), calls=%async_computation.18 | async-start | bytes 2621440 | tf_op jit(solution)/shard_map/all_gather | solution.py:258
  131.5 47.4 %all-gather.27.cloned.1.call-start = ((), (), s32[]{:S(2)}) async-start(), calls=%async_computation.17 | async-start | bytes 2621440 | tf_op jit(solution)/shard_map/all_gather | solution.py:259
  132.5 103.2 %all-gather.45.cloned.1.call-start = ((), (), s32[]{:S(2)}) async-start(), calls=%async_computation.42 | async-start | bytes 9437184 | tf_op jit(solution)/shard_map/all_gather | solution.py:226
  135.8 158.2 %all-gather.47.cloned.1.call-start = ((), (), s32[]{:S(2)}) async-start(), calls=%async_computation.43 | async-start | bytes 9437184 | tf_op jit(solution)/shard_map/all_gather | solution.py:228
  137.3 186.8 %all-gather.43.cloned.1.call-start = ((), (), s32[]{:S(2)}) async-start(), calls=%async_computation.41 | async-start | bytes 2359296 | tf_op jit(solution)/shard_map/all_gather | solution.py:227
  138.2 268.9 %reduce-scatter.17.cloned.1.call-start = ((), (), s32[]{:S(2)}) async-start(), calls=%async_computation.19 | async-start | bytes 5242880 | tf_op jit(solution)/shard_map/reduce_scatter | solution.py:269
  330.2 126.7 %all-gather.49.cloned.1.call-start = ((), (), s32[]{:S(2)}) async-start(), calls=%async_computation.44 | async-start | bytes 7077888 | tf_op jit(solution)/shard_map/all_gather | solution.py:225
  332.5 172.5 %all-gather.31.cloned.1.call-start = ((), (), s32[]{:S(2)}) async-start(), calls=%async_computation.20 | async-start | bytes 2621440 | tf_op jit(solution)/shard_map/all_gather | solution.py:237
  420.7 130.6 %all-gather.37.cloned.1.call-start = ((), (), s32[]{:S(2)}) async-start(), calls=%async_computation.24 | async-start | bytes 2621440 | tf_op jit(solution)/shard_map/all_gather | solution.py:313
  421.5 158.7 %all-gather.51.cloned.1.call-start = ((), (), s32[]{:S(2)}) async-start(), calls=%async_computation.45 | async-start | bytes 2359296 | tf_op jit(solution)/shard_map/all_gather | solution.py:227
  422.1 183.0 %all-gather.35.cloned.1.call-start = ((), (), s32[]{:S(2)}) async-start(), calls=%async_computation.22 | async-start | bytes 2621440 | tf_op jit(solution)/shard_map/all_gather | solution.py:258
  520.1 109.6 %all-gather.33.cloned.1.call-start = ((), (), s32[]{:S(2)}) async-start(), calls=%async_computation.21 | async-start | bytes 2621440 | tf_op jit(solution)/shard_map/all_gather | solution.py:259
  522.3 163.8 %all-gather.53.cloned.1.call-start = ((), (), s32[]{:S(2)}) async-start(), calls=%async_computation.46 | async-start | bytes 9437184 | tf_op jit(solution)/shard_map/all_gather | solution.py:226
  522.9 221.7 %all-gather.55.cloned.1.call-start = ((), (), s32[]{:S(2)}) async-start(), calls=%async_computation.47 | async-start | bytes 9437184 | tf_op jit(solution)/shard_map/all_gather | solution.py:228
  523.4 268.7 %reduce-scatter.21.cloned.1.call-start = ((), (), s32[]{:S(2)}) async-start(), calls=%async_computation.25 | async-start | bytes 5242880 | tf_op jit(solution)/shard_map/reduce_scatter | solution.py:333
  654.0 185.7 %reduce-scatter.23.cloned.1.call-start = ((), (), s32[]{:S(2)}) async-start(), calls=%async_computation.26 | async-start | bytes 5242880 | tf_op jit(solution)/shard_map/reduce_scatter | solution.py:334
  654.6 277.4 %reduce-scatter.25.cloned.1.call-start = ((), (), s32[]{:S(2)}) async-start(), calls=%async_computation.27 | async-start | bytes 5242880 | tf_op jit(solution)/shard_map/reduce_scatter | solution.py:350
  855.0 157.0 %reduce-scatter.19.cloned.1.call-start = ((), (), s32[]{:S(2)}) async-start(), calls=%async_computation.23 | async-start | bytes 5242880 | tf_op jit(solution)/shard_map/reduce_scatter | solution.py:269
  884.1 180.0 %all-gather.39.cloned.1.call-start = ((), (), s32[]{:S(2)}) async-start(), calls=%async_computation.28 | async-start | bytes 2621440 | tf_op jit(solution)/shard_map/all_gather | solution.py:313
  1017.6 171.2 %reduce-scatter.27.cloned.1.call-start = ((), (), s32[]{:S(2)}) async-start(), calls=%async_computation.29 | async-start | bytes 5242880 | tf_op jit(solution)/shard_map/reduce_scatter | solution.py:333
  1092.4 144.0 %reduce-scatter.29.cloned.1.call-start = ((), (), s32[]{:S(2)}) async-start(), calls=%async_computation.30 | async-start | bytes 5242880 | tf_op jit(solution)/shard_map/reduce_scatter | solution.py:334
  1093.2 188.6 %reduce-scatter.39.cloned.1.call-start = ((), (), s32[]{:S(2)}) async-start(), calls=%async_computation.35 | async-start | bytes 2359296 | tf_op jit(solution)/shard_map/reduce_scatter | solution.py:372
  1096.6 229.7 %reduce-scatter.37.cloned.1.call-start = ((), (), s32[]{:S(2)}) async-start(), calls=%async_computation.34 | async-start | bytes 2359296 | tf_op jit(solution)/shard_map/reduce_scatter | solution.py:372
  1101.0 300.4 %reduce-scatter.43.cloned.1.call-start = ((), (), s32[]{:S(2)}) async-start(), calls=%async_computation.37 | async-start | bytes 9437184 | tf_op jit(solution)/shard_map/reduce_scatter | solution.py:369
  1109.5 366.4 %reduce-scatter.41.cloned.1.call-start = ((), (), s32[]{:S(2)}) async-start(), calls=%async_computation.36 | async-start | bytes 9437184 | tf_op jit(solution)/shard_map/reduce_scatter | solution.py:369
  1130.5 420.6 %reduce-scatter.47.cloned.1.call-start = ((), (), s32[]{:S(2)}) async-start(), calls=%async_computation.39 | async-start | bytes 9437184 | tf_op jit(solution)/shard_map/reduce_scatter | solution.py:375
  1142.9 483.0 %reduce-scatter.45.cloned.1.call-start = ((), (), s32[]{:S(2)}) async-start(), calls=%async_computation.38 | async-start | bytes 9437184 | tf_op jit(solution)/shard_map/reduce_scatter | solution.py:375
  1155.3 549.6 %reduce-scatter.31.cloned.1.call-start = ((), (), s32[]{:S(2)}) async-start(), calls=%async_computation.31 | async-start | bytes 5242880 | tf_op jit(solution)/shard_map/reduce_scatter | solution.py:350
  1253.4 517.2 %reduce-scatter.35.cloned.1.call-start = ((), (), s32[]{:S(2)}) async-start(), calls=%async_computation.33 | async-start | bytes 7077888 | tf_op jit(solution)/shard_map/reduce_scatter | solution.py:366
  1261.8 574.3 %reduce-scatter.33.cloned.1.call-start = ((), (), s32[]{:S(2)}) async-start(), calls=%async_computation.32 | async-start | bytes 7077888 | tf_op jit(solution)/shard_map/reduce_scatter | solution.py:366
  (78 other events, 5018.4 us)
Sparse Core Ops, SparseCore 0:
  26.3 44.1 all-gather.24
  73.0 45.3 all-gather.40
  131.6 22.5 all-gather.28
  156.3 22.5 all-gather.26
  181.2 54.4 all-gather.44
  238.0 55.9 all-gather.46
  295.9 28.1 all-gather.42
  330.4 76.7 reduce-scatter.16
  409.8 47.1 all-gather.48
  459.0 45.9 all-gather.30
  506.7 44.6 all-gather.36
  553.2 26.8 all-gather.50
  582.4 22.5 all-gather.34
  607.1 22.5 all-gather.32
  631.6 54.3 all-gather.52
  688.5 55.9 all-gather.54
  747.6 44.5 reduce-scatter.20
  795.1 44.4 reduce-scatter.22
  855.2 76.7 reduce-scatter.24
  934.7 77.3 reduce-scatter.18
  1017.7 46.3 all-gather.38
  1092.5 96.1 reduce-scatter.26
  1191.9 44.4 reduce-scatter.28
  1240.5 41.2 reduce-scatter.38
  1285.0 41.2 reduce-scatter.36
  1330.0 71.2 reduce-scatter.42
  1404.7 71.2 reduce-scatter.40
  1479.8 71.2 reduce-scatter.46
  1554.6 71.2 reduce-scatter.44
  1628.1 76.7 reduce-scatter.30
  1708.3 62.2 reduce-scatter.34
  1774.3 61.7 reduce-scatter.32
where the time goes:
time: 1860 us; the launch traced here: 1850 us
  waiting for transfers between devices  1400 us (75%)
  matrix products  235 us (13%)
  blocking collectives  71.9 us (4%)
  local copies, waits for them, and re-layouts  70.2 us (4%)
  other arithmetic  50.1 us (3%)
    reduce_scatter x2, waiting for transfers between devices, per_device(): lax.psum_scatter(up_term.astype(jnp.bfloat16), ('dp', 'row'), scatter_dim...  147 us
    reduce_scatter x2, waiting for transfers between devices, per_device(): lax.psum_scatter(down_term.astype(jnp.bfloat16), ('dp', 'row'), scatter_d...  146 us
    reduce_scatter x2, waiting for transfers between devices, per_device(): lax.psum_scatter(partial_sum, 'col', scatter_dimension=1, tiled=True)  140 us
    reduce_scatter x2, waiting for transfers between devices, per_device(): lax.psum_scatter(feature_grad, 'col', scatter_dimension=1, tiled=True)  123 us
    all_gather x2, waiting for transfers between devices, per_device(): lax.all_gather(down_weight[layer_index], ('dp', 'row'), axis=1, tiled=True)  95.8 us
    reduce_scatter x2, waiting for transfers between devices, per_device(): lax.psum_scatter(qkv_term.astype(jnp.bfloat16), ('dp', 'row'), scatter_di...  89.9 us
    reduce_scatter x2, waiting for transfers between devices, per_device(): lax.psum_scatter(value_grads, 'row', scatter_dimension=0, tiled=True)  89.4 us
    all_gather x2, waiting for transfers between devices, per_device(): features = lax.all_gather(normed, 'col', axis=1, tiled=True)  87.6 us
  transfers between devices with their start and end apart: 32, of which 32 were waited for; matrix products, arithmetic and copies ran while one was open for 14% of the time, Pallas kernels for 0%

commit v1 on v0

v1 whole, which is shorter than its diff:
```python
import math

import jax
import jax.numpy as jnp
from jax import lax
from jax.experimental import pallas as pl
from jax.experimental.pallas import tpu as pltpu
from jax.sharding import Mesh
from jax.sharding import PartitionSpec as P

HEAD_DIM = 64
ROT = 32
EPSILON = 1e-05
NEGATIVE = -1e30
LANES = 128
HEADS_TILE = LANES // HEAD_DIM
VMEM_BYTES = 40 * 1024 * 1024
F32 = jnp.float32
BF16 = jnp.bfloat16
ANY = pl.BlockSpec(memory_space=pl.ANY)
COST = pl.CostEstimate(flops=1, bytes_accessed=1, transcendentals=0)


def contract(left, right, left_dim, right_dim):
    return lax.dot_general(
        left, right, (((left_dim,), (right_dim,)), ((), ())), preferred_element_type=F32
    )


def shift(value, axis, step):
    size = lax.axis_size(axis)
    return lax.ppermute(value, axis, [(i, (i + step) % size) for i in range(size)])


def swap_core(value):
    return shift(value, "core", 1)


class Order:
    def __init__(self):
        self.last = []
        self.links = {}
        self.newest = {}

    def now(self, values):
        def one(value):
            while id(value) in self.newest:
                value = self.newest[id(value)][1]
            return value

        return jax.tree.map(one, values)

    def after(self, values, *others):
        leaves, tree = jax.tree.flatten(self.now(values))
        held = self.now([other for other in (*self.last, *others) if other is not None])
        every = {id(value): value for value in (*leaves, *held)}
        if held:
            for old, new in zip(every.values(), lax.optimization_barrier(tuple(every.values()))):
                self.newest[id(old)] = (old, new)
        return self.now(jax.tree.unflatten(tree, leaves))

    def run(self, function, *values):
        out = function(*self.after(values))
        self.last = jax.tree.leaves(out)
        return out

    def send(self, value, axis, step, depth=2):
        queue = self.links.setdefault(axis, [])
        held = queue[-depth] if len(queue) >= depth else None
        out = shift(self.after([value], held)[0], axis, step)
        queue.append(out)
        return out

    def wait(self, *values):
        out = self.after(list(values))
        self.last = [*self.last, *out]
        return out


def sum_over(value, axis):
    size = lax.axis_size(axis)
    if size & (size - 1):
        return value + sum(shift(value, axis, k) for k in range(1, size))
    step = 1
    while step < size:
        value = value + lax.ppermute(value, axis, [(i, i ^ step) for i in range(size)])
        step *= 2
    return value


def width_table(layout):
    n_y, n_x, n_c = lax.axis_size("dp"), lax.axis_size("x"), lax.axis_size("core")
    y, x, c = lax.axis_index("dp"), lax.axis_index("x"), lax.axis_index("core")
    begins = jnp.stack(
        [
            ((((y - a + n_y) % n_y) * n_x + (x - b + n_x) % n_x) * n_c + (c - k + n_c) % n_c)
            * layout.place
            for a in range(n_y)
            for b in range(n_x)
            for k in range(n_c)
        ]
    )
    return jnp.concatenate(
        [begins // layout.part, begins % layout.part, c[None], begins]
    ).astype(jnp.int32)


class Layout:
    def __init__(self, own_tokens, part):
        self.n_y, self.n_x, self.n_c, self.n_z = (
            lax.axis_size(name) for name in ("dp", "x", "core", "col")
        )
        self.own_tokens = own_tokens
        self.tokens = own_tokens * self.n_c
        self.part = part
        self.width = part * self.n_z
        self.places = self.n_y * self.n_x * self.n_c
        self.place = self.width // self.places
        self.block = self.place * self.n_c
        self.blocks = self.n_y * self.n_x

    def fetch(self, table, gathered, core, places, target, sems, first):
        copies = []
        for slot, at in enumerate(places):
            begin = pl.multiple_of(table[self.places + at], self.place)
            copies.append(
                pltpu.make_async_copy(
                    gathered.at[core * self.n_z + table[at], :, pl.ds(begin, self.place)],
                    target.at[:, slot * self.place : (slot + 1) * self.place],
                    sems.at[first + slot],
                )
            )
        return copies


def kernel_call(body, table, inputs, in_specs, out_shape, out_specs, scratch, name, grid=(1,), aliases=None):
    return pl.pallas_call(
        body,
        grid_spec=pltpu.PrefetchScalarGridSpec(
            num_scalar_prefetch=1,
            grid=grid,
            in_specs=in_specs,
            out_specs=out_specs,
            scratch_shapes=scratch,
        ),
        out_shape=out_shape,
        input_output_aliases=aliases or {},
        compiler_params=pltpu.CompilerParams(vmem_limit_bytes=VMEM_BYTES),
        cost_estimate=COST,
        name=name,
    )(table, *inputs)


def full(array_or_shape):
    shape = getattr(array_or_shape, "shape", array_or_shape)
    return pl.BlockSpec(tuple(shape), lambda i, t: (0,) * len(shape))


def start_all(copies):
    for copy in copies:
        copy.start()


def wait_all(copies):
    for copy in copies:
        copy.wait()


def rope(value, cosine, lower, upper):
    half = ROT // 2
    return (
        value * cosine
        + pltpu.roll(value, LANES - half, 1) * lower
        + pltpu.roll(value, half, 1) * upper
    )


def rope_tables(place_values):
    half = ROT // 2
    freq_table = 1.0 / 10000.0 ** (jnp.arange(half, dtype=F32) * 2.0 / ROT)
    angles = place_values.astype(F32)[:, None] * freq_table
    cosine, sine = jnp.cos(angles), jnp.sin(angles)
    rest = jnp.ones((angles.shape[0], HEAD_DIM - ROT), F32)
    none = jnp.zeros_like(sine)
    pair = lambda *pieces: jnp.concatenate(pieces * HEADS_TILE, axis=1)
    return (
        pair(cosine, cosine, rest),
        pair(-sine, none, 0.0 * rest),
        pair(none, sine, 0.0 * rest),
    )


class Stream:
    def __init__(self, layout, table, gathered, weights, features, buffers, sems, w_sems, window=None):
        self.layout, self.features, self.buffers = layout, features, buffers
        if window is not None:
            weights = [ref.at[:, window] for ref in weights]
        n_c = layout.n_c
        self.pieces = [
            [
                layout.fetch(
                    table,
                    gathered,
                    core,
                    range(b * n_c, (b + 1) * n_c),
                    features.at[core, b],
                    sems.at[core, b],
                    0,
                )
                for b in range(layout.blocks)
            ]
            for core in range(n_c)
        ]
        self.weights = [
            pltpu.make_async_copy(ref, buffer, w_sems.at[b])
            for b, (ref, buffer) in enumerate(zip(weights, buffers))
        ]
        for core in range(n_c):
            for b in range(layout.blocks):
                if core == 0:
                    self.weights[b].start()
                start_all(self.pieces[core][b])

    def run(self, total, parts, product, finish):
        last = self.layout.blocks - 1
        for core in range(self.layout.n_c):
            for b in range(last + 1):
                if core == 0:
                    self.weights[b].wait()
                wait_all(self.pieces[core][b])
                for part in parts:
                    term = product(self.features[core, b], self.buffers[b], part)
                    if 0 < b:
                        term = total[:, part] + term
                    if b < last:
                        total[:, part] = term
                    else:
                        finish(core, part, term)

    @staticmethod
    def scratch(layout, shape, outputs):
        n_c, count = layout.n_c, layout.blocks
        return [
            pltpu.VMEM((n_c, count, layout.own_tokens, layout.block), BF16),
            *[pltpu.VMEM(shape, BF16) for _ in range(count)],
            pltpu.SemaphoreType.DMA((n_c, count, n_c)),
            pltpu.SemaphoreType.DMA((count,)),
            pltpu.VMEM((layout.own_tokens, outputs), F32),
        ]


def chunks(size, step=256):
    step = math.gcd(size, step)
    return [slice(begin, begin + step) for begin in range(0, size, step)]


def project_qkv(layout, table, gathered, blocks, bias, tables):
    columns = bias.shape[1] // 3
    rows, count = layout.own_tokens, layout.blocks

    def body(table_ref, g_ref, *rest):
        w_refs, rest = rest[:count], rest[count:]
        bias_ref, cos_ref, low_ref, up_ref, q_ref, kv_ref, features = rest[:7]
        buffers, (sems, w_sems, total) = rest[7 : 7 + count], rest[7 + count :]
        window = slice(0, 3 * columns)
        stream = Stream(layout, table_ref, g_ref, w_refs, features, buffers, sems, w_sems, window)

        def finish(core, part, value):
            here = slice(core * rows, (core + 1) * rows)
            value = value + bias_ref[:, part]
            for lanes in chunks(columns, LANES):
                piece = value[:, lanes]
                if part.start < 2 * columns:
                    piece = rope(piece, cos_ref[here], low_ref[here], up_ref[here])
                begin = part.start + lanes.start
                if part.start < columns:
                    q_ref[here, begin : begin + LANES] = piece.astype(BF16)
                else:
                    kv_ref[here, begin - columns : begin - columns + LANES] = piece.astype(BF16)

        stream.run(
            total,
            [slice(i * columns, (i + 1) * columns) for i in range(3)],
            lambda f, w, part: jnp.dot(f, w[:, part], preferred_element_type=F32),
            finish,
        )

    out = [
        jax.ShapeDtypeStruct((layout.tokens, columns), BF16),
        jax.ShapeDtypeStruct((layout.tokens, 2 * columns), BF16),
    ]
    return kernel_call(
        body,
        table,
        [gathered, *blocks, bias, *tables],
        [ANY] * (1 + count) + [full(bias)] + [full(t) for t in tables],
        out,
        [full(o) for o in out],
        Stream.scratch(layout, (layout.block, 3 * columns), 3 * columns),
        "project_qkv",
    )


def gelu_and_slope(v):
    inner = math.sqrt(2 / math.pi) * v * (1.0 + 0.044715 * v * v)
    curve = jnp.tanh(inner)
    slope = 0.5 * (1.0 + curve) + 0.5 * v * (1.0 - curve * curve) * math.sqrt(2 / math.pi) * (
        1.0 + 3 * 0.044715 * v * v
    )
    return 0.5 * v * (1.0 + curve), slope


def project_up(layout, table, gathered, blocks, bias, active_grad=None):
    hidden = bias.shape[1]
    window = slice(blocks[0].shape[1] - hidden, blocks[0].shape[1])
    rows, count = layout.own_tokens, layout.blocks
    known = active_grad is not None

    def body(table_ref, g_ref, *rest):
        w_refs, rest = rest[:count], rest[count:]
        if known:
            grad_ref, rest = rest[0], rest[1:]
        bias_ref, act_ref, slope_ref, features = rest[:4]
        buffers, (sems, w_sems, total, act_buf, slope_buf, out_sems) = rest[4 : 4 + count], rest[4 + count :]
        stream = Stream(layout, table_ref, g_ref, w_refs, features, buffers, sems, w_sems, window)
        outs = []
        parts = chunks(hidden)

        def finish(core, part, value):
            here = slice(core * rows, (core + 1) * rows)
            active, slope = gelu_and_slope(value + bias_ref[:, part])
            act_buf[here, part] = active.astype(BF16)
            if known:
                slope = slope * grad_ref[here, part].astype(F32)
            slope_buf[here, part] = slope.astype(BF16)
            if part.stop == hidden:
                for i, (buffer, ref) in enumerate(((act_buf, act_ref), (slope_buf, slope_ref))):
                    outs.append(
                        pltpu.make_async_copy(buffer.at[here], ref.at[here], out_sems.at[core, i])
                    )
                    outs[-1].start()

        stream.run(
            total,
            parts,
            lambda f, w, part: jnp.dot(f, w[:, part], preferred_element_type=F32),
            finish,
        )
        wait_all(outs)

    out = [jax.ShapeDtypeStruct((layout.tokens, hidden), BF16)] * 2
    extra = [active_grad] if known else []
    return kernel_call(
        body,
        table,
        [gathered, *blocks, *extra, bias],
        [ANY] * (1 + count) + [full(e) for e in extra] + [full(bias)],
        out,
        [ANY, ANY],
        Stream.scratch(layout, (layout.block, hidden), hidden)
        + [pltpu.VMEM((layout.tokens, hidden), BF16)] * 2
        + [pltpu.SemaphoreType.DMA((layout.n_c, 2))],
        "project_up",
    )


def branch_grads(layout, table, gathered, blocks, columns, slope=None):
    rows, count = layout.own_tokens, layout.blocks
    height = blocks[0].shape[0]
    hidden = height - columns
    known = slope is not None

    def body(table_ref, g_ref, *rest):
        w_refs, rest = rest[:count], rest[count:]
        if known:
            slope_ref, rest = rest[0], rest[1:]
        mixed_ref, hidden_ref, features = rest[:3]
        buffers, (sems, w_sems, total, mixed_buf, hidden_buf, out_sems) = (
            rest[3 : 3 + count],
            rest[3 + count :],
        )
        stream = Stream(layout, table_ref, g_ref, w_refs, features, buffers, sems, w_sems)
        outs = []

        def finish(core, part, value):
            here = slice(core * rows, (core + 1) * rows)
            if part.start < columns:
                mixed_buf[here, part] = value.astype(BF16)
            else:
                to = slice(part.start - columns, part.stop - columns)
                if known:
                    value = value * slope_ref[here, to].astype(F32)
                hidden_buf[here, to] = value.astype(BF16)
            if part.stop == height:
                for i, (buffer, ref) in enumerate(((mixed_buf, mixed_ref), (hidden_buf, hidden_ref))):
                    outs.append(
                        pltpu.make_async_copy(buffer.at[here], ref.at[here], out_sems.at[core, i])
                    )
                    outs[-1].start()

        stream.run(
            total,
            chunks(height, math.gcd(columns, 256)),
            lambda f, w, part: contract(f, w[part, :], 1, 1),
            finish,
        )
        wait_all(outs)

    out = [
        jax.ShapeDtypeStruct((layout.tokens, columns), BF16),
        jax.ShapeDtypeStruct((layout.tokens, hidden), BF16),
    ]
    extra = [slope] if known else []
    return kernel_call(
        body,
        table,
        [gathered, *blocks, *extra],
        [ANY] * (1 + count) + [full(e) for e in extra],
        out,
        [ANY, ANY],
        Stream.scratch(layout, blocks[0].shape, height)
        + [pltpu.VMEM(o.shape, BF16) for o in out]
        + [pltpu.SemaphoreType.DMA((layout.n_c, 2))],
        "branch_grads",
    )


def project_back(layout, table, lefts, weights, transposed, name):
    rows, count = layout.own_tokens, len(weights)
    per_block = len(weights[0])
    sizes = [left.shape[1] for left in lefts]
    flat = [w for block in weights for w in block]
    n = len(lefts)

    def body(table_ref, *rest):
        left_refs, rest = rest[:n], rest[n:]
        w_refs, rest = rest[: len(flat)], rest[len(flat) :]
        out_refs, rest = rest[:3], rest[3:]
        left_bufs, rest = rest[:n], rest[n:]
        w_bufs, (out_buf, sems, w_sems, out_sems) = rest[: len(flat)], rest[len(flat) :]
        core = table_ref[2 * layout.places]
        copies = []
        for half, which in enumerate((lax.rem(core + 1, layout.n_c), core)):
            begin = pl.multiple_of(which * rows, rows)
            copies.append(
                [
                    pltpu.make_async_copy(
                        ref.at[pl.ds(begin, rows), :], buf.at[half], sems.at[half, i]
                    )
                    for i, (ref, buf) in enumerate(zip(left_refs, left_bufs))
                ]
            )
        w_copies = [
            pltpu.make_async_copy(ref, buf, w_sems.at[i])
            for i, (ref, buf) in enumerate(zip(w_refs, w_bufs))
        ]
        start_all(copies[0] + w_copies)
        start_all(copies[1])
        outs = []
        for half in range(2):
            wait_all(copies[half])
            for b in range(count):
                if half == 0:
                    wait_all(w_copies[b * per_block : (b + 1) * per_block])
                total = None
                at = 0
                for i, buf in enumerate(left_bufs):
                    if per_block == 1:
                        here = slice(at, at + sizes[i])
                        w = w_bufs[b][:, here] if transposed else w_bufs[b][here, :]
                        at += sizes[i]
                    else:
                        w = w_bufs[b * per_block + i][...]
                    term = contract(buf[half], w, 1, 1 if transposed else 0)
                    total = term if total is None else total + term
                out_buf[half, :, b * layout.block : (b + 1) * layout.block] = total.astype(BF16)
            pieces = [out_buf.at[0, : rows // 2], out_buf.at[0, rows // 2 :]] if half == 0 else [out_buf.at[1]]
            for piece in pieces:
                at = len(outs)
                outs.append(pltpu.make_async_copy(piece, out_refs[at], out_sems.at[at]))
                outs[-1].start()
        wait_all(outs)

    out = [jax.ShapeDtypeStruct((size, layout.width), BF16) for size in (rows // 2, rows // 2, rows)]
    return kernel_call(
        body,
        table,
        [*lefts, *flat],
        [ANY] * (n + len(flat)),
        out,
        [ANY] * 3,
        [pltpu.VMEM((2, rows, size), BF16) for size in sizes]
        + [pltpu.VMEM(w.shape, BF16) for w in flat]
        + [
            pltpu.VMEM((2, rows, layout.width), BF16),
            pltpu.SemaphoreType.DMA((2, n)),
            pltpu.SemaphoreType.DMA((len(flat),)),
            pltpu.SemaphoreType.DMA((3,)),
        ],
        name,
    )


def merge_cores(layout, table, own, received):
    rows = layout.own_tokens // 2
    place, places, n_c = layout.place, layout.places, layout.n_c

    def body(table_ref, own_ref, first_ref, second_ref, out_ref):
        def write(other_ref):
            for at in range(places):
                begin = pl.multiple_of(table_ref[2 * places + 1 + at], place)
                there = at // n_c * n_c + (n_c - at % n_c) % n_c if n_c != 2 else at ^ 1
                total = own_ref[:, at * place : (at + 1) * place].astype(F32)
                total = total + other_ref[:, there * place : (there + 1) * place].astype(F32)
                out_ref[:, pl.ds(begin, place)] = total.astype(BF16)

        pl.when(pl.program_id(0) == 0)(lambda: write(first_ref))
        pl.when(pl.program_id(0) == 1)(lambda: write(second_ref))

    spec = pl.BlockSpec((rows, layout.width), lambda i, t: (i, 0))
    return kernel_call(
        body,
        table,
        [own, *received],
        [spec] + [full(piece) for piece in received],
        jax.ShapeDtypeStruct((layout.own_tokens, layout.width), BF16),
        spec,
        [],
        "merge_cores",
        grid=(2,),
    )


def fetch_blocks(layout, table, gathered, which, features, sems):
    n_c, rows = layout.n_c, layout.own_tokens
    return [
        [
            layout.fetch(
                table,
                gathered,
                core,
                range(b * n_c, (b + 1) * n_c),
                features.at[i, pl.ds(core * rows, rows), :],
                sems.at[i, core],
                0,
            )
            for core in range(n_c)
        ]
        for i, b in enumerate(which)
    ]


def grad_in(layout, table, gathered, right, which, added=None):
    n = right.shape[1]
    count, place, n_c, block = len(which), layout.place, layout.n_c, layout.block
    final = added is not None
    extra = list(added or [])

    def body(table_ref, g_ref, right_ref, *rest):
        add_refs, rest = rest[: len(extra)], rest[len(extra) :]
        outs, rest = rest[: len(out)], rest[len(out) :]
        features, right_buf, sems, right_sem, rest = *rest[:4], rest[4:]
        pieces = fetch_blocks(layout, table_ref, g_ref, which, features, sems)
        right_copy = pltpu.make_async_copy(right_ref, right_buf, right_sem)
        right_copy.start()
        for group in pieces:
            for piece in group:
                start_all(piece)
        add_bufs, rest = rest[: len(extra)], rest[len(extra) :]
        if final:
            add_sems, rest = rest[0], rest[1:]
            add_copies = [
                pltpu.make_async_copy(ref, buf, add_sems.at[i])
                for i, (ref, buf) in enumerate(zip(add_refs, add_bufs))
            ]
            start_all(add_copies)
        right_copy.wait()
        if not final:
            out_buf, out_sems = rest
        copies = []
        for i in range(count):
            for piece in pieces[i]:
                wait_all(piece)
            if final and i == 0:
                wait_all(add_copies)
            for k in range(n_c):
                value = contract(features[i, :, k * place : (k + 1) * place], right_buf[...], 0, 0)
                begin = i * block + k * place
                if not final:
                    out_buf[begin : begin + place, :] = value.astype(BF16)
                    continue
                for buf in add_bufs:
                    value = value + buf[begin : begin + place, :].astype(F32)
                if k > 0:
                    away = outs[2] if i == 0 else outs[3]
                    at = (max(i - 1, 0) * (n_c - 1) + k - 1) * place
                    away[at : at + place, :] = value.astype(BF16)
                elif i == 0:
                    outs[0][...] = value
                else:
                    outs[1][(i - 1) * place : i * place, :] = value.astype(BF16)
            if not final:
                here = slice(i * block, (i + 1) * block)
                copies.append(pltpu.make_async_copy(out_buf.at[here], outs[0].at[here], out_sems.at[i]))
                copies[-1].start()
        wait_all(copies)

    if final:
        away = (n_c - 1) * place
        out = [
            jax.ShapeDtypeStruct((place, n), F32),
            jax.ShapeDtypeStruct(((count - 1) * place, n), BF16),
            jax.ShapeDtypeStruct((away, n), BF16),
            jax.ShapeDtypeStruct(((count - 1) * away, n), BF16),
        ]
        more = [pltpu.VMEM(e.shape, BF16) for e in extra]
        more.append(pltpu.SemaphoreType.DMA((len(extra),)))
    else:
        out = [jax.ShapeDtypeStruct((count * block, n), BF16)]
        more = [pltpu.VMEM(out[0].shape, BF16), pltpu.SemaphoreType.DMA((count,))]
    return kernel_call(
        body,
        table,
        [gathered, right, *extra],
        [ANY] * (2 + len(extra)),
        out,
        [full(o) for o in out] if final else [ANY],
        [
            pltpu.VMEM((count, layout.tokens, block), BF16),
            pltpu.VMEM(right.shape, BF16),
            pltpu.SemaphoreType.DMA((count, n_c, n_c)),
            pltpu.SemaphoreType.DMA,
        ]
        + more,
        "grad_in",
    )


def grad_out(layout, table, lefts, gathered, which, added=None):
    sizes = [left.shape[1] for left in lefts]
    m, n = sum(sizes), len(lefts)
    count, place, n_c, block = len(which), layout.place, layout.n_c, layout.block
    final = added is not None
    extra = [e for block_added in added for e in block_added] if final else []
    per_block = len(extra) // count

    def body(table_ref, g_ref, *rest):
        left_refs, rest = rest[:n], rest[n:]
        add_refs, rest = rest[: len(extra)], rest[len(extra) :]
        outs, rest = rest[: len(out)], rest[len(out) :]
        features, sems, left_sems, rest = *rest[:3], rest[3:]
        left_bufs, rest = rest[:n], rest[n:]
        left_copies = [
            pltpu.make_async_copy(ref, buf, left_sems.at[i])
            for i, (ref, buf) in enumerate(zip(left_refs, left_bufs))
        ]
        pieces = fetch_blocks(layout, table_ref, g_ref, which, features, sems)
        start_all(left_copies[:1])
        for piece in pieces[0]:
            start_all(piece)
        start_all(left_copies[1:])
        for group in pieces[1:]:
            for piece in group:
                start_all(piece)
        add_bufs, rest = rest[: len(extra)], rest[len(extra) :]
        if final:
            add_sems, rest = rest[0], rest[1:]
            add_copies = [
                pltpu.make_async_copy(ref, buf, add_sems.at[i])
                for i, (ref, buf) in enumerate(zip(add_refs, add_bufs))
            ]
            start_all(add_copies)
        if not final:
            out_buf, out_sems = rest
        copies = []
        for i in range(count):
            for piece in pieces[i]:
                wait_all(piece)
            if final:
                wait_all(add_copies[i * per_block : (i + 1) * per_block])
            at = 0
            for j, (left_buf, size) in enumerate(zip(left_bufs, sizes)):
                if i == 0:
                    left_copies[j].wait()
                for part in chunks(size):
                    rows = slice(at + part.start, at + part.stop)
                    value = contract(left_buf[:, part], features[i], 0, 0)
                    if not final:
                        out_buf[i, rows, :] = value.astype(BF16)
                        continue
                    for buf in add_bufs[i * per_block : (i + 1) * per_block]:
                        value = value + buf[rows, :].astype(F32)
                    if i == 0:
                        outs[0][rows, :] = value[:, :place]
                        outs[2][rows, :] = value[:, place:].astype(BF16)
                    else:
                        outs[1][i - 1, rows, :] = value[:, :place].astype(BF16)
                        outs[3][i - 1, rows, :] = value[:, place:].astype(BF16)
                at += size
            if not final:
                copies.append(pltpu.make_async_copy(out_buf.at[i], outs[i], out_sems.at[i]))
                copies[-1].start()
        wait_all(copies)

    if final:
        out = [
            jax.ShapeDtypeStruct((m, place), F32),
            jax.ShapeDtypeStruct((count - 1, m, place), BF16),
            jax.ShapeDtypeStruct((m, block - place), BF16),
            jax.ShapeDtypeStruct((count - 1, m, block - place), BF16),
        ]
        more = [pltpu.VMEM(e.shape, BF16) for e in extra]
        more.append(pltpu.SemaphoreType.DMA((len(extra),)))
    else:
        out = [jax.ShapeDtypeStruct((m, block), BF16)] * count
        more = [pltpu.VMEM((count, m, block), BF16), pltpu.SemaphoreType.DMA((count,))]
    return kernel_call(
        body,
        table,
        [gathered, *lefts, *extra],
        [ANY] * (1 + n + len(extra)),
        out,
        [full(o) for o in out] if final else [ANY] * count,
        [
            pltpu.VMEM((count, layout.tokens, block), BF16),
            pltpu.SemaphoreType.DMA((count, n_c, n_c)),
            pltpu.SemaphoreType.DMA((n,)),
        ]
        + [pltpu.VMEM(left.shape, BF16) for left in lefts]
        + more,
        "grad_out",
    )


def place_in(layout, table, layer, owns, others, shape, held, parts):
    rows, n = owns[0].shape
    step = n // parts
    inputs = [*owns, *others]

    def body(table_ref, *refs):
        refs, out_ref = refs[: len(inputs)], refs[-1]

        def write(sources):
            value = sum(ref[...].astype(F32) for ref in sources)
            if parts == 1:
                out_ref[...] = value
            else:
                for i in range(parts):
                    out_ref[:, i, :] = value[:, i * step : (i + 1) * step]

        pl.when(pl.program_id(0) == 0)(lambda: write(refs[: len(owns)]))
        pl.when(pl.program_id(0) == 1)(lambda: write(refs[len(owns) :]))

    half = lambda i, t: lax.rem(t[2 * layout.places] + i, layout.n_c)
    if parts == 1:
        spec = pl.BlockSpec((None, rows, n), lambda i, t: (layer, 0, half(i, t)))
    else:
        spec = pl.BlockSpec((None, rows, parts, step), lambda i, t: (layer, 0, 0, half(i, t)))
    more = [] if held is None else [held]
    return kernel_call(
        body,
        table,
        inputs + more,
        [full(v) for v in inputs] + [ANY] * len(more),
        jax.ShapeDtypeStruct(shape, F32),
        spec,
        [],
        "place_in",
        grid=(2,),
        aliases={1 + len(inputs): 0} if more else None,
    )


def place_out(layout, table, layer, owns, others, shapes, held):
    m, place = owns[0].shape
    inputs = [*owns, *others]
    sizes = [shape[1] // layout.n_c for shape in shapes]
    more = [] if held is None else list(held)

    def body(table_ref, *refs):
        refs, out_refs = refs[: len(inputs)], refs[len(inputs) + len(more) :]

        def write(sources):
            at = 0
            for ref, size in zip(out_refs, sizes):
                ref[...] = sum(source[at : at + size, :].astype(F32) for source in sources)
                at += size

        pl.when(pl.program_id(0) == 0)(lambda: write(refs[: len(owns)]))
        pl.when(pl.program_id(0) == 1)(lambda: write(refs[len(owns) :]))

    half = lambda i, t: lax.rem(t[2 * layout.places] + i, layout.n_c)
    return kernel_call(
        body,
        table,
        inputs + more,
        [full(v) for v in inputs] + [ANY] * len(more),
        [jax.ShapeDtypeStruct(shape, F32) for shape in shapes],
        [pl.BlockSpec((None, size, place), lambda i, t: (layer, half(i, t), 0)) for size in sizes],
        [],
        "place_out",
        grid=(2,),
        aliases={1 + len(inputs) + i: i for i in range(len(more))} or None,
    )


def head_part(value, head):
    lane = lax.broadcasted_iota(jnp.int32, value.shape, 1)
    keep = (lane >= head * HEAD_DIM) & (lane < (head + 1) * HEAD_DIM)
    return jnp.where(keep, value, jnp.zeros_like(value))


def mask_bias(query_begin, key_begin, starts, shape, key_axis):
    key_place = key_begin + lax.broadcasted_iota(jnp.int32, shape, key_axis)
    query_place = query_begin + lax.broadcasted_iota(jnp.int32, shape, 1 - key_axis)
    allowed = (key_place >= starts) & (key_place <= query_place)
    return jnp.where(allowed, 0.0, NEGATIVE).astype(F32)


def attend(begins, queries, key_values, starts, before=None):
    tokens, columns = queries.shape
    own = before is None
    block_q = math.gcd(tokens, 256 if own else 512)
    heads, pairs = columns // HEAD_DIM, columns // LANES
    keys = key_values.shape[0]
    steps = tokens // block_q
    tall = LANES + 16

    def body(begin_ref, q_ref, kv_ref, start_ref, *rest):
        if not own:
            (old_ref, old_log_ref), rest = rest[:2], rest[2:]
        low_ref, mixed_ref, log_ref, turned = rest
        step = pl.program_id(0)

        @pl.when(step == 0)
        def _():
            for pair in range(pairs):
                there = slice(columns + pair * LANES, columns + (pair + 1) * LANES)
                turned[pair * tall : pair * tall + LANES, :] = kv_ref[:, there].T
                turned[pair * tall + LANES : (pair + 1) * tall, :] = jnp.ones((16, keys), BF16)

        def work(count, at):
            bias = mask_bias(
                begin_ref[0] + at * block_q, begin_ref[1], start_ref[...], (count, block_q), 0
            )
            for pair in range(pairs):
                here = slice(pair * LANES, (pair + 1) * LANES)
                q = q_ref[:, here] * jnp.asarray(HEAD_DIM**-0.5, BF16)
                shares, terms = [], []
                for head in range(HEADS_TILE):
                    index = HEADS_TILE * pair + head
                    score = contract(kv_ref[:count, here], head_part(q, head), 1, 1) + bias
                    top = jnp.max(score, axis=0, keepdims=True)
                    weight = jnp.exp(score - top).astype(BF16)
                    found = jnp.dot(
                        turned[pair * tall : (pair + 1) * tall, :count],
                        weight,
                        preferred_element_type=F32,
                    )
                    value = found[head * HEAD_DIM : (head + 1) * HEAD_DIM]
                    total = found[LANES : LANES + 1]
                    joined = top + jnp.log(total)
                    if own:
                        value = value * (1.0 / total)
                    else:
                        old = old_log_ref[index : index + 1, :]
                        most = jnp.maximum(old, joined)
                        joined = most + jnp.log(jnp.exp(old - most) + jnp.exp(joined - most))
                        value = value * jnp.exp(top - joined)
                        shares.append(jnp.broadcast_to(jnp.exp(old - joined), value.shape))
                    log_ref[index : index + 1, :] = joined
                    terms.append(value)
                value = jnp.concatenate(terms, axis=0).T
                if not own:
                    value = value + old_ref[:, here] * jnp.concatenate(shares, axis=0).T
                mixed_ref[:, here] = value
                low_ref[:, here] = value.astype(BF16)

        if own:
            for at in range(steps):
                pl.when(step == at)(lambda at=at: work((at + 1) * block_q, at))
        else:
            work(keys, step)

    row = lambda i, s: (i, 0)
    lane = lambda i, s: (0, i)
    wide = pl.BlockSpec((block_q, columns), row)
    slim = pl.BlockSpec((heads, block_q), lane)
    extra = [] if own else list(before)
    return kernel_call(
        body,
        begins,
        [queries, key_values, starts, *extra],
        [wide, full(key_values), pl.BlockSpec((1, block_q), lane)] + ([] if own else [wide, slim]),
        [
            jax.ShapeDtypeStruct((tokens, columns), BF16),
            jax.ShapeDtypeStruct((tokens, columns), F32),
            jax.ShapeDtypeStruct((heads, tokens), F32),
        ],
        [wide, wide, slim],
        [pltpu.VMEM((pairs * tall, keys), BF16)],
        "attend_own" if own else "attend_far",
        grid=(steps,),
    )


def attend_backward(begins, queries, key_values, starts, mixed, logs, mixed_grad, own, before=None):
    tokens, columns = queries.shape
    block_q = math.gcd(tokens, 256)
    heads = columns // HEAD_DIM
    keys = key_values.shape[0]
    steps = tokens // block_q
    scale = HEAD_DIM**-0.5
    pairs = columns // LANES

    def body(begin_ref, q_ref, kv_ref, start_ref, mixed_ref, log_ref, grad_ref, *rest):
        if before is not None:
            before_ref, rest = rest[0], rest[1:]
        dq_ref, dkv_ref, turned, key_sum, value_sum = rest
        step = pl.program_id(0)

        @pl.when(step == 0)
        def _():
            key_sum[...] = jnp.zeros_like(key_sum)
            value_sum[...] = jnp.zeros_like(value_sum)
            for pair in range(pairs):
                here = slice(pair * LANES, (pair + 1) * LANES)
                turned[here, :] = kv_ref[:, here].T

        def work(count, at):
            bias = mask_bias(
                begin_ref[0] + at * block_q, begin_ref[1], start_ref[...], (count, block_q), 0
            )
            for pair in range(pairs):
                here = slice(pair * LANES, (pair + 1) * LANES)
                there = slice(columns + pair * LANES, columns + (pair + 1) * LANES)
                q, grad = q_ref[:, here], grad_ref[:, here]
                product = (mixed_ref[:, here] * grad.astype(F32)).T
                k, v = kv_ref[:count, here], kv_ref[:count, there]
                key_terms, value_terms, query_terms = [], [], []
                for head in range(HEADS_TILE):
                    q_head, grad_head = head_part(q, head), head_part(grad, head)
                    inner = slice(head * HEAD_DIM, (head + 1) * HEAD_DIM)
                    delta = jnp.sum(product[inner], axis=0, keepdims=True)
                    index = HEADS_TILE * pair + head
                    score = contract(k, q_head, 1, 1) * scale + bias
                    weight = jnp.exp(score - log_ref[index : index + 1, :])
                    weight_grad = contract(v, grad_head, 1, 1)
                    score_grad = (weight * (weight_grad - delta)).astype(BF16)
                    value_terms.append(
                        jnp.dot(weight.astype(BF16), grad_head, preferred_element_type=F32)
                    )
                    key_terms.append(jnp.dot(score_grad, q_head, preferred_element_type=F32))
                    begin = pair * LANES + head * HEAD_DIM
                    query_terms.append(
                        jnp.dot(
                            turned[begin : begin + HEAD_DIM, :count],
                            score_grad,
                            preferred_element_type=F32,
                        )
                    )
                value_sum[:count, here] += value_terms[0] + value_terms[1]
                key_sum[:count, here] += key_terms[0] + key_terms[1]
                found = jnp.concatenate(query_terms, axis=0).T * scale
                if before is not None:
                    found = found + before_ref[:, here]
                dq_ref[:, here] = found

        if own:
            for at in range(steps):
                pl.when(step == at)(lambda at=at: work((at + 1) * block_q, at))
        else:
            work(keys, step)

        @pl.when(step == steps - 1)
        def _():
            dkv_ref[:, :columns] = (key_sum[...] * scale).astype(dkv_ref.dtype)
            dkv_ref[:, columns:] = value_sum[...].astype(dkv_ref.dtype)

    row = lambda i, s: (i, 0)
    lane = lambda i, s: (0, i)
    wide = pl.BlockSpec((block_q, columns), row)
    extra = [] if before is None else [before]
    out = [
        jax.ShapeDtypeStruct((tokens, columns), F32),
        jax.ShapeDtypeStruct((keys, 2 * columns), F32 if own else BF16),
    ]
    return kernel_call(
        body,
        begins,
        [queries, key_values, starts, mixed, logs, mixed_grad, *extra],
        [
            wide,
            full(key_values),
            pl.BlockSpec((1, block_q), lane),
            wide,
            pl.BlockSpec((heads, block_q), lane),
            wide,
        ]
        + [wide] * len(extra),
        out,
        [wide, full(out[1])],
        [
            pltpu.VMEM((columns, keys), BF16),
            pltpu.VMEM((keys, columns), F32),
            pltpu.VMEM((keys, columns), F32),
        ],
        "attend_backward",
        grid=(steps,),
    )


def join_qkv_grads(table, query_grad, own_pairs, far_pairs, tables):
    tokens, columns = query_grad.shape
    rows = math.gcd(tokens, 512)

    def body(table_ref, q_ref, own_ref, *rest):
        far_refs, (cos_ref, low_ref, up_ref, out_ref, sum_ref) = rest[: len(far_pairs)], rest[len(far_pairs) :]

        @pl.when(pl.program_id(0) == 0)
        def _():
            sum_ref[...] = jnp.zeros_like(sum_ref)

        cosine, lower, upper = cos_ref[...], -low_ref[...], -up_ref[...]
        for tile in range(3 * columns // LANES):
            here = slice(tile * LANES, (tile + 1) * LANES)
            if tile < columns // LANES:
                value = q_ref[:, here]
            else:
                there = slice(tile * LANES - columns, (tile + 1) * LANES - columns)
                value = own_ref[:, there]
                for ref in far_refs:
                    value = value + ref[:, there].astype(F32)
            if tile < 2 * columns // LANES:
                value = rope(value, cosine, lower, upper)
            low = value.astype(BF16)
            out_ref[:, here] = low
            sum_ref[:, here] += jnp.sum(low.astype(F32), axis=0, keepdims=True)

    row = lambda i, s: (i, 0)
    spec = lambda array: pl.BlockSpec((rows, array.shape[1]), row)
    out = [
        jax.ShapeDtypeStruct((tokens, 3 * columns), BF16),
        jax.ShapeDtypeStruct((1, 3 * columns), F32),
    ]
    inputs = [query_grad, own_pairs, *far_pairs, *tables]
    return kernel_call(
        body,
        table,
        inputs,
        [spec(array) for array in inputs],
        out,
        [spec(out[0]), full(out[1])],
        [],
        "join_qkv_grads",
        grid=(tokens // rows,),
    )


def core_half(value, axis, which):
    size = value.shape[axis] // lax.axis_size("core")
    return lax.dynamic_slice_in_dim(value, which * size, size, axis)


def in_core_order(own, other, axis):
    core = lax.axis_index("core")
    return jnp.where(
        core == 0,
        jnp.concatenate([own, other], axis=axis),
        jnp.concatenate([other, own], axis=axis),
    )


class Gather:
    def __init__(self, order, block, first, second):
        self.order, self.first, self.second = order, first, second
        self.n1, self.n2 = lax.axis_size(first), lax.axis_size(second)
        self.found = {(0, 0): block}

    def near(self, depth=1):
        for i in range(1, self.n1):
            self.found[i, 0] = self.order.send(self.found[0, 0], self.first, i, depth)

    def side(self, depth=1):
        for j in range(1, self.n2):
            self.found[0, j] = self.order.send(self.found[0, 0], self.second, j, depth)

    def cross(self, depth=1):
        for i in range(1, self.n1):
            for j in range(1, self.n2):
                self.found[i, j] = self.order.send(self.found[i, 0], self.second, j, depth)

    def blocks(self):
        if self.first == "x":
            return [self.found[b, a] for a in range(self.n2) for b in range(self.n1)]
        return [self.found[a, b] for a in range(self.n1) for b in range(self.n2)]


class ScatterIn:
    def __init__(self, order, layout, table, features, right):
        self.order, self.layout, self.table = order, layout, table
        self.features, self.right = features, right

    parts = None

    def compute(self):
        layout, n_x = self.layout, self.layout.n_x
        which = [a * n_x + b for a in range(1, layout.n_y) for b in range(n_x)]
        (self.parts,) = self.order.run(
            lambda f, r: grad_in(layout, self.table, f, r, which), self.features, self.right
        )

    def begin(self, depth=1):
        if self.parts is None:
            self.compute()
        size = self.layout.n_x * self.layout.block
        self.received = [
            self.order.send(self.parts[(a - 1) * size : a * size], "dp", -a, depth)
            for a in range(1, self.layout.n_y)
        ]

    def middle(self):
        layout = self.layout
        self.first, self.others, away, others_away = self.order.run(
            lambda f, r, d: grad_in(layout, self.table, f, r, range(layout.n_x), d),
            self.features,
            self.right,
            self.received,
        )
        self.others_away = self.order.send(others_away, "core", 1, 1)
        self.away = self.order.send(away, "core", 1, 2)

    def finish(self, depth=1):
        place = self.layout.place
        near, cross = [], []
        for b in range(1, self.layout.n_x):
            here = slice((b - 1) * place, b * place)
            near.append(self.order.send(self.others[here], "x", -b, depth))
            cross.append(self.order.send(self.others_away[here], "x", -b, depth + 1))
        self.sums = ([self.first, *near], [self.away, *cross])


class ScatterOut:
    def __init__(self, order, layout, table, lefts, grad):
        self.order, self.layout, self.table = order, layout, table
        self.lefts, self.grad = lefts, grad
        self.received = [[] for _ in range(layout.n_y)]

    def compute(self):
        layout, n_x = self.layout, self.layout.n_x
        which = [a * n_x + b for a in range(layout.n_y) for b in range(1, n_x)]
        self.parts = self.order.run(
            lambda l, g: grad_out(layout, self.table, l, g, which), self.lefts, self.grad
        )

    def begin(self, a, depth=1):
        n_x = self.layout.n_x
        for b in range(1, n_x):
            part = self.parts[a * (n_x - 1) + b - 1]
            self.received[a].append(self.order.send(part, "x", -b, depth))

    def middle(self):
        layout = self.layout
        which = [a * layout.n_x for a in range(layout.n_y)]
        self.first, self.others, away, others_away = self.order.run(
            lambda l, g, d: grad_out(layout, self.table, l, g, which, d),
            self.lefts,
            self.grad,
            self.received,
        )
        self.others_away = self.order.send(others_away, "core", 1, 1)
        self.away = self.order.send(away, "core", 1, 2)

    def finish(self, depth=1):
        near, cross = [], []
        for a in range(1, self.layout.n_y):
            near.append(self.order.send(self.others[a - 1], "dp", -a, depth))
            cross.append(self.order.send(self.others_away[a - 1], "dp", -a, depth + 1))
        self.sums = ([self.first, *near], [self.away, *cross])


def per_device(
    layer_input,
    segment_ids,
    positions,
    norm_gain,
    norm_bias,
    qkv_weight,
    qkv_bias,
    dense_weight,
    dense_bias,
    up_weight,
    up_bias,
    down_weight,
    down_bias,
    output_cotangent,
):
    layer_count = qkv_weight.shape[0]
    last = layer_count - 1
    core, x = lax.axis_index("core"), lax.axis_index("x")
    z, n_z = lax.axis_index("col"), lax.axis_size("col")
    layout = Layout(*layer_input.shape)
    n_x = layout.n_x
    tokens, width = layout.tokens, layout.width
    columns = qkv_weight.shape[3] // layout.n_c
    hidden = up_weight.shape[2] // layout.n_c
    table = width_table(layout)
    query_begin = x * tokens
    begins = [
        jnp.stack([query_begin, (x - b + n_x) % n_x * tokens]).astype(jnp.int32) for b in range(n_x)
    ]
    order = Order()


    def pieces_of(layer, group):
        which = order.after([core])[0]
        pieces = []
        for half in (which, 1 - which):
            if group == "out":
                parts = [core_half(w[layer], 0, half) for w in (dense_weight, down_weight)]
                pieces.append(jnp.concatenate(parts, axis=0))
                continue
            parts = []
            if group in ("qkv", "in"):
                parts.append(core_half(qkv_weight[layer], 2, half).reshape(-1, 3 * columns))
            if group in ("up", "in"):
                parts.append(core_half(up_weight[layer], 1, half))
            pieces.append(parts[0] if len(parts) == 1 else jnp.concatenate(parts, axis=1))
        return (*pieces, 1 if group == "out" else 0)

    def make_ready(layer, groups):
        pieces = [pieces_of(layer, group) for group in groups]
        swapped = [swap_core(other) for _, other, _ in pieces]
        blocks = [
            jnp.concatenate([own, other], axis=axis)
            for (own, _, axis), other in zip(pieces, swapped)
        ]
        for group, block in zip(groups, order.wait(*blocks)):
            ways = ("dp", "x") if group == "out" else ("x", "dp")
            gathers[layer, group] = Gather(order, block, *ways)

    def blocks_of(layer, group):
        if (layer, group) not in gathers:
            group = "in"
        return gathers[layer, group].blocks()


    def gather_features(block):
        return lax.all_gather(order.after([block])[0], ("core", "col"), axis=0, tiled=False)

    def scatter_features(summed):
        return lax.psum_scatter(order.after([summed])[0], "col", scatter_dimension=1, tiled=True)

    def to_owner(lefts, weights, transposed, name):
        *away, own = order.run(
            lambda *a: project_back(layout, table, a[0], a[1], transposed, name), lefts, weights
        )
        received = [order.send(piece, "core", 1, 2) for piece in away]
        return order.run(lambda a, b: merge_cores(layout, table, a, b), own, received)

    def moments(value, axes):
        mean = jnp.sum(value, axis=axes) / width
        return mean, jnp.sum(value * value, axis=axes) / width

    def inverse_of(mean, square):
        return lax.rsqrt(square - mean * mean + EPSILON)

    def normalise(residual, layer):
        stats = jnp.stack([jnp.sum(residual, axis=1), jnp.sum(residual * residual, axis=1)])
        stats = sum_over(stats, "col") / width
        inverse = inverse_of(stats[0], stats[1])
        centred = (residual - stats[0][:, None]) * inverse[:, None]
        return (centred * norm_gain[layer] + norm_bias[layer]).astype(BF16), centred, inverse

    def qkv_shift(layer):
        return core_half(qkv_bias[layer], 1, core).reshape(1, -1)

    def up_shift(layer):
        return core_half(up_bias[layer], 0, core).reshape(1, -1)

    def send_pairs(k, pairs):
        k["pairs"] = [pairs] + [order.send(pairs, "x", b) for b in range(1, n_x)]

    def project_q(layer):
        k = kept[layer]
        k["q"], pairs = order.run(
            lambda f, w, b, t: project_qkv(layout, table, f, w, b, t),
            k["features"],
            blocks_of(layer, "qkv"),
            qkv_shift(layer),
            tables,
        )
        send_pairs(k, pairs)

    def own_attention(layer):
        k = kept[layer]
        k["found"] = order.run(attend, begins[0], k["q"], k["pairs"][0], starts)

    def far_attention(layer):
        k = kept[layer]
        for b in range(1, n_x):
            k["found"] = order.run(
                attend, begins[b], k["q"], k["pairs"][b], starts, k["found"][1:]
            )
        k["mixed_low"], k["mixed"], k["logs"] = k["found"]

    def far_gradients(layer):
        k = kept[layer]
        query_grad, k["away_pairs"] = [], []
        for b in range(1, n_x):
            found, pair_grad = order.run(
                lambda *a: attend_backward(*a[:7], False, *a[7:]),
                begins[b],
                k["q"],
                k["pairs"][b],
                starts,
                k["mixed"],
                k["logs"],
                k["mixed_grad"],
                *query_grad,
            )
            query_grad = [found]
            k["away_pairs"].append(order.send(pair_grad, "x", -b))
        k["query_grad"] = query_grad

    def own_gradients(layer):
        k = kept[layer]
        k["query_grad"], k["own_pairs"] = order.run(
            lambda *a: attend_backward(*a[:7], True, *a[7:]),
            begins[0],
            k["q"],
            k["pairs"][0],
            starts,
            k["mixed"],
            k["logs"],
            k["mixed_grad"],
            *k["query_grad"],
        )

    def join_gradients(layer):
        k = kept[layer]
        k["qkv_low"], k["qkv_sum"] = order.run(
            lambda *a: join_qkv_grads(table, *a),
            k["query_grad"],
            k["own_pairs"],
            k["away_pairs"],
            tables,
        )

    gathers = {}
    kept = [dict() for _ in range(layer_count)]
    outputs = [None] * layer_count

    def out_pairs(layer):
        return [(block,) for block in gathers[layer, "out"].blocks()]

    def in_pairs(layer):
        if (layer, "in") in gathers:
            return [(block,) for block in gathers[layer, "in"].blocks()]
        return list(zip(gathers[layer, "qkv"].blocks(), gathers[layer, "up"].blocks()))


    def arrived(*transfers):
        order.wait(*transfers)

    residual = layer_input.astype(F32)
    raw = gather_features(layer_input)
    make_ready(0, ["qkv"])
    qkv, up, out = [None] * 3
    gathers[0, "qkv"].near()
    gathers[0, "qkv"].side()
    grad_features = gather_features(output_cotangent)
    make_ready(0, ["up", "out"])
    qkv, up, out = (gathers[0, group] for group in ("qkv", "up", "out"))
    arrived(qkv.found[1, 0], qkv.found[0, 1])
    up.near()
    qkv.cross()
    query_segments = lax.dynamic_slice_in_dim(segment_ids, query_begin, tokens, 0)
    starts = jnp.sum(
        (segment_ids[:, None] < query_segments[None, :]).astype(jnp.int32), axis=0, keepdims=True
    )
    places = lax.dynamic_slice_in_dim(positions, query_begin, tokens, 0)
    tables = rope_tables(order.after([places])[0])
    starts, *tables = order.wait(starts, *tables)
    affine = order.after([jnp.stack([norm_gain[0], norm_bias[0]])])[0]
    spread = [affine] + [shift(affine, "col", k) for k in range(1, n_z)]
    spread = jnp.stack(spread)[(z - jnp.arange(n_z) + n_z) % n_z]
    (spread,) = order.wait(spread)
    arrived(up.found[1, 0], *qkv.blocks()[1:])
    out.near()
    out.side()
    (raw,) = order.wait(raw)
    blocks = raw.reshape(layout.n_c, n_z, layout.own_tokens, layout.part).astype(F32)
    mean, square = moments(blocks, (1, 3))
    inverse = inverse_of(mean, square)
    gain, bias = (spread[:, i][None, :, None, :] for i in range(2))
    normed = (blocks - mean[:, None, :, None]) * inverse[:, None, :, None] * gain + bias
    kept[0]["features"] = normed.astype(BF16).reshape(raw.shape)
    kept[0]["inverse"] = lax.dynamic_index_in_dim(inverse, core, 0, keepdims=False)
    own_mean = lax.dynamic_index_in_dim(mean, core, 0, keepdims=False)
    (kept[0]["features"],) = order.wait(kept[0]["features"])
    for layer in range(last):
        k = kept[layer]
        project_q(layer)
        if layer == 0:
            up.side(2)
        own_attention(layer)
        arrived(*k["pairs"][1:])
        if layer == 0:
            arrived(up.found[0, 1], out.found[1, 0], out.found[0, 1])
            out.cross()
            up.cross()
        far_attention(layer)
        make_ready(layer + 1, ["in", "out"])
        in_next, out_next = gathers[layer + 1, "in"], gathers[layer + 1, "out"]
        if layer == 0:
            arrived(grad_features, *up.blocks()[1:])
        out_next.near()
        k["active"], k["slope"] = order.run(
            lambda f, w, b: project_up(layout, table, f, w, b),
            k["features"],
            blocks_of(layer, "up"),
            up_shift(layer),
        )
        arrived(*blocks_of(layer, "out")[1:])
        summed = to_owner([k["mixed_low"], k["active"]], out_pairs(layer), False, "project_out")
        arrived(*[out_next.found[a, 0] for a in range(1, layout.n_y)])
        branch = scatter_features(summed)
        order.wait(summed)
        in_next.near()
        in_next.side()
        arrived(*[v for at, v in in_next.found.items() if at != (0, 0)])
        (branch,) = order.wait(branch)
        residual = residual + branch.astype(F32) + dense_bias[layer] + down_bias[layer]
        outputs[layer] = residual
        normed, kept[layer + 1]["centred"], kept[layer + 1]["inverse"] = normalise(residual, layer + 1)
        (normed,) = order.wait(normed)
        kept[layer + 1]["features"] = gather_features(normed)
        order.wait(normed)
        out_next.side(1)
        out_next.cross(2)
        in_next.cross()
        arrived(*in_next.blocks()[1:])
        order.wait(kept[layer + 1]["features"])


    k = kept[last]
    project_q(last)
    k["mixed_grad"], k["active_grad"] = order.run(
        lambda g, w: branch_grads(layout, table, g, w, columns),
        grad_features,
        blocks_of(last, "out"),
    )
    k["active"], k["up_low"] = order.run(
        lambda f, w, b, g: project_up(layout, table, f, w, b, g),
        k["features"],
        blocks_of(last, "up"),
        up_shift(last),
        k["active_grad"],
    )
    arrived(*k["pairs"][1:])
    gradient = output_cotangent.astype(F32)
    sums = [None] * layer_count
    held = {"up": None, "qkv": None, "out": None}
    shapes = {
        "up": (layer_count, layout.place, layout.n_c * hidden),
        "qkv": (layer_count, layout.place, 3, layout.n_c * columns),
        "out": [
            (layer_count, layout.n_c * columns, layout.place),
            (layer_count, layout.n_c * hidden, layout.place),
        ],
    }

    def place(layer, group, scatter):
        if group == "out":
            held[group] = order.run(
                lambda a, b, h: place_out(layout, table, layer, a, b, shapes[group], h),
                *scatter.sums,
                held[group],
            )
        else:
            held[group] = order.run(
                lambda a, b, h: place_in(
                    layout, table, layer, a, b, shapes[group], h, 3 if group == "qkv" else 1
                ),
                *scatter.sums,
                held[group],
            )

    def norm_backward(layer, normed_grad, gradient):
        k = kept[layer]
        normed_grad = normed_grad.astype(F32)
        scaled_grad = normed_grad * norm_gain[layer]
        means = jnp.stack(
            [jnp.sum(scaled_grad, axis=1), jnp.sum(scaled_grad * k["centred"], axis=1)]
        )
        means = sum_over(means, "col") / width
        new = gradient + k["inverse"][:, None] * (
            scaled_grad - means[0][:, None] - k["centred"] * means[1][:, None]
        )

        def to_both(value):
            return in_core_order(value, jnp.zeros_like(value), value.ndim - 1).reshape(-1)

        sums[layer] = jnp.concatenate(
            [
                jnp.sum(normed_grad * k["centred"], axis=0),
                jnp.sum(normed_grad, axis=0),
                to_both(k["qkv_sum"].reshape(3, columns)),
                jnp.sum(gradient, axis=0),
                to_both(jnp.sum(k["up_low"], axis=0, dtype=F32)),
            ]
        )
        return new

    kept[0]["centred"] = (layer_input.astype(F32) - own_mean[:, None]) * kept[0]["inverse"][:, None]

    for layer in reversed(range(layer_count)):
        k = kept[layer]
        if layer < last:
            (grad_features,) = order.wait(grad_features)
            if layer + 1 == last:
                branch = scatter_features(out_summed)
                outputs[last] = residual + branch.astype(F32) + dense_bias[last] + down_bias[last]
            k["mixed_grad"], k["up_low"] = order.run(
                lambda g, w, s: branch_grads(layout, table, g, w, columns, s),
                grad_features,
                blocks_of(layer, "out"),
                k["slope"],
            )
        up = ScatterIn(order, layout, table, k["features"], k["up_low"])
        out_lefts = lambda: [k["mixed_low"], k["active"]]
        if layer == last:
            up.begin()
            own_attention(last)
            far_attention(last)
            out = ScatterOut(order, layout, table, out_lefts(), grad_features)
        else:
            out = ScatterOut(order, layout, table, out_lefts(), grad_features)
            out.compute()
            out.begin(layout.n_y - 1)
            up.begin()
        far_gradients(layer)
        own_gradients(layer)
        if layer == last:
            out.compute()
            arrived(*up.received)
            up.middle()
        arrived(*k["away_pairs"])
        join_gradients(layer)
        qkv = ScatterIn(order, layout, table, k["features"], k["qkv_low"])
        if layer == last:
            summed = to_owner([k["qkv_low"], k["up_low"]], in_pairs(layer), True, "feature_grads")
            normed_grad = scatter_features(summed)
            order.wait(summed)
            for a in range(layout.n_y):
                out.begin(a, 1)
            qkv.begin()
            out_summed = to_owner([k["mixed_low"], k["active"]], out_pairs(layer), False, "project_out")
            arrived(*qkv.received)
            qkv.middle()
            (normed_grad,) = order.wait(normed_grad)
            gradient = norm_backward(layer, normed_grad, gradient)
            (low,) = order.wait(gradient.astype(BF16))
            arrived(*[v for row in out.received for v in row])
            grad_features = gather_features(low)
            order.wait(low)
            up.finish()
            qkv.finish(2)
            out.middle()
            out.finish()
            place(layer, "up", up)
            place(layer, "qkv", qkv)
            place(layer, "out", out)
        else:
            for a in range(layout.n_y - 1):
                out.begin(a, 2)
            qkv.compute()
            qkv.begin(2)
            summed = to_owner([k["qkv_low"], k["up_low"]], in_pairs(layer), True, "feature_grads")
            arrived(*up.received, *qkv.received, *[v for row in out.received for v in row])
            normed_grad = scatter_features(summed)
            order.wait(summed)
            up.middle()
            up.finish(2)
            out.middle()
            out.finish(2)
            qkv.middle()
            qkv.finish(2)
            (normed_grad,) = order.wait(normed_grad)
            gradient = norm_backward(layer, normed_grad, gradient)
            if layer == 0:
                small = jnp.stack(sums)
                for axis in ("core", "x", "dp"):
                    small = sum_over(small, axis)
            place(layer, "up", up)
            place(layer, "out", out)
            place(layer, "qkv", qkv)

    small, gradient, outputs = order.now((small, gradient, outputs))
    held = order.now(held)
    part, both = layout.part, layout.n_c * columns
    ends = [0]
    for size in (part, part, 3 * both, part, layout.n_c * hidden):
        ends.append(ends[-1] + size)
    gain_grad, shift_grad, qkv_grad, out_bias_grad, up_grad = [
        small[:, begin:end] for begin, end in zip(ends[:-1], ends[1:])
    ]
    return (
        jnp.stack(outputs),
        gradient,
        gain_grad,
        shift_grad,
        held["qkv"],
        qkv_grad.reshape(layer_count, 3, both),
        held["out"][0],
        out_bias_grad,
        held["up"],
        up_grad,
        held["out"][1],
        out_bias_grad,
    )


def solution(mesh):
    n_y, n_row, n_z = (mesh.shape[name] for name in ("dp", "row", "col"))
    split = Mesh(mesh.devices.reshape(n_y, n_row // 2, 2, n_z), ("dp", "x", "core", "col"))
    rows = ("dp", "x", "core")
    placed = (
        P(rows, "col"),
        P("dp"),
        P("dp"),
        P(None, "col"),
        P(None, "col"),
        P(None, rows, None, "col"),
        P(None, None, "col"),
        P(None, "col", rows),
        P(None, "col"),
        P(None, rows, "col"),
        P(None, "col"),
        P(None, "col", rows),
        P(None, "col"),
        P(rows, "col"),
    )
    return jax.shard_map(
        per_device,
        mesh=split,
        in_specs=placed,
        out_specs=(
            P(None, rows, "col"),
            P(rows, "col"),
            P(None, "col"),
            P(None, "col"),
            P(None, rows, None, "col"),
            P(None, None, "col"),
            P(None, "col", rows),
            P(None, "col"),
            P(None, rows, "col"),
            P(None, "col"),
            P(None, "col", rows),
            P(None, "col"),
        ),
        check_vma=False,
    )
```

time: 1860 us -> 795 us (0.43)
  waiting for transfers between devices: 1400 us -> 290 us
  Pallas kernels: 0 us -> 274 us
  matrix products: 235 us -> 0 us
  blocking collectives: 71.9 us -> 0 us
  starting transfers between devices: 2.5 us -> 67.8 us
  local copies, waits for them, and re-layouts: 70.2 us -> 104 us
    reduce_scatter x16 -> x4, waiting for transfers between devices: 854 us -> 8.74 us  [scatter_features(): lax.psum_scatter(order.after([summed])[0], 'col', scatter_dimension=1, ti...]
    all_gather x16 -> x4, waiting for transfers between devices: 542 us -> 5.74 us  [gather_features(): lax.all_gather(order.after([block])[0], ('core', 'col'), axis=0, tiled=Fa...]
    ppermute x0 -> x76, waiting for transfers between devices: none -> 274 us  [the longest x67 255 us: shift(): lax.ppermute(value, axis, [(i, (i + step) % size) for i in range(size)])]
    pallas_call x0 -> x42, Pallas kernels: none -> 274 us  [kernel_call(): pl.pallas_call(body, grid_spec=pltpu.PrefetchScalarGridSpec(num_scalar_pr...]
    dot_general x42 -> x0, matrix products: 235 us -> none  [the longest x2 26.2 us: per_device(): jnp.einsum('td,fd->tf', grad_features, gathered_down, preferred_element_t...]
    psum x5 -> x0, blocking collectives: 71.9 us -> none  [the longest x1 25.1 us: per_device(): lax.psum((jnp.stack([entry[0] for entry in ordered_small]), jnp.stack([en...]
    ppermute x0 -> x76, starting transfers between devices: none -> 67.2 us  [the longest x67 60.8 us: shift(): lax.ppermute(value, axis, [(i, (i + step) % size) for i in range(size)])]
    unnamed x148 -> x282, local copies, waits for them, and re-layouts: 17.3 us -> 72.9 us
  transfers between devices with their start and end apart: 32 -> 84, of which waited for: 32 -> 40; matrix products, arithmetic and copies ran while one was open for 14% -> 9% of each run, Pallas kernels for 0% -> 32%
where the time goes in v1:
time: 795 us; the launch traced here: 789 us
  waiting for transfers between devices  290 us (36%)
  Pallas kernels  274 us (34%)
  local copies, waits for them, and re-layouts  104 us (13%)
  starting transfers between devices  67.8 us (9%)
  other arithmetic  37.1 us (5%)
  between operations  16.5 us (2%)
    pallas_call x42, Pallas kernels, kernel_call(): pl.pallas_call(body, grid_spec=pltpu.PrefetchScalarGridSpec(num_scalar_pr...  274 us
    ppermute x67, waiting for transfers between devices, shift(): lax.ppermute(value, axis, [(i, (i + step) % size) for i in range(size)])  255 us
    unnamed x282, local copies, waits for them, and re-layouts  72.9 us
    ppermute x67, starting transfers between devices, shift(): lax.ppermute(value, axis, [(i, (i + step) % size) for i in range(size)])  60.8 us
    ppermute x9, waiting for transfers between devices, sum_over(): lax.ppermute(value, axis, [(i, i ^ step) for i in range(size)])  19.2 us
  transfers between devices with their start and end apart: 84, of which 40 were waited for; matrix products, arithmetic and copies ran while one was open for 9% of the time, Pallas kernels for 32%

profile of v1, /device:TPU:0, one launch (start us, length us, event | category | flops | bytes accessed | tf_op | source)
XLA Modules:
  0.0 788.9 jit_solution(13842719152103543008)
XLA Ops:
  30.7 14.1 %collective-permute-done.2.rest_2_.rest_6_ = bf16[512,768]{1,0:T(8,128)(2,1)S(1)} collective-permute-done((bf16[512,768]{1,0:T(8,128)(2,1)S(1)}, bf16[512,768]{1,0:T(8,128)(2,1)S(1)}, u32[]{:S(2)}, u32[]{:S(2)}) %collective-permute-start.2) | collective-permute-done | bytes 786464 | tf_op jit(solution)/shard_map/ppermute | solution.py:32
  80.2 10.0 %project_qkv.2 = (bf16[1024,256]{1,0:T(8,128)(2,1)S(1)}, bf16[1024,512]{1,0:T(8,128)(2,1)}) custom-call(s32[25]{0:T(128)S(1)} %concatenate.77.table_ref, bf16[8,512,512]{2,1,0:T(8,128)(2,1)S(1)} %fusion.3.g_ref, bf16[512,768]{1,0:T(8,128)(2,1)S(1)} %copy-done.57, bf16[512,768]{1,0:T(8,128)(2,1)} %collective-permute-done.1.rest_1_.rest_4_, ...), custom_call_target="tpu_custom_call" | custom-call | flops 1 | bytes 1 | tf_op jit(solution)/shard_map/project_qkv/pallas_call | solution.py:137
  92.3 11.3 %attend_own.2 = (bf16[1024,256]{1,0:T(8,128)(2,1)}, f32[1024,256]{1,0:T(8,128)S(1)}, f32[4,1024]{1,0:T(4,128)S(1)}) custom-call(s32[2]{0:T(128)S(1)} %get-tuple-element.1330.begin_ref, bf16[1024,256]{1,0:T(8,128)(2,1)S(1)} %get-tuple-element.1331.q_ref, bf16[1024,512]{1,0:T(8,128)(2,1)} %get-tuple-element.1332.kv_ref, s32[1,1024]{1,0:T(1,128)S(1)} %bitcast.103), custom_call_target="tpu_custom_call" | custom-call | flops 1 | bytes 1 | tf_op jit(solution)/shard_map/attend_own/pallas_call | solution.py:137
  103.6 19.5 %collective-permute-done.13.kv_ref = bf16[1024,512]{1,0:T(8,128)(2,1)S(1)} collective-permute-done((bf16[1024,512]{1,0:T(8,128)(2,1)}, bf16[1024,512]{1,0:T(8,128)(2,1)S(1)}, u32[]{:S(2)}, u32[]{:S(2)}) %collective-permute-start.13) | collective-permute-done | bytes 1048608 | tf_op jit(solution)/shard_map/ppermute | solution.py:32
  125.4 8.8 %attend_far.2 = (bf16[1024,256]{1,0:T(8,128)(2,1)S(1)}, f32[1024,256]{1,0:T(8,128)S(1)}, f32[4,1024]{1,0:T(4,128)S(1)}) custom-call(s32[2]{0:T(128)S(1)} %get-tuple-element.1319.begin_ref, bf16[1024,256]{1,0:T(8,128)(2,1)S(1)} %get-tuple-element.1331.q_ref, bf16[1024,512]{1,0:T(8,128)(2,1)S(1)} %copy-done.67, s32[1,1024]{1,0:T(1,128)S(1)} %bitcast.104, ...), custom_call_target="tpu_custom_call" | custom-call | flops 1 | bytes 1 | tf_op jit(solution)/shard_map/attend_far/pallas_call | solution.py:137
  154.2 16.1 %collective-permute-done.14.rest_3_.rest_9_ = bf16[512,1024]{1,0:T(8,128)(2,1)} collective-permute-done((bf16[512,1024]{1,0:T(8,128)(2,1)}, bf16[512,1024]{1,0:T(8,128)(2,1)}, u32[]{:S(2)}, u32[]{:S(2)}) %collective-permute-start.14) | collective-permute-done | bytes 1048608 | tf_op jit(solution)/shard_map/ppermute | solution.py:32
  173.5 9.7 %project_up.2 = (bf16[1024,1024]{1,0:T(8,128)(2,1)S(1)}, bf16[1024,1024]{1,0:T(8,128)(2,1)S(1)}) custom-call(s32[25]{0:T(128)S(1)} %concatenate.77.table_ref, bf16[8,512,512]{2,1,0:T(8,128)(2,1)S(1)} %copy-done.1, bf16[512,1024]{1,0:T(8,128)(2,1)} %pad_maximum_fusion.4.rest_0_.rest_3_, bf16[512,1024]{1,0:T(8,128)(2,1)} %collective-permute-done.5.rest_1_.rest_5_, ...), custom_call_target="tpu_custom_call" | custom-call | flops 1 | bytes 1 | tf_op jit(solution)/shard_map/project_up/pallas_call | solution.py:137
  184.6 7.9 project_out.2
  203.3 38.3 %collective-permute-done.22.rest_2_.rest_4_ = bf16[512,1792]{1,0:T(8,128)(2,1)S(1)} collective-permute-done((bf16[512,1792]{1,0:T(8,128)(2,1)S(1)}, bf16[512,1792]{1,0:T(8,128)(2,1)S(1)}, u32[]{:S(2)}, u32[]{:S(2)}) %collective-permute-start.22) | collective-permute-done | bytes 1835040 | tf_op jit(solution)/shard_map/ppermute | solution.py:32
  261.2 36.0 %collective-permute-done.25.rest_3_.rest_5_ = bf16[512,1792]{1,0:T(8,128)(2,1)S(1)} collective-permute-done((bf16[512,1792]{1,0:T(8,128)(2,1)}, bf16[512,1792]{1,0:T(8,128)(2,1)S(1)}, u32[]{:S(2)}, u32[]{:S(2)}) %collective-permute-start.25) | collective-permute-done | bytes 1835040 | tf_op jit(solution)/shard_map/ppermute | solution.py:32
  309.3 10.3 %project_qkv.3 = (bf16[1024,256]{1,0:T(8,128)(2,1)S(1)}, bf16[1024,512]{1,0:T(8,128)(2,1)}) custom-call(s32[25]{0:T(128)S(1)} %concatenate.77.table_ref, bf16[8,512,512]{2,1,0:T(8,128)(2,1)} %bitcast.91, bf16[512,1792]{1,0:T(8,128)(2,1)S(1)} %pad_maximum_fusion.1.rest_0_.rest_2_, bf16[512,1792]{1,0:T(8,128)(2,1)} %collective-permute-done.21.rest_1_.rest_3_, ...), custom_call_target="tpu_custom_call" | custom-call | flops 1 | bytes 1 | tf_op jit(solution)/shard_map/project_qkv/pallas_call | solution.py:137
  322.6 11.3 %branch_grads.2 = (bf16[1024,256]{1,0:T(8,128)(2,1)S(1)}, bf16[1024,1024]{1,0:T(8,128)(2,1)S(1)}) custom-call(s32[25]{0:T(128)S(1)} %concatenate.77.table_ref, bf16[8,512,512]{2,1,0:T(8,128)(2,1)S(1)} %bitcast.97, bf16[1280,512]{1,0:T(8,128)(2,1)S(1)} %copy-done.48, bf16[1280,512]{1,0:T(8,128)(2,1)} %collective-permute-done.26.rest_1_.rest_3_, ...), custom_call_target="tpu_custom_call" | custom-call | flops 1 | bytes 1 | tf_op jit(solution)/shard_map/branch_grads/pallas_call | solution.py:137
  336.9 10.2 %project_up.3 = (bf16[1024,1024]{1,0:T(8,128)(2,1)S(1)}, bf16[1024,1024]{1,0:T(8,128)(2,1)S(1)}) custom-call(s32[25]{0:T(128)S(1)} %concatenate.77.table_ref, bf16[8,512,512]{2,1,0:T(8,128)(2,1)} %bitcast.92, bf16[512,1792]{1,0:T(8,128)(2,1)S(1)} %copy-done.20, bf16[512,1792]{1,0:T(8,128)(2,1)} %collective-permute-done.21.rest_1_.rest_3_, ...), custom_call_target="tpu_custom_call" | custom-call | flops 1 | bytes 1 | tf_op jit(solution)/shard_map/project_up/pallas_call | solution.py:137
  353.2 10.9 %attend_own.3 = (bf16[1024,256]{1,0:T(8,128)(2,1)}, f32[1024,256]{1,0:T(8,128)S(1)}, f32[4,1024]{1,0:T(4,128)S(1)}) custom-call(s32[2]{0:T(128)S(1)} %get-tuple-element.1330.begin_ref, bf16[1024,256]{1,0:T(8,128)(2,1)S(1)} %get-tuple-element.1102.q_ref, bf16[1024,512]{1,0:T(8,128)(2,1)} %get-tuple-element.1103.kv_ref, s32[1,1024]{1,0:T(1,128)S(1)} %bitcast.105), custom_call_target="tpu_custom_call" | custom-call | flops 1 | bytes 1 | tf_op jit(solution)/shard_map/attend_own/pallas_call | solution.py:137
  364.1 9.8 %attend_far.3 = (bf16[1024,256]{1,0:T(8,128)(2,1)S(1)}, f32[1024,256]{1,0:T(8,128)S(1)}, f32[4,1024]{1,0:T(4,128)S(1)}) custom-call(s32[2]{0:T(128)S(1)} %get-tuple-element.1319.begin_ref, bf16[1024,256]{1,0:T(8,128)(2,1)S(1)} %get-tuple-element.1102.q_ref, bf16[1024,512]{1,0:T(8,128)(2,1)} %collective-permute-done.28.kv_ref, s32[1,1024]{1,0:T(1,128)S(1)} %bitcast.106, ...), custom_call_target="tpu_custom_call" | custom-call | flops 1 | bytes 1 | tf_op jit(solution)/shard_map/attend_far/pallas_call | solution.py:137
  374.0 14.1 %attend_backward.4 = (f32[1024,256]{1,0:T(8,128)S(1)}, bf16[1024,512]{1,0:T(8,128)(2,1)S(1)}) custom-call(s32[2]{0:T(128)S(1)} %get-tuple-element.1319.begin_ref, bf16[1024,256]{1,0:T(8,128)(2,1)S(1)} %get-tuple-element.1102.q_ref, bf16[1024,512]{1,0:T(8,128)(2,1)} %collective-permute-done.28.kv_ref, s32[1,1024]{1,0:T(1,128)S(1)} %bitcast.107, ...), custom_call_target="tpu_custom_call" | custom-call | flops 1 | bytes 1 | tf_op jit(solution)/shard_map/attend_backward/pallas_call | solution.py:137
  388.7 10.1 %attend_backward.5 = (f32[1024,256]{1,0:T(8,128)S(1)}, f32[1024,512]{1,0:T(8,128)S(1)}) custom-call(s32[2]{0:T(128)S(1)} %get-tuple-element.1330.begin_ref, bf16[1024,256]{1,0:T(8,128)(2,1)S(1)} %get-tuple-element.1102.q_ref, bf16[1024,512]{1,0:T(8,128)(2,1)} %get-tuple-element.1103.kv_ref, s32[1,1024]{1,0:T(1,128)S(1)} %bitcast.108, ...), custom_call_target="tpu_custom_call" | custom-call | flops 1 | bytes 1 | tf_op jit(solution)/shard_map/attend_backward/pallas_call | solution.py:137
  417.3 10.8 %feature_grads.2 = (bf16[256,2048]{1,0:T(8,128)(2,1)S(1)}, bf16[256,2048]{1,0:T(8,128)(2,1)S(1)}, bf16[512,2048]{1,0:T(8,128)(2,1)S(1)}) custom-call(s32[25]{0:T(128)S(1)} %concatenate.77.table_ref, bf16[1024,768]{1,0:T(8,128)(2,1)S(1)} %get-tuple-element.1194.right_ref.rest_0_, bf16[1024,1024]{1,0:T(8,128)(2,1)} %copy-done.15, ...), custom_call_target="tpu_custom_call" | custom-call | flops 1 | bytes 1 | tf_op jit(solution)/shard_map/feature_grads/pallas_call | solution.py:137
  445.1 7.9 project_out.3
  453.5 20.6 %collective-permute-done.38.rest_2_ = bf16[1280,512]{1,0:T(8,128)(2,1)S(1)} collective-permute-done((bf16[1280,512]{1,0:T(8,128)(2,1)S(1)}, bf16[1280,512]{1,0:T(8,128)(2,1)S(1)}, u32[]{:S(2)}, u32[]{:S(2)}) %collective-permute-start.38) | collective-permute-done | bytes 1310752 | tf_op jit(solution)/shard_map/ppermute | solution.py:32
  507.4 10.2 %collective-permute-done.43.refs_1_ = bf16[256,1024]{1,0:T(8,128)(2,1)S(1)} collective-permute-done((bf16[256,1024]{1,0:T(8,128)(2,1)}, bf16[256,1024]{1,0:T(8,128)(2,1)S(1)}, u32[]{:S(2)}, u32[]{:S(2)}) %collective-permute-start.43) | collective-permute-done | bytes 524320 | tf_op jit(solution)/shard_map/ppermute | solution.py:32
  532.1 9.6 %collective-permute-done.44.refs_3_ = bf16[256,1024]{1,0:T(8,128)(2,1)S(1)} collective-permute-done((bf16[256,1024]{1,0:T(8,128)(2,1)S(1)}, bf16[256,1024]{1,0:T(8,128)(2,1)S(1)}, u32[]{:S(2)}, u32[]{:S(2)}) %collective-permute-start.44) | collective-permute-done | bytes 524320 | tf_op jit(solution)/shard_map/ppermute | solution.py:32
  550.2 8.0 %collective-permute-done.50.refs_1_ = bf16[256,768]{1,0:T(8,128)(2,1)S(1)} collective-permute-done((bf16[256,768]{1,0:T(8,128)(2,1)S(1)}, bf16[256,768]{1,0:T(8,128)(2,1)S(1)}, u32[]{:S(2)}, u32[]{:S(2)}) %collective-permute-start.50) | collective-permute-done | bytes 393248 | tf_op jit(solution)/shard_map/ppermute | solution.py:32
  567.5 11.3 %branch_grads.3 = (bf16[1024,256]{1,0:T(8,128)(2,1)S(1)}, bf16[1024,1024]{1,0:T(8,128)(2,1)S(1)}) custom-call(s32[25]{0:T(128)S(1)} %concatenate.77.table_ref, bf16[8,512,512]{2,1,0:T(8,128)(2,1)S(1)} %bitcast.100, bf16[1280,512]{1,0:T(8,128)(2,1)S(1)} %copy-done.52, bf16[1280,512]{1,0:T(8,128)(2,1)} %collective-permute-done.12.rest_3_.rest_1_, ...), custom_call_target="tpu_custom_call" | custom-call | flops 1 | bytes 1 | tf_op jit(solution)/shard_map/branch_grads/pallas_call | solution.py:137
  589.8 12.6 %attend_backward.6 = (f32[1024,256]{1,0:T(8,128)S(1)}, bf16[1024,512]{1,0:T(8,128)(2,1)S(1)}) custom-call(s32[2]{0:T(128)S(1)} %get-tuple-element.1319.begin_ref, bf16[1024,256]{1,0:T(8,128)(2,1)S(1)} %get-tuple-element.1331.q_ref, bf16[1024,512]{1,0:T(8,128)(2,1)S(1)} %copy-done.68, s32[1,1024]{1,0:T(1,128)S(1)} %bitcast.109, f32[1024,256]{1,0:T(8,128)S(1)} %copy-done.65, ...), custom_call_target="tpu_custom_call" | custom-call | flops 1 | bytes 1 | tf_op jit(solution)/shard_map/attend_backward/pallas_call | solution.py:137
  604.5 10.3 %attend_backward.7 = (f32[1024,256]{1,0:T(8,128)S(1)}, f32[1024,512]{1,0:T(8,128)S(1)}) custom-call(s32[2]{0:T(128)S(1)} %get-tuple-element.1330.begin_ref, bf16[1024,256]{1,0:T(8,128)(2,1)S(1)} %get-tuple-element.1331.q_ref, bf16[1024,512]{1,0:T(8,128)(2,1)} %get-tuple-element.1332.kv_ref, s32[1,1024]{1,0:T(1,128)S(1)} %bitcast.110, ...), custom_call_target="tpu_custom_call" | custom-call | flops 1 | bytes 1 | tf_op jit(solution)/shard_map/attend_backward/pallas_call | solution.py:137
  614.8 21.8 %collective-permute-done.53.rest_0_ = bf16[1024,512]{1,0:T(8,128)(2,1)S(1)} collective-permute-done((bf16[1024,512]{1,0:T(8,128)(2,1)S(1)}, bf16[1024,512]{1,0:T(8,128)(2,1)S(1)}, u32[]{:S(2)}, u32[]{:S(2)}) %collective-permute-start.53) | collective-permute-done | bytes 1048608 | tf_op jit(solution)/shard_map/ppermute | solution.py:32
  645.6 11.2 %feature_grads.3 = (bf16[256,2048]{1,0:T(8,128)(2,1)S(1)}, bf16[256,2048]{1,0:T(8,128)(2,1)S(1)}, bf16[512,2048]{1,0:T(8,128)(2,1)S(1)}) custom-call(s32[25]{0:T(128)S(1)} %concatenate.77.table_ref, bf16[1024,768]{1,0:T(8,128)(2,1)S(1)} %get-tuple-element.1430.right_ref.rest_0_, bf16[1024,1024]{1,0:T(8,128)(2,1)} %copy-done.17, ...), custom_call_target="tpu_custom_call" | custom-call | flops 1 | bytes 1 | tf_op jit(solution)/shard_map/feature_grads/pallas_call | solution.py:137
  663.5 10.2 %collective-permute-done.56.rest_2_ = bf16[1280,512]{1,0:T(8,128)(2,1)} collective-permute-done((bf16[1280,512]{1,0:T(8,128)(2,1)}, bf16[1280,512]{1,0:T(8,128)(2,1)}, u32[]{:S(2)}, u32[]{:S(2)}) %collective-permute-start.56) | collective-permute-done | bytes 1310752 | tf_op jit(solution)/shard_map/ppermute | solution.py:32
  673.7 10.0 %collective-permute-done.55.rest_0_ = bf16[1024,768]{1,0:T(8,128)(2,1)} collective-permute-done((bf16[1024,768]{1,0:T(8,128)(2,1)}, bf16[1024,768]{1,0:T(8,128)(2,1)}, u32[]{:S(2)}, u32[]{:S(2)}) %collective-permute-start.55) | collective-permute-done | bytes 1572896 | tf_op jit(solution)/shard_map/ppermute | solution.py:32
  701.3 6.5 grad_out.7
  748.3 7.9 %collective-permute-done.75.refs_3_ = bf16[1280,256]{1,0:T(8,128)(2,1)S(1)} collective-permute-done((bf16[1280,256]{1,0:T(8,128)(2,1)}, bf16[1280,256]{1,0:T(8,128)(2,1)S(1)}, u32[]{:S(2)}, u32[]{:S(2)}) %collective-permute-start.75) | collective-permute-done | bytes 655392 | tf_op jit(solution)/shard_map/ppermute | solution.py:32
  (580 shorter events, 355.1 us)
Async XLA Ops:
  7.2 65.9 %all-gather.11.cloned.1.call-start = ((), (), s32[]{:S(2)}) async-start(), calls=%async_computation.9 | async-start | bytes 4718592 | tf_op jit(solution)/shard_map/all_gather | solution.py:1249
  7.9 146.3 %all-gather.9.cloned.1.call-start = ((), (), s32[]{:S(2)}) async-start(), calls=%async_computation.8 | async-start | bytes 4718592 | tf_op jit(solution)/shard_map/all_gather | solution.py:1249
  18.6 226.8 %reduce-scatter.5.cloned.1.call-start = ((), (), s32[]{:S(2)}) async-start(), calls=%async_computation.4 | async-start | bytes 2621440 | tf_op jit(solution)/shard_map/reduce_scatter | solution.py:1252
  71.0 53.2 %collective-permute-start.11 = (bf16[1280,512]{1,0:T(8,128)(2,1)S(1)}, bf16[1280,512]{1,0:T(8,128)(2,1)}, u32[]{:S(2)}, u32[]{:S(2)}) collective-permute-start(bf16[1280,512]{1,0:T(8,128)(2,1)S(1)} %pad_maximum_fusion.2.rest_2_.rest_0_), channel_id=1, source_target_pairs={{0,16},{16,0},{1,17},{17,1},{2,18},{18,2},{3,19},{19,3},{4,20},{20... | collective-permute-start | bytes 3932168 | tf_op jit(solution)/shard_map/ppermute | solution.py:32
  72.2 52.0 %collective-permute-start.12 = (bf16[1280,512]{1,0:T(8,128)(2,1)S(1)}, bf16[1280,512]{1,0:T(8,128)(2,1)}, u32[]{:S(2)}, u32[]{:S(2)}) collective-permute-start(bf16[1280,512]{1,0:T(8,128)(2,1)S(1)} %pad_maximum_fusion.2.rest_2_.rest_0_), channel_id=1, source_target_pairs={{0,8},{8,0},{1,9},{9,1},{2,10},{10,2},{3,11},{11,3},{4,12},{12,4},... | collective-permute-start | bytes 3932168 | tf_op jit(solution)/shard_map/ppermute | solution.py:32
  90.2 32.9 %collective-permute-start.13 = (bf16[1024,512]{1,0:T(8,128)(2,1)}, bf16[1024,512]{1,0:T(8,128)(2,1)S(1)}, u32[]{:S(2)}, u32[]{:S(2)}) collective-permute-start(bf16[1024,512]{1,0:T(8,128)(2,1)} %get-tuple-element.1332.kv_ref), channel_id=1, source_target_pairs={{0,8},{8,0},{1,9},{9,1},{2,10},{10,2},{3,11},{11,3},{4,12},{12,4},... | collective-permute-start | bytes 3145736 | tf_op jit(solution)/shard_map/ppermute | solution.py:32
  91.5 32.7 %collective-permute-start.10 = (bf16[512,1024]{1,0:T(8,128)(2,1)}, bf16[512,1024]{1,0:T(8,128)(2,1)}, u32[]{:S(2)}, u32[]{:S(2)}) collective-permute-start(bf16[512,1024]{1,0:T(8,128)(2,1)} %pad_maximum_fusion.4.rest_0_.rest_3_), channel_id=1, source_target_pairs={{0,16},{16,0},{1,17},{17,1},{2,18},{18,2},{3,19},{19,3},{4,20},{20... | collective-permute-start | bytes 3145736 | tf_op jit(solution)/shard_map/ppermute | solution.py:32
  145.9 38.6 %collective-permute-start.18 = (bf16[1280,512]{1,0:T(8,128)(2,1)}, bf16[1280,512]{1,0:T(8,128)(2,1)}, u32[]{:S(2)}, u32[]{:S(2)}) collective-permute-start(bf16[1280,512]{1,0:T(8,128)(2,1)} %collective-permute-done.11.rest_4_.rest_2_), channel_id=1, source_target_pairs={{0,8},{8,0},{1,9},{9,1},{2,10},{10,2},{3,11},{11,3},{4,12},{12,4},... | collective-permute-start | bytes 3932168 | tf_op jit(solution)/shard_map/ppermute | solution.py:32
  170.3 30.1 %collective-permute-start.17 = (bf16[1280,512]{1,0:T(8,128)(2,1)}, bf16[1280,512]{1,0:T(8,128)(2,1)}, u32[]{:S(2)}, u32[]{:S(2)}) collective-permute-start(bf16[1280,512]{1,0:T(8,128)(2,1)} %pad_maximum_fusion.3.rest_0_.rest_2_), channel_id=1, source_target_pairs={{0,16},{16,0},{1,17},{17,1},{2,18},{18,2},{3,19},{19,3},{4,20},{20... | collective-permute-start | bytes 3932168 | tf_op jit(solution)/shard_map/ppermute | solution.py:32
  200.5 103.8 %all-gather.13.cloned.1.call-start = ((), (), s32[]{:S(2)}) async-start(), calls=%async_computation.10 | async-start | bytes 4718592 | tf_op jit(solution)/shard_map/all_gather | solution.py:1249
  200.7 40.9 %collective-permute-start.22 = (bf16[512,1792]{1,0:T(8,128)(2,1)S(1)}, bf16[512,1792]{1,0:T(8,128)(2,1)S(1)}, u32[]{:S(2)}, u32[]{:S(2)}) collective-permute-start(bf16[512,1792]{1,0:T(8,128)(2,1)S(1)} %pad_maximum_fusion.1.rest_0_.rest_2_), channel_id=1, source_target_pairs={{0,16},{16,0},{1,17},{17,1},{2,18},{18,2},{3,19},{19,3},{4,20},{20... | collective-permute-start | bytes 5505032 | tf_op jit(solution)/shard_map/ppermute | solution.py:32
  201.8 41.0 %collective-permute-start.21 = (bf16[512,1792]{1,0:T(8,128)(2,1)S(1)}, bf16[512,1792]{1,0:T(8,128)(2,1)}, u32[]{:S(2)}, u32[]{:S(2)}) collective-permute-start(bf16[512,1792]{1,0:T(8,128)(2,1)S(1)} %pad_maximum_fusion.1.rest_0_.rest_2_), channel_id=1, source_target_pairs={{0,8},{8,0},{1,9},{9,1},{2,10},{10,2},{3,11},{11,3},{4,12},{12,4},... | collective-permute-start | bytes 5505032 | tf_op jit(solution)/shard_map/ppermute | solution.py:32
  257.6 233.2 %reduce-scatter.7.cloned.1.call-start = ((), (), s32[]{:S(2)}) async-start(), calls=%async_computation.5 | async-start | bytes 2621440 | tf_op jit(solution)/shard_map/reduce_scatter | solution.py:1252
  257.7 39.6 %collective-permute-start.25 = (bf16[512,1792]{1,0:T(8,128)(2,1)}, bf16[512,1792]{1,0:T(8,128)(2,1)S(1)}, u32[]{:S(2)}, u32[]{:S(2)}) collective-permute-start(bf16[512,1792]{1,0:T(8,128)(2,1)} %collective-permute-done.21.rest_1_.rest_3_), channel_id=1, source_target_pairs={{0,16},{16,0},{1,17},{17,1},{2,18},{18,2},{3,19},{19,3},{4,20},{20... | collective-permute-start | bytes 5505032 | tf_op jit(solution)/shard_map/ppermute | solution.py:32
  259.2 60.5 %collective-permute-start.26 = (bf16[1280,512]{1,0:T(8,128)(2,1)}, bf16[1280,512]{1,0:T(8,128)(2,1)}, u32[]{:S(2)}, u32[]{:S(2)}) collective-permute-start(bf16[1280,512]{1,0:T(8,128)(2,1)} %pad_maximum_fusion.3.rest_0_.rest_2_), channel_id=1, source_target_pairs={{0,8},{8,0},{1,9},{9,1},{2,10},{10,2},{3,11},{11,3},{4,12},{12,4},... | collective-permute-start | bytes 3932168 | tf_op jit(solution)/shard_map/ppermute | solution.py:32
  260.7 60.5 %collective-permute-start.27 = (bf16[1280,512]{1,0:T(8,128)(2,1)}, bf16[1280,512]{1,0:T(8,128)(2,1)}, u32[]{:S(2)}, u32[]{:S(2)}) collective-permute-start(bf16[1280,512]{1,0:T(8,128)(2,1)} %collective-permute-done.17.rest_2_.rest_4_), channel_id=1, source_target_pairs={{0,8},{8,0},{1,9},{9,1},{2,10},{10,2},{3,11},{11,3},{4,12},{12,4},... | collective-permute-start | bytes 3932168 | tf_op jit(solution)/shard_map/ppermute | solution.py:32
  351.6 54.4 %collective-permute-start.29 = (bf16[1024,1024]{1,0:T(8,128)(2,1)}, bf16[1024,1024]{1,0:T(8,128)(2,1)}, u32[]{:S(2)}, u32[]{:S(2)}) collective-permute-start(bf16[1024,1024]{1,0:T(8,128)(2,1)} %grad_in.8), channel_id=1, source_target_pairs={{0,16},{16,0},{1,17},{17,1},{2,18},{18,2},{3,19},{19,3},{4,20},{20... | collective-permute-start | bytes 6291464 | tf_op jit(solution)/shard_map/ppermute | solution.py:32
  435.3 128.5 %all-gather.15.cloned.1.call-start = ((), (), s32[]{:S(2)}) async-start(), calls=%async_computation.11 | async-start | bytes 4718592 | tf_op jit(solution)/shard_map/all_gather | solution.py:1249
  443.0 36.8 %collective-permute-start.31 = (bf16[1024,768]{1,0:T(8,128)(2,1)}, bf16[1024,768]{1,0:T(8,128)(2,1)}, u32[]{:S(2)}, u32[]{:S(2)}) collective-permute-start(bf16[1024,768]{1,0:T(8,128)(2,1)} %grad_in.10), channel_id=1, source_target_pairs={{0,16},{16,0},{1,17},{17,1},{2,18},{18,2},{3,19},{19,3},{4,20},{20... | collective-permute-start | bytes 4718600 | tf_op jit(solution)/shard_map/ppermute | solution.py:32
  443.6 30.5 %collective-permute-start.38 = (bf16[1280,512]{1,0:T(8,128)(2,1)S(1)}, bf16[1280,512]{1,0:T(8,128)(2,1)S(1)}, u32[]{:S(2)}, u32[]{:S(2)}) collective-permute-start(bf16[1280,512]{1,0:T(8,128)(2,1)S(1)} %copy-done.95), channel_id=1, source_target_pairs={{0,8},{8,0},{1,9},{9,1},{2,10},{10,2},{3,11},{11,3},{4,12},{12,4},... | collective-permute-start | bytes 3932168 | tf_op jit(solution)/shard_map/ppermute | solution.py:32
  475.2 30.1 %collective-permute-start.39 = (bf16[1280,512]{1,0:T(8,128)(2,1)}, bf16[1280,512]{1,0:T(8,128)(2,1)}, u32[]{:S(2)}, u32[]{:S(2)}) collective-permute-start(bf16[1280,512]{1,0:T(8,128)(2,1)} %get-tuple-element.1191), channel_id=1, source_target_pairs={{0,8},{8,0},{1,9},{9,1},{2,10},{10,2},{3,11},{11,3},{4,12},{12,4},... | collective-permute-start | bytes 3932168 | tf_op jit(solution)/shard_map/ppermute | solution.py:32
  505.3 221.9 %reduce-scatter.11.cloned.1.call-start = ((), (), s32[]{:S(2)}) async-start(), calls=%async_computation.7 | async-start | bytes 2621440 | tf_op jit(solution)/shard_map/reduce_scatter | solution.py:1252
  528.5 33.0 %collective-permute-start.48 = (bf16[1280,256]{1,0:T(8,128)(2,1)S(1)}, bf16[1280,256]{1,0:T(8,128)(2,1)S(1)}, u32[]{:S(2)}, u32[]{:S(2)}) collective-permute-start(bf16[1280,256]{1,0:T(8,128)(2,1)S(1)} %get-tuple-element.1264), channel_id=1, source_target_pairs={{0,4},{4,0},{1,5},{5,1},{2,6},{6,2},{3,7},{7,3},{8,12},{12,8},{9,1... | collective-permute-start | bytes 1966088 | tf_op jit(solution)/shard_map/ppermute | solution.py:32
  528.6 32.9 %collective-permute-start.47 = (bf16[1280,256]{1,0:T(8,128)(2,1)S(1)}, bf16[1280,256]{1,0:T(8,128)(2,1)S(1)}, u32[]{:S(2)}, u32[]{:S(2)}) collective-permute-start(bf16[1280,256]{1,0:T(8,128)(2,1)S(1)} %bitcast.114), channel_id=1, source_target_pairs={{0,16},{16,0},{1,17},{17,1},{2,18},{18,2},{3,19},{19,3},{4,20},{20... | collective-permute-start | bytes 1966088 | tf_op jit(solution)/shard_map/ppermute | solution.py:32
  530.1 31.4 %collective-permute-start.49 = (bf16[1280,256]{1,0:T(8,128)(2,1)S(1)}, bf16[1280,256]{1,0:T(8,128)(2,1)S(1)}, u32[]{:S(2)}, u32[]{:S(2)}) collective-permute-start(bf16[1280,256]{1,0:T(8,128)(2,1)S(1)} %bitcast.183), channel_id=1, source_target_pairs={{0,16},{16,0},{1,17},{17,1},{2,18},{18,2},{3,19},{19,3},{4,20},{20... | collective-permute-start | bytes 1966088 | tf_op jit(solution)/shard_map/ppermute | solution.py:32
  583.7 55.0 %collective-permute-start.54 = (bf16[1280,512]{1,0:T(8,128)(2,1)S(1)}, bf16[1280,512]{1,0:T(8,128)(2,1)S(1)}, u32[]{:S(2)}, u32[]{:S(2)}) collective-permute-start(bf16[1280,512]{1,0:T(8,128)(2,1)S(1)} %get-tuple-element.1311), channel_id=1, source_target_pairs={{0,8},{8,0},{1,9},{9,1},{2,10},{10,2},{3,11},{11,3},{4,12},{12,4},... | collective-permute-start | bytes 3932168 | tf_op jit(solution)/shard_map/ppermute | solution.py:32
  602.5 34.1 %collective-permute-start.53 = (bf16[1024,512]{1,0:T(8,128)(2,1)S(1)}, bf16[1024,512]{1,0:T(8,128)(2,1)S(1)}, u32[]{:S(2)}, u32[]{:S(2)}) collective-permute-start(bf16[1024,512]{1,0:T(8,128)(2,1)S(1)} %get-tuple-element.1328), channel_id=1, source_target_pairs={{0,8},{8,0},{1,9},{9,1},{2,10},{10,2},{3,11},{11,3},{4,12},{12,4},... | collective-permute-start | bytes 3145736 | tf_op jit(solution)/shard_map/ppermute | solution.py:32
  603.1 60.4 %collective-permute-start.52 = (bf16[1024,1024]{1,0:T(8,128)(2,1)}, bf16[1024,1024]{1,0:T(8,128)(2,1)}, u32[]{:S(2)}, u32[]{:S(2)}) collective-permute-start(bf16[1024,1024]{1,0:T(8,128)(2,1)} %grad_in.12), channel_id=1, source_target_pairs={{0,16},{16,0},{1,17},{17,1},{2,18},{18,2},{3,19},{19,3},{4,20},{20... | collective-permute-start | bytes 6291464 | tf_op jit(solution)/shard_map/ppermute | solution.py:32
  642.6 41.1 %collective-permute-start.55 = (bf16[1024,768]{1,0:T(8,128)(2,1)}, bf16[1024,768]{1,0:T(8,128)(2,1)}, u32[]{:S(2)}, u32[]{:S(2)}) collective-permute-start(bf16[1024,768]{1,0:T(8,128)(2,1)} %grad_in.13), channel_id=1, source_target_pairs={{0,16},{16,0},{1,17},{17,1},{2,18},{18,2},{3,19},{19,3},{4,20},{20... | collective-permute-start | bytes 4718600 | tf_op jit(solution)/shard_map/ppermute | solution.py:32
  683.7 88.5 %reduce-scatter.9.cloned.1.call-start = ((), (), s32[]{:S(2)}) async-start(), calls=%async_computation.6 | async-start | bytes 2621440 | tf_op jit(solution)/shard_map/reduce_scatter | solution.py:1252
  726.7 33.1 %collective-permute-start.72 = (bf16[256,768]{1,0:T(8,128)(2,1)}, bf16[256,768]{1,0:T(8,128)(2,1)S(1)}, u32[]{:S(2)}, u32[]{:S(2)}) collective-permute-start(bf16[256,768]{1,0:T(8,128)(2,1)} %copy-done.100), channel_id=1, source_target_pairs={{0,4},{4,0},{1,5},{5,1},{2,6},{6,2},{3,7},{7,3},{8,12},{12,8},{9,1... | collective-permute-start | bytes 1179656 | tf_op jit(solution)/shard_map/ppermute | solution.py:32
  726.7 33.1 %collective-permute-start.71 = (bf16[256,768]{1,0:T(8,128)(2,1)}, bf16[256,768]{1,0:T(8,128)(2,1)S(1)}, u32[]{:S(2)}, u32[]{:S(2)}) collective-permute-start(bf16[256,768]{1,0:T(8,128)(2,1)} %copy-done.101), channel_id=1, source_target_pairs={{0,8},{8,0},{1,9},{9,1},{2,10},{10,2},{3,11},{11,3},{4,12},{12,4},... | collective-permute-start | bytes 1179656 | tf_op jit(solution)/shard_map/ppermute | solution.py:32
  (185 other events, 1826.2 us)
Sparse Core Ops, SparseCore 0:
  9.6 49.8 all-gather.10
  61.1 45.8 all-gather.8
  200.6 44.7 reduce-scatter.4
  257.8 46.4 all-gather.12
  435.4 41.6 reduce-scatter.6
  505.4 45.8 all-gather.14
  683.9 42.5 reduce-scatter.10
  728.8 43.3 reduce-scatter.8

commit v2 on v1

--- a/solution.py
+++ b/solution.py
@@ -1,4 +1,5 @@
 import math
+from types import SimpleNamespace
 
 import jax
 import jax.numpy as jnp
@@ -14,10 +15,16 @@
 NEGATIVE = -1e30
 LANES = 128
 HEADS_TILE = LANES // HEAD_DIM
-VMEM_BYTES = 40 * 1024 * 1024
+MEBI = 1024 * 1024
+PIECES = 4
+VMEM_MEBI = 40
+MORE_MEBI = 40
 F32 = jnp.float32
 BF16 = jnp.bfloat16
 ANY = pl.BlockSpec(memory_space=pl.ANY)
+HBM = pl.BlockSpec(memory_space=pltpu.HBM)
+Y, X, C, Z = "dp", "x", "core", "col"
+QKV, UP, OUT, IN = range(4)
 COST = pl.CostEstimate(flops=1, bytes_accessed=1, transcendentals=0)
 
 
@@ -30,10 +37,6 @@
 def shift(value, axis, step):
     size = lax.axis_size(axis)
     return lax.ppermute(value, axis, [(i, (i + step) % size) for i in range(size)])
-
-
-def swap_core(value):
-    return shift(value, "core", 1)
 
 
 class Order:
@@ -89,8 +92,8 @@
 
 
 def width_table(layout):
-    n_y, n_x, n_c = lax.axis_size("dp"), lax.axis_size("x"), lax.axis_size("core")
-    y, x, c = lax.axis_index("dp"), lax.axis_index("x"), lax.axis_index("core")
+    n_y, n_x, n_c = lax.axis_size(Y), lax.axis_size(X), lax.axis_size(C)
+    y, x, c = lax.axis_index(Y), lax.axis_index(X), lax.axis_index(C)
     begins = jnp.stack(
         [
             ((((y - a + n_y) % n_y) * n_x + (x - b + n_x) % n_x) * n_c + (c - k + n_c) % n_c)
@@ -108,7 +111,7 @@
 class Layout:
     def __init__(self, own_tokens, part):
         self.n_y, self.n_x, self.n_c, self.n_z = (
-            lax.axis_size(name) for name in ("dp", "x", "core", "col")
+            lax.axis_size(name) for name in (Y, X, C, Z)
         )
         self.own_tokens = own_tokens
         self.tokens = own_tokens * self.n_c
@@ -133,7 +136,7 @@
         return copies
 
 
-def kernel_call(body, table, inputs, in_specs, out_shape, out_specs, scratch, name, grid=(1,), aliases=None):
+def kernel_call(body, table, inputs, in_specs, out_shape, out_specs, scratch, name, grid=(1,), aliases=None, mebi=VMEM_MEBI):
     return pl.pallas_call(
         body,
         grid_spec=pltpu.PrefetchScalarGridSpec(
@@ -145,7 +148,7 @@
         ),
         out_shape=out_shape,
         input_output_aliases=aliases or {},
-        compiler_params=pltpu.CompilerParams(vmem_limit_bytes=VMEM_BYTES),
+        compiler_params=pltpu.CompilerParams(vmem_limit_bytes=mebi * MEBI),
         cost_estimate=COST,
         name=name,
     )(table, *inputs)
@@ -183,10 +186,12 @@
     rest = jnp.ones((angles.shape[0], HEAD_DIM - ROT), F32)
     none = jnp.zeros_like(sine)
     pair = lambda *pieces: jnp.concatenate(pieces * HEADS_TILE, axis=1)
-    return (
-        pair(cosine, cosine, rest),
-        pair(-sine, none, 0.0 * rest),
-        pair(none, sine, 0.0 * rest),
+    return jnp.stack(
+        [
+            pair(cosine, cosine, rest),
+            pair(-sine, none, 0.0 * rest),
+            pair(none, sine, 0.0 * rest),
+        ]
     )
 
 
@@ -260,18 +265,22 @@
 
     def body(table_ref, g_ref, *rest):
         w_refs, rest = rest[:count], rest[count:]
-        bias_ref, cos_ref, low_ref, up_ref, q_ref, kv_ref, features = rest[:7]
-        buffers, (sems, w_sems, total) = rest[7 : 7 + count], rest[7 + count :]
+        bias_ref, tables_ref, q_ref, kv_ref, features = rest[:5]
+        buffers, (sems, w_sems, total, turns, turn_sem) = rest[5 : 5 + count], rest[5 + count :]
         window = slice(0, 3 * columns)
         stream = Stream(layout, table_ref, g_ref, w_refs, features, buffers, sems, w_sems, window)
+        turn = pltpu.make_async_copy(tables_ref, turns, turn_sem)
+        turn.start()
 
         def finish(core, part, value):
+            if core == 0 and part.start == 0:
+                turn.wait()
             here = slice(core * rows, (core + 1) * rows)
             value = value + bias_ref[:, part]
             for lanes in chunks(columns, LANES):
                 piece = value[:, lanes]
                 if part.start < 2 * columns:
-                    piece = rope(piece, cos_ref[here], low_ref[here], up_ref[here])
+                    piece = rope(piece, *(turns[i, here, :] for i in range(3)))
                 begin = part.start + lanes.start
                 if part.start < columns:
                     q_ref[here, begin : begin + LANES] = piece.astype(BF16)
@@ -292,12 +301,14 @@
     return kernel_call(
         body,
         table,
-        [gathered, *blocks, bias, *tables],
-        [ANY] * (1 + count) + [full(bias)] + [full(t) for t in tables],
+        [gathered, *blocks, bias, tables],
+        [HBM] * (1 + count) + [full(bias), HBM],
         out,
         [full(o) for o in out],
-        Stream.scratch(layout, (layout.block, 3 * columns), 3 * columns),
+        Stream.scratch(layout, (layout.block, 3 * columns), 3 * columns)
+        + [pltpu.VMEM(tables.shape, F32), pltpu.SemaphoreType.DMA],
         "project_qkv",
+        mebi=MORE_MEBI,
     )
 
 
@@ -354,13 +365,14 @@
         body,
         table,
         [gathered, *blocks, *extra, bias],
-        [ANY] * (1 + count) + [full(e) for e in extra] + [full(bias)],
+        [HBM] * (1 + count) + [full(e) for e in extra] + [full(bias)],
         out,
         [ANY, ANY],
         Stream.scratch(layout, (layout.block, hidden), hidden)
         + [pltpu.VMEM((layout.tokens, hidden), BF16)] * 2
         + [pltpu.SemaphoreType.DMA((layout.n_c, 2))],
         "project_up",
+        mebi=MORE_MEBI,
     )
 
 
@@ -415,13 +427,14 @@
         body,
         table,
         [gathered, *blocks, *extra],
-        [ANY] * (1 + count) + [full(e) for e in extra],
+        [HBM] * (1 + count) + [full(e) for e in extra],
         out,
         [ANY, ANY],
         Stream.scratch(layout, blocks[0].shape, height)
         + [pltpu.VMEM(o.shape, BF16) for o in out]
         + [pltpu.SemaphoreType.DMA((layout.n_c, 2))],
         "branch_grads",
+        mebi=MORE_MEBI,
     )
 
 
@@ -431,11 +444,12 @@
     sizes = [left.shape[1] for left in lefts]
     flat = [w for block in weights for w in block]
     n = len(lefts)
+    step = rows // PIECES
 
     def body(table_ref, *rest):
         left_refs, rest = rest[:n], rest[n:]
         w_refs, rest = rest[: len(flat)], rest[len(flat) :]
-        out_refs, rest = rest[:3], rest[3:]
+        out_refs, rest = rest[: PIECES + 1], rest[PIECES + 1 :]
         left_bufs, rest = rest[:n], rest[n:]
         w_bufs, (out_buf, sems, w_sems, out_sems) = rest[: len(flat)], rest[len(flat) :]
         core = table_ref[2 * layout.places]
@@ -474,38 +488,42 @@
                     term = contract(buf[half], w, 1, 1 if transposed else 0)
                     total = term if total is None else total + term
                 out_buf[half, :, b * layout.block : (b + 1) * layout.block] = total.astype(BF16)
-            pieces = [out_buf.at[0, : rows // 2], out_buf.at[0, rows // 2 :]] if half == 0 else [out_buf.at[1]]
+            pieces = [out_buf.at[0, i * step : (i + 1) * step] for i in range(PIECES)]
+            pieces = pieces if half == 0 else [out_buf.at[1]]
             for piece in pieces:
                 at = len(outs)
                 outs.append(pltpu.make_async_copy(piece, out_refs[at], out_sems.at[at]))
                 outs[-1].start()
         wait_all(outs)
 
-    out = [jax.ShapeDtypeStruct((size, layout.width), BF16) for size in (rows // 2, rows // 2, rows)]
+    out = [jax.ShapeDtypeStruct((size, layout.width), BF16) for size in [step] * PIECES + [rows]]
     return kernel_call(
         body,
         table,
         [*lefts, *flat],
-        [ANY] * (n + len(flat)),
+        [ANY] * n + [HBM] * len(flat),
         out,
-        [ANY] * 3,
+        [ANY] * (PIECES + 1),
         [pltpu.VMEM((2, rows, size), BF16) for size in sizes]
         + [pltpu.VMEM(w.shape, BF16) for w in flat]
         + [
             pltpu.VMEM((2, rows, layout.width), BF16),
             pltpu.SemaphoreType.DMA((2, n)),
             pltpu.SemaphoreType.DMA((len(flat),)),
-            pltpu.SemaphoreType.DMA((3,)),
+            pltpu.SemaphoreType.DMA((PIECES + 1,)),
         ],
         name,
+        mebi=MORE_MEBI,
     )
 
 
 def merge_cores(layout, table, own, received):
-    rows = layout.own_tokens // 2
+    rows = layout.own_tokens // PIECES
     place, places, n_c = layout.place, layout.places, layout.n_c
 
-    def body(table_ref, own_ref, first_ref, second_ref, out_ref):
+    def body(table_ref, own_ref, *refs):
+        out_ref = refs[PIECES]
+
         def write(other_ref):
             for at in range(places):
                 begin = pl.multiple_of(table_ref[2 * places + 1 + at], place)
@@ -514,8 +532,8 @@
                 total = total + other_ref[:, there * place : (there + 1) * place].astype(F32)
                 out_ref[:, pl.ds(begin, place)] = total.astype(BF16)
 
-        pl.when(pl.program_id(0) == 0)(lambda: write(first_ref))
-        pl.when(pl.program_id(0) == 1)(lambda: write(second_ref))
+        for i in range(PIECES):
+            pl.when(pl.program_id(0) == i)(lambda i=i: write(refs[i]))
 
     spec = pl.BlockSpec((rows, layout.width), lambda i, t: (i, 0))
     return kernel_call(
@@ -527,7 +545,7 @@
         spec,
         [],
         "merge_cores",
-        grid=(2,),
+        grid=(PIECES,),
     )
 
 
@@ -591,14 +609,12 @@
                     continue
                 for buf in add_bufs:
                     value = value + buf[begin : begin + place, :].astype(F32)
-                if k > 0:
-                    away = outs[2] if i == 0 else outs[3]
-                    at = (max(i - 1, 0) * (n_c - 1) + k - 1) * place
-                    away[at : at + place, :] = value.astype(BF16)
-                elif i == 0:
+                if i > 0:
+                    outs[2][begin - block : begin - block + place, :] = value.astype(BF16)
+                elif k > 0:
+                    outs[1][(k - 1) * place : k * place, :] = value.astype(BF16)
+                else:
                     outs[0][...] = value
-                else:
-                    outs[1][(i - 1) * place : i * place, :] = value.astype(BF16)
             if not final:
                 here = slice(i * block, (i + 1) * block)
                 copies.append(pltpu.make_async_copy(out_buf.at[here], outs[0].at[here], out_sems.at[i]))
@@ -606,12 +622,10 @@
         wait_all(copies)
 
     if final:
-        away = (n_c - 1) * place
         out = [
             jax.ShapeDtypeStruct((place, n), F32),
-            jax.ShapeDtypeStruct(((count - 1) * place, n), BF16),
-            jax.ShapeDtypeStruct((away, n), BF16),
-            jax.ShapeDtypeStruct(((count - 1) * away, n), BF16),
+            jax.ShapeDtypeStruct((block - place, n), BF16),
+            jax.ShapeDtypeStruct(((count - 1) * block, n), BF16),
         ]
         more = [pltpu.VMEM(e.shape, BF16) for e in extra]
         more.append(pltpu.SemaphoreType.DMA((len(extra),)))
@@ -622,7 +636,7 @@
         body,
         table,
         [gathered, right, *extra],
-        [ANY] * (2 + len(extra)),
+        [HBM] + [ANY] * (1 + len(extra)),
         out,
         [full(o) for o in out] if final else [ANY],
         [
@@ -633,6 +647,7 @@
         ]
         + more,
         "grad_in",
+        mebi=MORE_MEBI,
     )
 
 
@@ -692,10 +707,9 @@
                         value = value + buf[rows, :].astype(F32)
                     if i == 0:
                         outs[0][rows, :] = value[:, :place]
-                        outs[2][rows, :] = value[:, place:].astype(BF16)
+                        outs[1][rows, :] = value[:, place:].astype(BF16)
                     else:
-                        outs[1][i - 1, rows, :] = value[:, :place].astype(BF16)
-                        outs[3][i - 1, rows, :] = value[:, place:].astype(BF16)
+                        outs[1 + i][rows, :] = value.astype(BF16)
                 at += size
             if not final:
                 copies.append(pltpu.make_async_copy(out_buf.at[i], outs[i], out_sems.at[i]))
@@ -705,9 +719,8 @@
     if final:
         out = [
             jax.ShapeDtypeStruct((m, place), F32),
-            jax.ShapeDtypeStruct((count - 1, m, place), BF16),
             jax.ShapeDtypeStruct((m, block - place), BF16),
-            jax.ShapeDtypeStruct((count - 1, m, block - place), BF16),
+            *[jax.ShapeDtypeStruct((m, block), BF16)] * (count - 1),
         ]
         more = [pltpu.VMEM(e.shape, BF16) for e in extra]
         more.append(pltpu.SemaphoreType.DMA((len(extra),)))
@@ -718,7 +731,7 @@
         body,
         table,
         [gathered, *lefts, *extra],
-        [ANY] * (1 + n + len(extra)),
+        [HBM] + [ANY] * (n + len(extra)),
         out,
         [full(o) for o in out] if final else [ANY] * count,
         [
@@ -729,6 +742,30 @@
         + [pltpu.VMEM(left.shape, BF16) for left in lefts]
         + more,
         "grad_out",
+        mebi=MORE_MEBI,
+    )
+
+
+def fold(table, away, near, rows):
+    m, n = away.shape
+    spec = pl.BlockSpec((m, n), lambda i, t: (1, 0) if rows else (0, 1))
+
+    def body(table_ref, away_ref, *refs):
+        near_refs, out_ref = refs[:-1], refs[-1]
+        total = away_ref[...].astype(F32)
+        for ref in near_refs:
+            total = total + ref[...].astype(F32)
+        out_ref[...] = total.astype(BF16)
+
+    return kernel_call(
+        body,
+        table,
+        [away, *near],
+        [full(away)] + [spec] * len(near),
+        jax.ShapeDtypeStruct((m, n), BF16),
+        full(away),
+        [],
+        "fold",
     )
 
 
@@ -746,7 +783,7 @@
                 out_ref[...] = value
             else:
                 for i in range(parts):
-                    out_ref[:, i, :] = value[:, i * step : (i + 1) * step]
+                    out_ref[i] = value[:, i * step : (i + 1) * step]
 
         pl.when(pl.program_id(0) == 0)(lambda: write(refs[: len(owns)]))
         pl.when(pl.program_id(0) == 1)(lambda: write(refs[len(owns) :]))
@@ -755,13 +792,13 @@
     if parts == 1:
         spec = pl.BlockSpec((None, rows, n), lambda i, t: (layer, 0, half(i, t)))
     else:
-        spec = pl.BlockSpec((None, rows, parts, step), lambda i, t: (layer, 0, 0, half(i, t)))
+        spec = pl.BlockSpec((None, parts, rows, step), lambda i, t: (layer, 0, 0, half(i, t)))
     more = [] if held is None else [held]
     return kernel_call(
         body,
         table,
         inputs + more,
-        [full(v) for v in inputs] + [ANY] * len(more),
+        [pl.BlockSpec((rows, n), lambda i, t: (0, 0)) for v in inputs] + [ANY] * len(more),
         jax.ShapeDtypeStruct(shape, F32),
         spec,
         [],
@@ -794,7 +831,7 @@
         body,
         table,
         inputs + more,
-        [full(v) for v in inputs] + [ANY] * len(more),
+        [pl.BlockSpec((m, place), lambda i, t: (0, 0)) for v in inputs] + [ANY] * len(more),
         [jax.ShapeDtypeStruct(shape, F32) for shape in shapes],
         [pl.BlockSpec((None, size, place), lambda i, t: (layer, half(i, t), 0)) for size in sizes],
         [],
@@ -1015,13 +1052,13 @@
     rows = math.gcd(tokens, 512)
 
     def body(table_ref, q_ref, own_ref, *rest):
-        far_refs, (cos_ref, low_ref, up_ref, out_ref, sum_ref) = rest[: len(far_pairs)], rest[len(far_pairs) :]
+        far_refs, (turn_ref, out_ref, sum_ref) = rest[: len(far_pairs)], rest[len(far_pairs) :]
 
         @pl.when(pl.program_id(0) == 0)
         def _():
             sum_ref[...] = jnp.zeros_like(sum_ref)
 
-        cosine, lower, upper = cos_ref[...], -low_ref[...], -up_ref[...]
+        cosine, lower, upper = turn_ref[0], -turn_ref[1], -turn_ref[2]
         for tile in range(3 * columns // LANES):
             here = slice(tile * LANES, (tile + 1) * LANES)
             if tile < columns // LANES:
@@ -1043,12 +1080,13 @@
         jax.ShapeDtypeStruct((tokens, 3 * columns), BF16),
         jax.ShapeDtypeStruct((1, 3 * columns), F32),
     ]
-    inputs = [query_grad, own_pairs, *far_pairs, *tables]
+    inputs = [query_grad, own_pairs, *far_pairs]
     return kernel_call(
         body,
         table,
-        inputs,
-        [spec(array) for array in inputs],
+        [*inputs, tables],
+        [spec(array) for array in inputs]
+        + [pl.BlockSpec((3, rows, LANES), lambda i, s: (0, i, 0))],
         out,
         [spec(out[0]), full(out[1])],
         [],
@@ -1057,15 +1095,107 @@
     )
 
 
+def cut_weights(layout, table, sources):
+    n = len(sources)
+    pieces = [source.pieces for source in sources]
+
+    def body(table_ref, *rest):
+        refs, outs, sems = rest[:n], rest[n : 3 * n], rest[3 * n]
+        core = table_ref[2 * layout.places]
+        copies = []
+        for i, source in enumerate(sources):
+            for j in range(pieces[i]):
+                for k, half in enumerate((core, 1 - core)):
+                    copies.append(
+                        pltpu.make_async_copy(
+                            source.read(refs[i], half, j),
+                            source.part(outs[2 * i + k], j),
+                            sems.at[i, j, k],
+                        )
+                    )
+        start_all(copies)
+        wait_all(copies)
+
+    return kernel_call(
+        body,
+        table,
+        [source.array for source in sources],
+        [HBM] * n,
+        [jax.ShapeDtypeStruct(source.shape, BF16) for source in sources for _ in range(2)],
+        [HBM] * (2 * n),
+        [pltpu.SemaphoreType.DMA((n, max(pieces), 2))],
+        "cut_weights",
+    )
+
+
+def join_weights(table, sources, shape, owns, received):
+    n = len(sources)
+
+    def body(table_ref, *rest):
+        refs, out_ref = rest[: 2 * n], rest[2 * n]
+        for i, source in enumerate(sources):
+            out_ref[source.place()] = refs[i][...]
+            out_ref[source.other()] = refs[n + i][...]
+
+    out = jax.ShapeDtypeStruct(shape, BF16)
+    arrays = [*owns, *received]
+    return kernel_call(
+        body, table, arrays, [full(a) for a in arrays], out, full(out), [], "join_weights"
+    )
+
+
+class RowSource:
+    def __init__(self, array, layer, begin):
+        self.array, self.layer, self.begin = array, layer, begin
+        self.split = array.ndim == 4
+        self.pieces = array.shape[1] if self.split else 1
+        self.rows = array.shape[-2]
+        self.size = array.shape[-1] // 2
+        self.shape = (self.rows, self.pieces * self.size)
+
+    def read(self, ref, core, piece):
+        here = pl.ds(pl.multiple_of(core * self.size, self.size), self.size)
+        return ref.at[self.layer, piece, :, here] if self.split else ref.at[self.layer, :, here]
+
+    def place(self):
+        return slice(0, self.rows), slice(self.begin, self.begin + self.shape[1])
+
+    def other(self):
+        return slice(self.rows, 2 * self.rows), slice(self.begin, self.begin + self.shape[1])
+
+    def part(self, target, piece):
+        return target.at[:, piece * self.size : (piece + 1) * self.size]
+
+
+class ColumnSource:
+    pieces = 1
+
+    def __init__(self, array, layer, begin):
+        self.array, self.layer, self.begin = array, layer, begin
+        self.size, self.columns = array.shape[1] // 2, array.shape[2]
+        self.shape = (self.size, self.columns)
+
+    def read(self, ref, core, piece):
+        return ref.at[self.layer, pl.ds(pl.multiple_of(core * self.size, self.size), self.size), :]
+
+    def place(self):
+        return slice(self.begin, self.begin + self.size), slice(0, self.columns)
+
+    def other(self):
+        return slice(self.begin, self.begin + self.size), slice(self.columns, 2 * self.columns)
+
+    def part(self, target, piece):
+        return target
+
+
 def core_half(value, axis, which):
-    size = value.shape[axis] // lax.axis_size("core")
+    size = value.shape[axis] // lax.axis_size(C)
     return lax.dynamic_slice_in_dim(value, which * size, size, axis)
 
 
 def in_core_order(own, other, axis):
-    core = lax.axis_index("core")
     return jnp.where(
-        core == 0,
+        lax.axis_index(C) == 0,
         jnp.concatenate([own, other], axis=axis),
         jnp.concatenate([other, own], axis=axis),
     )
@@ -1080,18 +1210,23 @@
     def near(self, depth=1):
         for i in range(1, self.n1):
             self.found[i, 0] = self.order.send(self.found[0, 0], self.first, i, depth)
+        return [self.found[i, 0] for i in range(1, self.n1)]
 
     def side(self, depth=1):
         for j in range(1, self.n2):
             self.found[0, j] = self.order.send(self.found[0, 0], self.second, j, depth)
+        return [self.found[0, j] for j in range(1, self.n2)]
 
     def cross(self, depth=1):
+        found = []
         for i in range(1, self.n1):
             for j in range(1, self.n2):
                 self.found[i, j] = self.order.send(self.found[i, 0], self.second, j, depth)
+                found.append(self.found[i, j])
+        return found
 
     def blocks(self):
-        if self.first == "x":
+        if self.first == X:
             return [self.found[b, a] for a in range(self.n2) for b in range(self.n1)]
         return [self.found[a, b] for a in range(self.n1) for b in range(self.n2)]
 
@@ -1100,8 +1235,6 @@
     def __init__(self, order, layout, table, features, right):
         self.order, self.layout, self.table = order, layout, table
         self.features, self.right = features, right
-
-    parts = None
 
     def compute(self):
         layout, n_x = self.layout, self.layout.n_x
@@ -1111,33 +1244,33 @@
         )
 
     def begin(self, depth=1):
-        if self.parts is None:
-            self.compute()
         size = self.layout.n_x * self.layout.block
         self.received = [
-            self.order.send(self.parts[(a - 1) * size : a * size], "dp", -a, depth)
+            self.order.send(self.parts[(a - 1) * size : a * size], Y, -a, depth)
             for a in range(1, self.layout.n_y)
         ]
 
     def middle(self):
         layout = self.layout
-        self.first, self.others, away, others_away = self.order.run(
+        self.first, self.away, self.others = self.order.run(
             lambda f, r, d: grad_in(layout, self.table, f, r, range(layout.n_x), d),
             self.features,
             self.right,
             self.received,
         )
-        self.others_away = self.order.send(others_away, "core", 1, 1)
-        self.away = self.order.send(away, "core", 1, 2)
-
-    def finish(self, depth=1):
-        place = self.layout.place
-        near, cross = [], []
-        for b in range(1, self.layout.n_x):
-            here = slice((b - 1) * place, b * place)
-            near.append(self.order.send(self.others[here], "x", -b, depth))
-            cross.append(self.order.send(self.others_away[here], "x", -b, depth + 1))
-        self.sums = ([self.first, *near], [self.away, *cross])
+
+    def finish(self, depth=2):
+        block = self.layout.block
+        self.near = [
+            self.order.send(self.others[(b - 1) * block : b * block], X, -b, depth)
+            for b in range(1, self.layout.n_x)
+        ]
+
+    def swap(self):
+        away = self.order.run(
+            lambda a, b: fold(self.table, a, b, True), self.away, self.near
+        )
+        self.sums = ([self.first, *self.near], [self.order.send(away, C, 1, 3)])
 
 
 class ScatterOut:
@@ -1157,26 +1290,31 @@
         n_x = self.layout.n_x
         for b in range(1, n_x):
             part = self.parts[a * (n_x - 1) + b - 1]
-            self.received[a].append(self.order.send(part, "x", -b, depth))
+            self.received[a].append(self.order.send(part, X, -b, depth))
+
+    def all_received(self):
+        return [value for row in self.received for value in row]
 
     def middle(self):
         layout = self.layout
         which = [a * layout.n_x for a in range(layout.n_y)]
-        self.first, self.others, away, others_away = self.order.run(
+        self.first, self.away, *self.others = self.order.run(
             lambda l, g, d: grad_out(layout, self.table, l, g, which, d),
             self.lefts,
             self.grad,
             self.received,
         )
-        self.others_away = self.order.send(others_away, "core", 1, 1)
-        self.away = self.order.send(away, "core", 1, 2)
-
-    def finish(self, depth=1):
-        near, cross = [], []
-        for a in range(1, self.layout.n_y):
-            near.append(self.order.send(self.others[a - 1], "dp", -a, depth))
-            cross.append(self.order.send(self.others_away[a - 1], "dp", -a, depth + 1))
-        self.sums = ([self.first, *near], [self.away, *cross])
+
+    def finish(self, depth=2):
+        self.near = [
+            self.order.send(self.others[a - 1], Y, -a, depth) for a in range(1, self.layout.n_y)
+        ]
+
+    def swap(self):
+        away = self.order.run(
+            lambda a, b: fold(self.table, a, b, False), self.away, self.near
+        )
+        self.sums = ([self.first, *self.near], [self.order.send(away, C, 1, 3)])
 
 
 def per_device(
@@ -1197,8 +1335,8 @@
 ):
     layer_count = qkv_weight.shape[0]
     last = layer_count - 1
-    core, x = lax.axis_index("core"), lax.axis_index("x")
-    z, n_z = lax.axis_index("col"), lax.axis_size("col")
+    core, x = lax.axis_index(C), lax.axis_index(X)
+    z, n_z = lax.axis_index(Z), lax.axis_size(Z)
     layout = Layout(*layer_input.shape)
     n_x = layout.n_x
     tokens, width = layout.tokens, layout.width
@@ -1210,52 +1348,69 @@
         jnp.stack([query_begin, (x - b + n_x) % n_x * tokens]).astype(jnp.int32) for b in range(n_x)
     ]
     order = Order()
-
-
-    def pieces_of(layer, group):
-        which = order.after([core])[0]
-        pieces = []
-        for half in (which, 1 - which):
-            if group == "out":
-                parts = [core_half(w[layer], 0, half) for w in (dense_weight, down_weight)]
-                pieces.append(jnp.concatenate(parts, axis=0))
-                continue
-            parts = []
-            if group in ("qkv", "in"):
-                parts.append(core_half(qkv_weight[layer], 2, half).reshape(-1, 3 * columns))
-            if group in ("up", "in"):
-                parts.append(core_half(up_weight[layer], 1, half))
-            pieces.append(parts[0] if len(parts) == 1 else jnp.concatenate(parts, axis=1))
-        return (*pieces, 1 if group == "out" else 0)
+    gathers = {}
+    kept = [SimpleNamespace(layer=layer) for layer in range(layer_count)]
+    outputs = [None] * layer_count
+    sums = [None] * layer_count
+
+    def arrived(*transfers):
+        order.wait(*transfers)
+
+
+    def sources_of(layer, group):
+        if group == OUT:
+            shape = (columns + hidden, layout.block)
+            return shape, [
+                ColumnSource(dense_weight, layer, 0),
+                ColumnSource(down_weight, layer, columns),
+            ]
+        sources = []
+        if group != UP:
+            sources.append(RowSource(qkv_weight.transpose(0, 2, 1, 3), layer, 0))
+        if group != QKV:
+            begin = 3 * columns if group == IN else 0
+            sources.append(RowSource(up_weight, layer, begin))
+        return (layout.block, sum(source.shape[1] for source in sources)), sources
 
     def make_ready(layer, groups):
-        pieces = [pieces_of(layer, group) for group in groups]
-        swapped = [swap_core(other) for _, other, _ in pieces]
-        blocks = [
-            jnp.concatenate([own, other], axis=axis)
-            for (own, _, axis), other in zip(pieces, swapped)
-        ]
-        for group, block in zip(groups, order.wait(*blocks)):
-            ways = ("dp", "x") if group == "out" else ("x", "dp")
+        found = []
+        for group in groups:
+            shape, sources = sources_of(layer, group)
+
+            def cut(arrays, sources=sources):
+                for source, array in zip(sources, arrays):
+                    source.array = array
+                return cut_weights(layout, table, sources)
+
+            parts = order.run(cut, [source.array for source in sources])
+            found.append((sources, shape, parts[::2], parts[1::2]))
+        swapped = [[shift(value, C, 1) for value in order.after(away)] for *_, away in found]
+        for group, (sources, shape, owns, _), received in zip(groups, found, swapped):
+            block = order.run(
+                lambda o, r, s=sources, h=shape: join_weights(table, s, h, o, r), owns, received
+            )
+            ways = (Y, X) if group == OUT else (X, Y)
             gathers[layer, group] = Gather(order, block, *ways)
 
     def blocks_of(layer, group):
         if (layer, group) not in gathers:
-            group = "in"
+            group = IN
         return gathers[layer, group].blocks()
 
 
     def gather_features(block):
-        return lax.all_gather(order.after([block])[0], ("core", "col"), axis=0, tiled=False)
+        return lax.all_gather(order.after([block])[0], (C, Z), axis=0, tiled=False)
 
     def scatter_features(summed):
-        return lax.psum_scatter(order.after([summed])[0], "col", scatter_dimension=1, tiled=True)
-
-    def to_owner(lefts, weights, transposed, name):
+        return lax.psum_scatter(order.after([summed])[0], Z, scatter_dimension=1, tiled=True)
+
+    def to_owner(lefts, weights, transposed, name, awaited=()):
         *away, own = order.run(
             lambda *a: project_back(layout, table, a[0], a[1], transposed, name), lefts, weights
         )
-        received = [order.send(piece, "core", 1, 2) for piece in away]
+        received = [order.send(piece, C, 1, PIECES) for piece in away]
+        if awaited:
+            order.wait(*awaited)
         return order.run(lambda a, b: merge_cores(layout, table, a, b), own, received)
 
     def moments(value, axes):
@@ -1265,12 +1420,15 @@
     def inverse_of(mean, square):
         return lax.rsqrt(square - mean * mean + EPSILON)
 
-    def normalise(residual, layer):
+    def normalise(k, residual):
         stats = jnp.stack([jnp.sum(residual, axis=1), jnp.sum(residual * residual, axis=1)])
-        stats = sum_over(stats, "col") / width
-        inverse = inverse_of(stats[0], stats[1])
-        centred = (residual - stats[0][:, None]) * inverse[:, None]
-        return (centred * norm_gain[layer] + norm_bias[layer]).astype(BF16), centred, inverse
+        stats = sum_over(stats, Z) / width
+        k.inverse = inverse_of(stats[0], stats[1])
+        k.centred = (residual - stats[0][:, None]) * k.inverse[:, None]
+        normed = (k.centred * norm_gain[k.layer] + norm_bias[k.layer]).astype(BF16)
+        (normed,) = order.wait(normed)
+        k.features = gather_features(normed)
+        order.wait(normed)
 
     def qkv_shift(layer):
         return core_half(qkv_bias[layer], 1, core).reshape(1, -1)
@@ -1278,324 +1436,283 @@
     def up_shift(layer):
         return core_half(up_bias[layer], 0, core).reshape(1, -1)
 
-    def send_pairs(k, pairs):
-        k["pairs"] = [pairs] + [order.send(pairs, "x", b) for b in range(1, n_x)]
-
-    def project_q(layer):
-        k = kept[layer]
-        k["q"], pairs = order.run(
+    def project_q(k):
+        k.q, pairs = order.run(
             lambda f, w, b, t: project_qkv(layout, table, f, w, b, t),
-            k["features"],
-            blocks_of(layer, "qkv"),
-            qkv_shift(layer),
+            k.features,
+            blocks_of(k.layer, QKV),
+            qkv_shift(k.layer),
             tables,
         )
-        send_pairs(k, pairs)
-
-    def own_attention(layer):
-        k = kept[layer]
-        k["found"] = order.run(attend, begins[0], k["q"], k["pairs"][0], starts)
-
-    def far_attention(layer):
-        k = kept[layer]
+        k.pairs = [pairs] + [order.send(pairs, X, b) for b in range(1, n_x)]
+
+    def project_hidden(k, *grad):
+        k.active, k.slope = order.run(
+            lambda f, w, b, *g: project_up(layout, table, f, w, b, *g),
+            k.features,
+            blocks_of(k.layer, UP),
+            up_shift(k.layer),
+            *grad,
+        )
+
+    def grads_of_branch(k, grad_features, *slope):
+        k.mixed_grad, k.hidden_grad = order.run(
+            lambda g, w, *s: branch_grads(layout, table, g, w, columns, *s),
+            grad_features,
+            blocks_of(k.layer, OUT),
+            *slope,
+        )
+
+    def own_attention(k):
+        k.found = order.run(attend, begins[0], k.q, k.pairs[0], starts)
+
+    def far_attention(k):
         for b in range(1, n_x):
-            k["found"] = order.run(
-                attend, begins[b], k["q"], k["pairs"][b], starts, k["found"][1:]
-            )
-        k["mixed_low"], k["mixed"], k["logs"] = k["found"]
-
-    def far_gradients(layer):
-        k = kept[layer]
-        query_grad, k["away_pairs"] = [], []
+            k.found = order.run(attend, begins[b], k.q, k.pairs[b], starts, k.found[1:])
+        k.mixed_low, k.mixed, k.logs = k.found
+
+    def far_gradients(k):
+        k.query_grad, k.away_pairs = [], []
         for b in range(1, n_x):
             found, pair_grad = order.run(
                 lambda *a: attend_backward(*a[:7], False, *a[7:]),
-                begins[b],
-                k["q"],
-                k["pairs"][b],
-                starts,
-                k["mixed"],
-                k["logs"],
-                k["mixed_grad"],
-                *query_grad,
+                *(begins[b], k.q, k.pairs[b], starts, k.mixed, k.logs, k.mixed_grad),
+                *k.query_grad,
             )
-            query_grad = [found]
-            k["away_pairs"].append(order.send(pair_grad, "x", -b))
-        k["query_grad"] = query_grad
-
-    def own_gradients(layer):
-        k = kept[layer]
-        k["query_grad"], k["own_pairs"] = order.run(
+            k.query_grad = [found]
+            k.away_pairs.append(order.send(pair_grad, X, -b))
+
+    def own_gradients(k):
+        k.query_grad, k.own_pairs = order.run(
             lambda *a: attend_backward(*a[:7], True, *a[7:]),
-            begins[0],
-            k["q"],
-            k["pairs"][0],
-            starts,
-            k["mixed"],
-            k["logs"],
-            k["mixed_grad"],
-            *k["query_grad"],
-        )
-
-    def join_gradients(layer):
-        k = kept[layer]
-        k["qkv_low"], k["qkv_sum"] = order.run(
-            lambda *a: join_qkv_grads(table, *a),
-            k["query_grad"],
-            k["own_pairs"],
-            k["away_pairs"],
-            tables,
-        )
-
-    gathers = {}
-    kept = [dict() for _ in range(layer_count)]
-    outputs = [None] * layer_count
-
-    def out_pairs(layer):
-        return [(block,) for block in gathers[layer, "out"].blocks()]
-
-    def in_pairs(layer):
-        if (layer, "in") in gathers:
-            return [(block,) for block in gathers[layer, "in"].blocks()]
-        return list(zip(gathers[layer, "qkv"].blocks(), gathers[layer, "up"].blocks()))
-
-
-    def arrived(*transfers):
-        order.wait(*transfers)
+            *(begins[0], k.q, k.pairs[0], starts, k.mixed, k.logs, k.mixed_grad),
+            *k.query_grad,
+        )
+
+    def join_gradients(k):
+        k.qkv_low, k.qkv_sum = order.run(
+            lambda *a: join_qkv_grads(table, *a), k.query_grad, k.own_pairs, k.away_pairs, tables
+        )
+
+    def branch_sum(k):
+        lefts = [k.mixed_low, k.active]
+        pairs = [(block,) for block in blocks_of(k.layer, OUT)]
+        return to_owner(lefts, pairs, False, "project_out")
+
+    def feature_sum(k, *awaited):
+        if (k.layer, IN) in gathers:
+            pairs = [(block,) for block in blocks_of(k.layer, IN)]
+        else:
+            pairs = list(zip(blocks_of(k.layer, QKV), blocks_of(k.layer, UP)))
+        return to_owner([k.qkv_low, k.up_low], pairs, True, "feature_grads", awaited)
+
+    def add_branch(residual, branch, layer):
+        return residual + branch.astype(F32) + dense_bias[layer] + down_bias[layer]
+
 
     residual = layer_input.astype(F32)
     raw = gather_features(layer_input)
-    make_ready(0, ["qkv"])
-    qkv, up, out = [None] * 3
-    gathers[0, "qkv"].near()
-    gathers[0, "qkv"].side()
+    make_ready(0, [QKV])
+    qkv = gathers[0, QKV]
+    first_near, first_side = qkv.near(), qkv.side()
     grad_features = gather_features(output_cotangent)
-    make_ready(0, ["up", "out"])
-    qkv, up, out = (gathers[0, group] for group in ("qkv", "up", "out"))
-    arrived(qkv.found[1, 0], qkv.found[0, 1])
-    up.near()
-    qkv.cross()
+    make_ready(0, [UP, OUT])
+    up, out = gathers[0, UP], gathers[0, OUT]
+    arrived(*first_near, *first_side)
+    up_near, qkv_cross = up.near(), qkv.cross()
     query_segments = lax.dynamic_slice_in_dim(segment_ids, query_begin, tokens, 0)
     starts = jnp.sum(
         (segment_ids[:, None] < query_segments[None, :]).astype(jnp.int32), axis=0, keepdims=True
     )
     places = lax.dynamic_slice_in_dim(positions, query_begin, tokens, 0)
     tables = rope_tables(order.after([places])[0])
-    starts, *tables = order.wait(starts, *tables)
+    starts, tables = order.wait(starts, tables)
     affine = order.after([jnp.stack([norm_gain[0], norm_bias[0]])])[0]
-    spread = [affine] + [shift(affine, "col", k) for k in range(1, n_z)]
+    spread = [affine] + [shift(affine, Z, k) for k in range(1, n_z)]
     spread = jnp.stack(spread)[(z - jnp.arange(n_z) + n_z) % n_z]
     (spread,) = order.wait(spread)
-    arrived(up.found[1, 0], *qkv.blocks()[1:])
-    out.near()
-    out.side()
+    arrived(*up_near, *qkv_cross)
+    out_near, out_side = out.near(), out.side()
     (raw,) = order.wait(raw)
     blocks = raw.reshape(layout.n_c, n_z, layout.own_tokens, layout.part).astype(F32)
     mean, square = moments(blocks, (1, 3))
     inverse = inverse_of(mean, square)
     gain, bias = (spread[:, i][None, :, None, :] for i in range(2))
     normed = (blocks - mean[:, None, :, None]) * inverse[:, None, :, None] * gain + bias
-    kept[0]["features"] = normed.astype(BF16).reshape(raw.shape)
-    kept[0]["inverse"] = lax.dynamic_index_in_dim(inverse, core, 0, keepdims=False)
+    kept[0].inverse = lax.dynamic_index_in_dim(inverse, core, 0, keepdims=False)
     own_mean = lax.dynamic_index_in_dim(mean, core, 0, keepdims=False)
-    (kept[0]["features"],) = order.wait(kept[0]["features"])
-    for layer in range(last):
-        k = kept[layer]
-        project_q(layer)
+    (kept[0].features,) = order.wait(normed.astype(BF16).reshape(raw.shape))
+    for k in kept[:-1]:
+        layer = k.layer
+        project_q(k)
         if layer == 0:
-            up.side(2)
-        own_attention(layer)
-        arrived(*k["pairs"][1:])
+            up_side = up.side(2)
+        own_attention(k)
+        arrived(*k.pairs[1:])
         if layer == 0:
-            arrived(up.found[0, 1], out.found[1, 0], out.found[0, 1])
-            out.cross()
-            up.cross()
-        far_attention(layer)
-        make_ready(layer + 1, ["in", "out"])
-        in_next, out_next = gathers[layer + 1, "in"], gathers[layer + 1, "out"]
+            arrived(*up_side, *out_near, *out_side)
+            out_cross, up_cross = out.cross(), up.cross()
+        far_attention(k)
+        make_ready(layer + 1, [IN, OUT])
+        in_next, out_next = gathers[layer + 1, IN], gathers[layer + 1, OUT]
         if layer == 0:
-            arrived(grad_features, *up.blocks()[1:])
-        out_next.near()
-        k["active"], k["slope"] = order.run(
-            lambda f, w, b: project_up(layout, table, f, w, b),
-            k["features"],
-            blocks_of(layer, "up"),
-            up_shift(layer),
-        )
-        arrived(*blocks_of(layer, "out")[1:])
-        summed = to_owner([k["mixed_low"], k["active"]], out_pairs(layer), False, "project_out")
-        arrived(*[out_next.found[a, 0] for a in range(1, layout.n_y)])
+            arrived(grad_features, *up_cross, *out_cross)
+        next_near, next_side = out_next.near(), out_next.side()
+        project_hidden(k)
+        summed = branch_sum(k)
+        arrived(*next_near, *next_side)
         branch = scatter_features(summed)
         order.wait(summed)
-        in_next.near()
-        in_next.side()
-        arrived(*[v for at, v in in_next.found.items() if at != (0, 0)])
+        arrived(*in_next.near(), *in_next.side())
         (branch,) = order.wait(branch)
-        residual = residual + branch.astype(F32) + dense_bias[layer] + down_bias[layer]
-        outputs[layer] = residual
-        normed, kept[layer + 1]["centred"], kept[layer + 1]["inverse"] = normalise(residual, layer + 1)
-        (normed,) = order.wait(normed)
-        kept[layer + 1]["features"] = gather_features(normed)
-        order.wait(normed)
-        out_next.side(1)
-        out_next.cross(2)
-        in_next.cross()
-        arrived(*in_next.blocks()[1:])
-        order.wait(kept[layer + 1]["features"])
+        residual = outputs[layer] = add_branch(residual, branch, layer)
+        k = kept[layer + 1]
+        normalise(k, residual)
+        next_cross, in_cross = out_next.cross(), in_next.cross()
+        if k.layer == last:
+            arrived(*next_cross)
+            grads_of_branch(k, grad_features)
+        arrived(*in_cross)
+        order.wait(k.features)
 
 
     k = kept[last]
-    project_q(last)
-    k["mixed_grad"], k["active_grad"] = order.run(
-        lambda g, w: branch_grads(layout, table, g, w, columns),
-        grad_features,
-        blocks_of(last, "out"),
-    )
-    k["active"], k["up_low"] = order.run(
-        lambda f, w, b, g: project_up(layout, table, f, w, b, g),
-        k["features"],
-        blocks_of(last, "up"),
-        up_shift(last),
-        k["active_grad"],
-    )
-    arrived(*k["pairs"][1:])
+    project_q(k)
+    project_hidden(k, k.hidden_grad)
+    k.up_low = k.slope
     gradient = output_cotangent.astype(F32)
-    sums = [None] * layer_count
-    held = {"up": None, "qkv": None, "out": None}
+    held = {UP: None, QKV: None, OUT: None}
     shapes = {
-        "up": (layer_count, layout.place, layout.n_c * hidden),
-        "qkv": (layer_count, layout.place, 3, layout.n_c * columns),
-        "out": [
+        UP: (layer_count, layout.place, layout.n_c * hidden),
+        QKV: (layer_count, 3, layout.place, layout.n_c * columns),
+        OUT: [
             (layer_count, layout.n_c * columns, layout.place),
             (layer_count, layout.n_c * hidden, layout.place),
         ],
     }
 
     def place(layer, group, scatter):
-        if group == "out":
-            held[group] = order.run(
-                lambda a, b, h: place_out(layout, table, layer, a, b, shapes[group], h),
-                *scatter.sums,
-                held[group],
-            )
-        else:
-            held[group] = order.run(
-                lambda a, b, h: place_in(
-                    layout, table, layer, a, b, shapes[group], h, 3 if group == "qkv" else 1
-                ),
-                *scatter.sums,
-                held[group],
-            )
-
-    def norm_backward(layer, normed_grad, gradient):
-        k = kept[layer]
+        def write(owns, others, before):
+            if group == OUT:
+                return place_out(layout, table, layer, owns, others, shapes[group], before)
+            parts = 3 if group == QKV else 1
+            return place_in(layout, table, layer, owns, others, shapes[group], before, parts)
+
+        held[group] = order.run(write, *scatter.sums, held[group])
+
+    def norm_backward(k, normed_grad, gradient):
         normed_grad = normed_grad.astype(F32)
-        scaled_grad = normed_grad * norm_gain[layer]
-        means = jnp.stack(
-            [jnp.sum(scaled_grad, axis=1), jnp.sum(scaled_grad * k["centred"], axis=1)]
-        )
-        means = sum_over(means, "col") / width
-        new = gradient + k["inverse"][:, None] * (
-            scaled_grad - means[0][:, None] - k["centred"] * means[1][:, None]
+        scaled_grad = normed_grad * norm_gain[k.layer]
+        means = jnp.stack([jnp.sum(scaled_grad, axis=1), jnp.sum(scaled_grad * k.centred, axis=1)])
+        means = sum_over(means, Z) / width
+        new = gradient + k.inverse[:, None] * (
+            scaled_grad - means[0][:, None] - k.centred * means[1][:, None]
         )
 
         def to_both(value):
             return in_core_order(value, jnp.zeros_like(value), value.ndim - 1).reshape(-1)
 
-        sums[layer] = jnp.concatenate(
+        sums[k.layer] = jnp.concatenate(
             [
-                jnp.sum(normed_grad * k["centred"], axis=0),
+                jnp.sum(normed_grad * k.centred, axis=0),
                 jnp.sum(normed_grad, axis=0),
-                to_both(k["qkv_sum"].reshape(3, columns)),
+                to_both(k.qkv_sum.reshape(3, columns)),
                 jnp.sum(gradient, axis=0),
-                to_both(jnp.sum(k["up_low"], axis=0, dtype=F32)),
+                to_both(jnp.sum(k.up_low, axis=0, dtype=F32)),
             ]
         )
         return new
 
-    kept[0]["centred"] = (layer_input.astype(F32) - own_mean[:, None]) * kept[0]["inverse"][:, None]
-
-    for layer in reversed(range(layer_count)):
-        k = kept[layer]
-        if layer < last:
+    kept[0].centred = (layer_input.astype(F32) - own_mean[:, None]) * kept[0].inverse[:, None]
+    before = None
+
+    for k in reversed(kept):
+        layer = k.layer
+        scatter_in = lambda right: ScatterIn(order, layout, table, k.features, right)
+        if layer == last:
+            own_attention(k)
+            arrived(*k.pairs[1:])
+            up = scatter_in(k.up_low)
+            up.compute()
+            up.begin()
+            far_attention(k)
+        else:
             (grad_features,) = order.wait(grad_features)
+            branch = None
             if layer + 1 == last:
                 branch = scatter_features(out_summed)
-                outputs[last] = residual + branch.astype(F32) + dense_bias[last] + down_bias[last]
-            k["mixed_grad"], k["up_low"] = order.run(
-                lambda g, w, s: branch_grads(layout, table, g, w, columns, s),
-                grad_features,
-                blocks_of(layer, "out"),
-                k["slope"],
-            )
-        up = ScatterIn(order, layout, table, k["features"], k["up_low"])
-        out_lefts = lambda: [k["mixed_low"], k["active"]]
+            grads_of_branch(k, grad_features, k.slope)
+            k.up_low = k.hidden_grad
+            up = scatter_in(k.up_low)
+        out = ScatterOut(order, layout, table, [k.mixed_low, k.active], grad_features)
+        far_gradients(k)
+        if layer < last:
+            up.compute()
+            up.begin()
+        own_gradients(k)
+        out.compute()
+        if layer < last:
+            arrived(*k.away_pairs)
+            out.begin(layout.n_y - 1, 1)
+        else:
+            arrived(*k.away_pairs, *up.received)
+        join_gradients(k)
+        qkv = scatter_in(k.qkv_low)
+        awaited = [] if layer == last else [*up.received, *out.received[-1]]
+        summed = feature_sum(k, *awaited)
+        normed_grad = scatter_features(summed)
+        order.wait(summed)
+        for a in reversed(range(layout.n_y - (layer < last))):
+            out.begin(a, 1)
+        qkv.compute()
+        qkv.begin()
+        up.middle()
         if layer == last:
-            up.begin()
-            own_attention(last)
-            far_attention(last)
-            out = ScatterOut(order, layout, table, out_lefts(), grad_features)
+            (normed_grad,) = order.wait(normed_grad)
+            gradient = norm_backward(k, normed_grad, gradient)
+            (low,) = order.wait(gradient.astype(BF16))
+            arrived(*out.all_received(), *qkv.received)
+            grad_features = gather_features(low)
+            order.wait(low)
+            up.finish(1)
+            out.middle()
+            out.finish(1)
+            qkv.middle()
+            qkv.finish(1)
+            out_summed = branch_sum(k)
+            arrived(*up.near, *qkv.near, *out.near)
         else:
-            out = ScatterOut(order, layout, table, out_lefts(), grad_features)
-            out.compute()
-            out.begin(layout.n_y - 1)
-            up.begin()
-        far_gradients(layer)
-        own_gradients(layer)
-        if layer == last:
-            out.compute()
-            arrived(*up.received)
-            up.middle()
-        arrived(*k["away_pairs"])
-        join_gradients(layer)
-        qkv = ScatterIn(order, layout, table, k["features"], k["qkv_low"])
-        if layer == last:
-            summed = to_owner([k["qkv_low"], k["up_low"]], in_pairs(layer), True, "feature_grads")
-            normed_grad = scatter_features(summed)
-            order.wait(summed)
-            for a in range(layout.n_y):
-                out.begin(a, 1)
-            qkv.begin()
-            out_summed = to_owner([k["mixed_low"], k["active"]], out_pairs(layer), False, "project_out")
+            for scatter in before:
+                scatter.swap()
+            for group, scatter in zip((UP, QKV, OUT), before):
+                place(layer + 1, group, scatter)
+            if branch is not None:
+                outputs[last] = add_branch(residual, branch, last)
+                (outputs[last],) = order.wait(outputs[last])
+            arrived(*out.all_received())
+            up.finish(1)
+            out.middle()
+            out.finish(1)
+            (normed_grad,) = order.wait(normed_grad)
+            gradient = norm_backward(k, normed_grad, gradient)
+            (gradient,) = order.wait(gradient)
             arrived(*qkv.received)
             qkv.middle()
-            (normed_grad,) = order.wait(normed_grad)
-            gradient = norm_backward(layer, normed_grad, gradient)
-            (low,) = order.wait(gradient.astype(BF16))
-            arrived(*[v for row in out.received for v in row])
-            grad_features = gather_features(low)
-            order.wait(low)
-            up.finish()
-            qkv.finish(2)
-            out.middle()
-            out.finish()
-            place(layer, "up", up)
-            place(layer, "qkv", qkv)
-            place(layer, "out", out)
-        else:
-            for a in range(layout.n_y - 1):
-                out.begin(a, 2)
-            qkv.compute()
-            qkv.begin(2)
-            summed = to_owner([k["qkv_low"], k["up_low"]], in_pairs(layer), True, "feature_grads")
-            arrived(*up.received, *qkv.received, *[v for row in out.received for v in row])
-            normed_grad = scatter_features(summed)
-            order.wait(summed)
-            up.middle()
-            up.finish(2)
-            out.middle()
-            out.finish(2)
-            qkv.middle()
-            qkv.finish(2)
-            (normed_grad,) = order.wait(normed_grad)
-            gradient = norm_backward(layer, normed_grad, gradient)
-            if layer == 0:
-                small = jnp.stack(sums)
-                for axis in ("core", "x", "dp"):
-                    small = sum_over(small, axis)
-            place(layer, "up", up)
-            place(layer, "out", out)
-            place(layer, "qkv", qkv)
+            qkv.finish(1)
+        before = (up, qkv, out)
+
+    up, qkv, out = before
+    small = sum_over(jnp.stack(order.after(sums)), C)
+    up.swap()
+    place(0, UP, up)
+    (small,) = order.wait(small)
+    small = sum_over(small, X)
+    out.swap()
+    place(0, OUT, out)
+    (small,) = order.wait(small)
+    small = sum_over(small, Y)
+    qkv.swap()
+    place(0, QKV, qkv)
 
     small, gradient, outputs = order.now((small, gradient, outputs))
     held = order.now(held)
@@ -1611,54 +1728,54 @@
         gradient,
         gain_grad,
         shift_grad,
-        held["qkv"],
+        held[QKV].transpose(0, 2, 1, 3),
         qkv_grad.reshape(layer_count, 3, both),
-        held["out"][0],
+        held[OUT][0],
         out_bias_grad,
-        held["up"],
+        held[UP],
         up_grad,
-        held["out"][1],
+        held[OUT][1],
         out_bias_grad,
     )
 
 
 def solution(mesh):
-    n_y, n_row, n_z = (mesh.shape[name] for name in ("dp", "row", "col"))
-    split = Mesh(mesh.devices.reshape(n_y, n_row // 2, 2, n_z), ("dp", "x", "core", "col"))
-    rows = ("dp", "x", "core")
+    n_y, n_row, n_z = (mesh.shape[name] for name in mesh.axis_names)
+    split = Mesh(mesh.devices.reshape(n_y, n_row // 2, 2, n_z), (Y, X, C, Z))
+    rows = (Y, X, C)
     placed = (
-        P(rows, "col"),
-        P("dp"),
-        P("dp"),
-        P(None, "col"),
-        P(None, "col"),
-        P(None, rows, None, "col"),
-        P(None, None, "col"),
-        P(None, "col", rows),
-        P(None, "col"),
-        P(None, rows, "col"),
-        P(None, "col"),
-        P(None, "col", rows),
-        P(None, "col"),
-        P(rows, "col"),
+        P(rows, Z),
+        P(Y),
+        P(Y),
+        P(None, Z),
+        P(None, Z),
+        P(None, rows, None, Z),
+        P(None, None, Z),
+        P(None, Z, rows),
+        P(None, Z),
+        P(None, rows, Z),
+        P(None, Z),
+        P(None, Z, rows),
+        P(None, Z),
+        P(rows, Z),
     )
     return jax.shard_map(
         per_device,
         mesh=split,
         in_specs=placed,
         out_specs=(
-            P(None, rows, "col"),
-            P(rows, "col"),
-            P(None, "col"),
-            P(None, "col"),
-            P(None, rows, None, "col"),
-            P(None, None, "col"),
-            P(None, "col", rows),
-            P(None, "col"),
-            P(None, rows, "col"),
-            P(None, "col"),
-            P(None, "col", rows),
-            P(None, "col"),
+            P(None, rows, Z),
+            P(rows, Z),
+            P(None, Z),
+            P(None, Z),
+            P(None, rows, None, Z),
+            P(None, None, Z),
+            P(None, Z, rows),
+            P(None, Z),
+            P(None, rows, Z),
+            P(None, Z),
+            P(None, Z, rows),
+            P(None, Z),
         ),
         check_vma=False,
     )

time: 795 us -> 714 us (0.90)
  waiting for transfers between devices: 290 us -> 228 us
  local copies, waits for them, and re-layouts: 104 us -> 77.9 us
  Pallas kernels: 274 us -> 293 us
    ppermute x67 -> x66, waiting for transfers between devices: 255 us -> 192 us  [shift(): lax.ppermute(value, axis, [(i, (i + step) % size) for i in range(size)])]
    pallas_call x42 -> x58, Pallas kernels: 274 us -> 293 us  [kernel_call(): pl.pallas_call(body, grid_spec=pltpu.PrefetchScalarGridSpec(num_scalar_pr...]
    dynamic_slice x10 -> x2, local copies, waits for them, and re-layouts: 9.83 us -> 0.02 us  [core_half(): return lax.dynamic_slice_in_dim(value, which * size, size, axis)]
    concatenate x10 -> x2, other arithmetic: 9.8 us -> 0.01 us  [norm_backward(): jnp.concatenate([jnp.sum(normed_grad * k.centred, axis=0), jnp.sum(normed...]
    ppermute x67 -> x66, starting transfers between devices: 60.8 us -> 51.5 us  [shift(): lax.ppermute(value, axis, [(i, (i + step) % size) for i in range(size)])]
    ppermute x9, waiting for transfers between devices: 19.2 us -> 27.3 us  [sum_over(): lax.ppermute(value, axis, [(i, i ^ step) for i in range(size)])]
    unnamed x282 -> x259, local copies, waits for them, and re-layouts: 72.9 us -> 68.7 us
  transfers between devices with their start and end apart: 84 -> 83, of which waited for: 40 -> 48; matrix products, arithmetic and copies ran while one was open for 9% -> 5% of each run, Pallas kernels for 32% -> 37%
where the time goes in v2:
time: 714 us; the launch traced here: 708 us
  Pallas kernels  293 us (41%)
  waiting for transfers between devices  228 us (32%)
  local copies, waits for them, and re-layouts  77.9 us (11%)
  starting transfers between devices  61.7 us (9%)
  other arithmetic  31.9 us (4%)
  between operations  16.2 us (2%)
    pallas_call x58, Pallas kernels, kernel_call(): pl.pallas_call(body, grid_spec=pltpu.PrefetchScalarGridSpec(num_scalar_pr...  293 us
    ppermute x66, waiting for transfers between devices, shift(): lax.ppermute(value, axis, [(i, (i + step) % size) for i in range(size)])  192 us
    unnamed x259, local copies, waits for them, and re-layouts  68.7 us
    ppermute x66, starting transfers between devices, shift(): lax.ppermute(value, axis, [(i, (i + step) % size) for i in range(size)])  51.5 us
    ppermute x9, waiting for transfers between devices, sum_over(): lax.ppermute(value, axis, [(i, i ^ step) for i in range(size)])  27.3 us
  transfers between devices with their start and end apart: 83, of which 48 were waited for; matrix products, arithmetic and copies ran while one was open for 5% of the time, Pallas kernels for 37%

profile of v2, /device:TPU:0, one launch (start us, length us, event | category | flops | bytes accessed | tf_op | source)
XLA Modules:
  0.0 708.4 jit_solution(15382432814264770126)
XLA Ops:
  26.9 8.2 %collective-permute-done.5.rest_2_.rest_6_ = bf16[512,768]{1,0:T(8,128)(2,1)} collective-permute-done((bf16[512,768]{1,0:T(8,128)(2,1)}, bf16[512,768]{1,0:T(8,128)(2,1)}, u32[]{:S(2)}, u32[]{:S(2)}) %collective-permute-start.5) | collective-permute-done | bytes 786464 | tf_op jit(solution)/shard_map/ppermute | solution.py:39
  70.1 10.8 %project_qkv.2 = (bf16[1024,256]{1,0:T(8,128)(2,1)S(1)}, bf16[1024,512]{1,0:T(8,128)(2,1)}) custom-call(s32[25]{0:T(128)S(1)} %concatenate.43.table_ref, bf16[8,512,512]{2,1,0:T(8,128)(2,1)S(1)} %fusion.3.g_ref, bf16[512,768]{1,0:T(8,128)(2,1)} %join_weights.5.rest_0_.rest_2_, bf16[512,768]{1,0:T(8,128)(2,1)} %collective-permute-done.4.rest_1_.rest_4_, ...), custom_call_target="tpu_custom_call" | custom-call | flops 1 | bytes 1 | tf_op jit(solution)/shard_map/project_qkv/pallas_call | solution.py:140
  83.0 11.3 %attend_own.2 = (bf16[1024,256]{1,0:T(8,128)(2,1)}, f32[1024,256]{1,0:T(8,128)S(1)}, f32[4,1024]{1,0:T(4,128)S(1)}) custom-call(s32[2]{0:T(128)S(1)} %get-tuple-element.1383.begin_ref, bf16[1024,256]{1,0:T(8,128)(2,1)S(1)} %get-tuple-element.1384.q_ref, bf16[1024,512]{1,0:T(8,128)(2,1)} %get-tuple-element.1385.kv_ref, s32[1,1024]{1,0:T(1,128)S(1)} %bitcast.77), custom_call_target="tpu_custom_call" | custom-call | flops 1 | bytes 1 | tf_op jit(solution)/shard_map/attend_own/pallas_call | solution.py:140
  94.4 18.7 %collective-permute-done.14.kv_ref = bf16[1024,512]{1,0:T(8,128)(2,1)} collective-permute-done((bf16[1024,512]{1,0:T(8,128)(2,1)}, bf16[1024,512]{1,0:T(8,128)(2,1)}, u32[]{:S(2)}, u32[]{:S(2)}) %collective-permute-start.14) | collective-permute-done | bytes 1048608 | tf_op jit(solution)/shard_map/ppermute | solution.py:39
  115.6 9.8 %attend_far.2 = (bf16[1024,256]{1,0:T(8,128)(2,1)S(1)}, f32[1024,256]{1,0:T(8,128)S(1)}, f32[4,1024]{1,0:T(4,128)S(1)}) custom-call(s32[2]{0:T(128)S(1)} %get-tuple-element.1371.begin_ref, bf16[1024,256]{1,0:T(8,128)(2,1)S(1)} %get-tuple-element.1384.q_ref, bf16[1024,512]{1,0:T(8,128)(2,1)} %collective-permute-done.14.kv_ref, s32[1,1024]{1,0:T(1,128)S(1)} %bitcast.78, ...), custom_call_target="tpu_custom_call" | custom-call | flops 1 | bytes 1 | tf_op jit(solution)/shard_map/attend_far/pallas_call | solution.py:140
  146.3 9.7 %project_up.2 = (bf16[1024,1024]{1,0:T(8,128)(2,1)S(1)}, bf16[1024,1024]{1,0:T(8,128)(2,1)S(1)}) custom-call(s32[25]{0:T(128)S(1)} %concatenate.43.table_ref, bf16[8,512,512]{2,1,0:T(8,128)(2,1)S(1)} %copy-done.1, bf16[512,1024]{1,0:T(8,128)(2,1)} %join_weights.6.rest_0_.rest_3_, bf16[512,1024]{1,0:T(8,128)(2,1)} %collective-permute-done.6.rest_1_.rest_5_, ...), custom_call_target="tpu_custom_call" | custom-call | flops 1 | bytes 1 | tf_op jit(solution)/shard_map/project_up/pallas_call | solution.py:140
  157.3 7.9 %project_out.2 = (bf16[128,2048]{1,0:T(8,128)(2,1)S(1)}, bf16[128,2048]{1,0:T(8,128)(2,1)S(1)}, bf16[128,2048]{1,0:T(8,128)(2,1)S(1)}, bf16[128,2048]{1,0:T(8,128)(2,1)S(1)}, bf16[512,2048]{1,0:T(8,128)(2,1)S(1)}) custom-call(s32[25]{0:T(128)S(1)} %concatenate.43.table_ref, bf16[1024,256]{1,0:T(8,128)(2,1)S(1)} %copy-done.61, ...), custom_call_target="tpu_custom_call" | custom-call | flops 1 | bytes 1 | tf_op jit(solution)/shard_map/project_out/pallas_call | solution.py:140
  173.4 40.7 %collective-permute-done.27.rest_1_.rest_3_ = bf16[512,1792]{1,0:T(8,128)(2,1)S(1)} collective-permute-done((bf16[512,1792]{1,0:T(8,128)(2,1)S(1)}, bf16[512,1792]{1,0:T(8,128)(2,1)S(1)}, u32[]{:S(2)}, u32[]{:S(2)}) %collective-permute-start.27) | collective-permute-done | bytes 1835040 | tf_op jit(solution)/shard_map/ppermute | solution.py:39
  231.0 26.5 %collective-permute-done.32.rest_3_.rest_5_ = bf16[1280,512]{1,0:T(8,128)(2,1)S(1)} collective-permute-done((bf16[1280,512]{1,0:T(8,128)(2,1)}, bf16[1280,512]{1,0:T(8,128)(2,1)S(1)}, u32[]{:S(2)}, u32[]{:S(2)}) %collective-permute-start.32) | collective-permute-done | bytes 1310752 | tf_op jit(solution)/shard_map/ppermute | solution.py:39
  261.1 11.6 %branch_grads.2 = (bf16[1024,256]{1,0:T(8,128)(2,1)S(1)}, bf16[1024,1024]{1,0:T(8,128)(2,1)S(1)}) custom-call(s32[25]{0:T(128)S(1)} %concatenate.43.table_ref, bf16[8,512,512]{2,1,0:T(8,128)(2,1)S(1)} %bitcast.69, bf16[1280,512]{1,0:T(8,128)(2,1)S(1)} %copy-done.41, bf16[1280,512]{1,0:T(8,128)(2,1)} %collective-permute-done.22.rest_1_.rest_3_, ...), custom_call_target="tpu_custom_call" | custom-call | flops 1 | bytes 1 | tf_op jit(solution)/shard_map/branch_grads/pallas_call | solution.py:140
  280.7 9.5 %project_qkv.3 = (bf16[1024,256]{1,0:T(8,128)(2,1)S(1)}, bf16[1024,512]{1,0:T(8,128)(2,1)S(1)}) custom-call(s32[25]{0:T(128)S(1)} %concatenate.43.table_ref, bf16[8,512,512]{2,1,0:T(8,128)(2,1)} %bitcast.63, bf16[512,1792]{1,0:T(8,128)(2,1)S(1)} %join_weights.8.rest_0_.rest_2_, bf16[512,1792]{1,0:T(8,128)(2,1)S(1)} %copy-done.28, ...), custom_call_target="tpu_custom_call" | custom-call | flops 1 | bytes 1 | tf_op jit(solution)/shard_map/project_qkv/pallas_call | solution.py:140
  291.8 10.2 %project_up.3 = (bf16[1024,1024]{1,0:T(8,128)(2,1)S(1)}, bf16[1024,1024]{1,0:T(8,128)(2,1)S(1)}) custom-call(s32[25]{0:T(128)S(1)} %concatenate.43.table_ref, bf16[8,512,512]{2,1,0:T(8,128)(2,1)} %bitcast.64, bf16[512,1792]{1,0:T(8,128)(2,1)S(1)} %join_weights.8.rest_0_.rest_2_, bf16[512,1792]{1,0:T(8,128)(2,1)S(1)} %copy-done.29, ...), custom_call_target="tpu_custom_call" | custom-call | flops 1 | bytes 1 | tf_op jit(solution)/shard_map/project_up/pallas_call | solution.py:140
  302.1 9.5 %attend_own.3 = (bf16[1024,256]{1,0:T(8,128)(2,1)}, f32[1024,256]{1,0:T(8,128)S(1)}, f32[4,1024]{1,0:T(4,128)S(1)}) custom-call(s32[2]{0:T(128)S(1)} %get-tuple-element.1383.begin_ref, bf16[1024,256]{1,0:T(8,128)(2,1)S(1)} %get-tuple-element.1179.q_ref, bf16[1024,512]{1,0:T(8,128)(2,1)S(1)} %get-tuple-element.1180.kv_ref, s32[1,1024]{1,0:T(1,128)S(1)} %bitcast.79), custom_call_target="tpu_custom_call" | custom-call | flops 1 | bytes 1 | tf_op jit(solution)/shard_map/attend_own/pallas_call | solution.py:140
  324.3 8.6 %attend_far.3 = (bf16[1024,256]{1,0:T(8,128)(2,1)S(1)}, f32[1024,256]{1,0:T(8,128)S(1)}, f32[4,1024]{1,0:T(4,128)S(1)}) custom-call(s32[2]{0:T(128)S(1)} %get-tuple-element.1371.begin_ref, bf16[1024,256]{1,0:T(8,128)(2,1)S(1)} %get-tuple-element.1179.q_ref, bf16[1024,512]{1,0:T(8,128)(2,1)S(1)} %copy-done.71, s32[1,1024]{1,0:T(1,128)S(1)} %bitcast.80, ...), custom_call_target="tpu_custom_call" | custom-call | flops 1 | bytes 1 | tf_op jit(solution)/shard_map/attend_far/pallas_call | solution.py:140
  332.9 13.7 %attend_backward.4 = (f32[1024,256]{1,0:T(8,128)S(1)}, bf16[1024,512]{1,0:T(8,128)(2,1)}) custom-call(s32[2]{0:T(128)S(1)} %get-tuple-element.1371.begin_ref, bf16[1024,256]{1,0:T(8,128)(2,1)S(1)} %get-tuple-element.1179.q_ref, bf16[1024,512]{1,0:T(8,128)(2,1)S(1)} %copy-done.72, s32[1,1024]{1,0:T(1,128)S(1)} %bitcast.81, ...), custom_call_target="tpu_custom_call" | custom-call | flops 1 | bytes 1 | tf_op jit(solution)/shard_map/attend_backward/pallas_call | solution.py:140
  348.1 9.1 %attend_backward.5 = (f32[1024,256]{1,0:T(8,128)S(1)}, f32[1024,512]{1,0:T(8,128)S(1)}) custom-call(s32[2]{0:T(128)S(1)} %get-tuple-element.1383.begin_ref, bf16[1024,256]{1,0:T(8,128)(2,1)S(1)} %get-tuple-element.1179.q_ref, bf16[1024,512]{1,0:T(8,128)(2,1)S(1)} %get-tuple-element.1180.kv_ref, s32[1,1024]{1,0:T(1,128)S(1)} %bitcast.82, ...), custom_call_target="tpu_custom_call" | custom-call | flops 1 | bytes 1 | tf_op jit(solution)/shard_map/attend_backward/pallas_call | solution.py:140
  363.0 7.8 %collective-permute-done.34.rest_0_ = bf16[1024,512]{1,0:T(8,128)(2,1)S(1)} collective-permute-done((bf16[1024,512]{1,0:T(8,128)(2,1)}, bf16[1024,512]{1,0:T(8,128)(2,1)S(1)}, u32[]{:S(2)}, u32[]{:S(2)}) %collective-permute-start.34) | collective-permute-done | bytes 1048608 | tf_op jit(solution)/shard_map/ppermute | solution.py:39
  373.0 10.8 %feature_grads.2 = (bf16[128,2048]{1,0:T(8,128)(2,1)S(1)}, bf16[128,2048]{1,0:T(8,128)(2,1)S(1)}, bf16[128,2048]{1,0:T(8,128)(2,1)S(1)}, bf16[128,2048]{1,0:T(8,128)(2,1)S(1)}, bf16[512,2048]{1,0:T(8,128)(2,1)S(1)}) custom-call(s32[25]{0:T(128)S(1)} %concatenate.43.table_ref, bf16[1024,768]{1,0:T(8,128)(2,1)S(1)} %get-tuple-element.1300.right_ref.rest_0_, ...), custom_call_target="tpu_custom_call" | custom-call | flops 1 | bytes 1 | tf_op jit(solution)/shard_map/feature_grads/pallas_call | solution.py:140
  406.8 14.9 %collective-permute-done.36.rest_3_ = bf16[1280,512]{1,0:T(8,128)(2,1)S(1)} collective-permute-done((bf16[1280,512]{1,0:T(8,128)(2,1)}, bf16[1280,512]{1,0:T(8,128)(2,1)S(1)}, u32[]{:S(2)}, u32[]{:S(2)}) %collective-permute-start.36) | collective-permute-done | bytes 1310752 | tf_op jit(solution)/shard_map/ppermute | solution.py:39
  424.5 7.6 %reduce-scatter.7.cloned.1.call-done = bf16[512,512]{1,0:T(8,128)(2,1)} async-done(((bf16[512,2048]{1,0:T(8,128)(2,1)}), bf16[512,512]{1,0:T(8,128)(2,1)}) %reduce-scatter.7.cloned.1.call-update) | async-done | bytes 524304 | tf_op jit(solution)/shard_map/reduce_scatter | solution.py:1405
  446.5 6.7 collective-permute-done.37.rest_2_
  461.8 7.1 grad_out.5
  477.5 7.9 %project_out.3 = (bf16[128,2048]{1,0:T(8,128)(2,1)S(1)}, bf16[128,2048]{1,0:T(8,128)(2,1)S(1)}, bf16[128,2048]{1,0:T(8,128)(2,1)S(1)}, bf16[128,2048]{1,0:T(8,128)(2,1)S(1)}, bf16[512,2048]{1,0:T(8,128)(2,1)S(1)}) custom-call(s32[25]{0:T(128)S(1)} %concatenate.43.table_ref, bf16[1024,256]{1,0:T(8,128)(2,1)S(1)} %copy-done.65, ...), custom_call_target="tpu_custom_call" | custom-call | flops 1 | bytes 1 | tf_op jit(solution)/shard_map/project_out/pallas_call | solution.py:140
  499.1 6.7 collective-permute-done.46.refs_0_.refs_1_
  510.1 11.3 %branch_grads.3 = (bf16[1024,256]{1,0:T(8,128)(2,1)S(1)}, bf16[1024,1024]{1,0:T(8,128)(2,1)S(1)}) custom-call(s32[25]{0:T(128)S(1)} %concatenate.43.table_ref, bf16[8,512,512]{2,1,0:T(8,128)(2,1)S(1)} %bitcast.72, bf16[1280,512]{1,0:T(8,128)(2,1)S(1)} %copy-done.45, bf16[1280,512]{1,0:T(8,128)(2,1)} %collective-permute-done.13.rest_3_.rest_1_, ...), custom_call_target="tpu_custom_call" | custom-call | flops 1 | bytes 1 | tf_op jit(solution)/shard_map/branch_grads/pallas_call | solution.py:140
  521.5 14.1 %attend_backward.6 = (f32[1024,256]{1,0:T(8,128)S(1)}, bf16[1024,512]{1,0:T(8,128)(2,1)S(1)}) custom-call(s32[2]{0:T(128)S(1)} %get-tuple-element.1371.begin_ref, bf16[1024,256]{1,0:T(8,128)(2,1)S(1)} %copy-done.55, bf16[1024,512]{1,0:T(8,128)(2,1)} %collective-permute-done.14.kv_ref, s32[1,1024]{1,0:T(1,128)S(1)} %bitcast.83, f32[1024,256]{1,0:T(8,128)S(1)} %copy-done.67, ...), custom_call_target="tpu_custom_call" | custom-call | flops 1 | bytes 1 | tf_op jit(solution)/shard_map/attend_backward/pallas_call | solution.py:140
  541.6 10.1 %attend_backward.7 = (f32[1024,256]{1,0:T(8,128)S(1)}, f32[1024,512]{1,0:T(8,128)S(1)}) custom-call(s32[2]{0:T(128)S(1)} %get-tuple-element.1383.begin_ref, bf16[1024,256]{1,0:T(8,128)(2,1)S(1)} %copy-done.55, bf16[1024,512]{1,0:T(8,128)(2,1)} %get-tuple-element.1385.kv_ref, s32[1,1024]{1,0:T(1,128)S(1)} %bitcast.84, f32[1024,256]{1,0:T(8,128)S(1)} %copy-done.67, ...), custom_call_target="tpu_custom_call" | custom-call | flops 1 | bytes 1 | tf_op jit(solution)/shard_map/attend_backward/pallas_call | solution.py:140
  557.8 7.0 collective-permute-done.52.rest_0_
  569.4 12.8 %feature_grads.3 = (bf16[128,2048]{1,0:T(8,128)(2,1)S(1)}, bf16[128,2048]{1,0:T(8,128)(2,1)S(1)}, bf16[128,2048]{1,0:T(8,128)(2,1)S(1)}, bf16[128,2048]{1,0:T(8,128)(2,1)S(1)}, bf16[512,2048]{1,0:T(8,128)(2,1)S(1)}) custom-call(s32[25]{0:T(128)S(1)} %concatenate.43.table_ref, bf16[1024,768]{1,0:T(8,128)(2,1)S(1)} %get-tuple-element.1533.right_ref.rest_0_, ...), custom_call_target="tpu_custom_call" | custom-call | flops 1 | bytes 1 | tf_op jit(solution)/shard_map/feature_grads/pallas_call | solution.py:140
  587.8 6.0 collective-permute-done.54.rest_3_
  641.4 6.7 grad_out.7
  682.6 7.5 %collective-permute-done.69 = f32[2,5120]{1,0:T(2,128)S(1)} collective-permute-done((f32[2,5120]{1,0:T(2,128)S(1)}, f32[2,5120]{1,0:T(2,128)S(1)}, u32[]{:S(2)}, u32[]{:S(2)}) %collective-permute-start.69) | collective-permute-done | bytes 40992 | tf_op jit(solution)/shard_map/ppermute | solution.py:89
  (551 shorter events, 331.4 us)
Async XLA Ops:
  7.2 55.8 %all-gather.11.cloned.1.call-start = ((), (), s32[]{:S(2)}) async-start(), calls=%async_computation.9 | async-start | bytes 4718592 | tf_op jit(solution)/shard_map/all_gather | solution.py:1402
  7.9 126.4 %all-gather.9.cloned.1.call-start = ((), (), s32[]{:S(2)}) async-start(), calls=%async_computation.8 | async-start | bytes 4718592 | tf_op jit(solution)/shard_map/all_gather | solution.py:1402
  13.9 202.7 %reduce-scatter.5.cloned.1.call-start = ((), (), s32[]{:S(2)}) async-start(), calls=%async_computation.4 | async-start | bytes 2621440 | tf_op jit(solution)/shard_map/reduce_scatter | solution.py:1405
  60.9 52.2 %collective-permute-start.12 = (bf16[1280,512]{1,0:T(8,128)(2,1)S(1)}, bf16[1280,512]{1,0:T(8,128)(2,1)}, u32[]{:S(2)}, u32[]{:S(2)}) collective-permute-start(bf16[1280,512]{1,0:T(8,128)(2,1)S(1)} %join_weights.7.rest_2_.rest_0_), channel_id=1, source_target_pairs={{0,16},{16,0},{1,17},{17,1},{2,18},{18,2},{3,19},{19,3},{4,20},{20... | collective-permute-start | bytes 3932168 | tf_op jit(solution)/shard_map/ppermute | solution.py:39
  61.9 51.1 %collective-permute-start.13 = (bf16[1280,512]{1,0:T(8,128)(2,1)S(1)}, bf16[1280,512]{1,0:T(8,128)(2,1)}, u32[]{:S(2)}, u32[]{:S(2)}) collective-permute-start(bf16[1280,512]{1,0:T(8,128)(2,1)S(1)} %join_weights.7.rest_2_.rest_0_), channel_id=1, source_target_pairs={{0,8},{8,0},{1,9},{9,1},{2,10},{10,2},{3,11},{11,3},{4,12},{12,4},... | collective-permute-start | bytes 3932168 | tf_op jit(solution)/shard_map/ppermute | solution.py:39
  81.0 32.0 %collective-permute-start.14 = (bf16[1024,512]{1,0:T(8,128)(2,1)}, bf16[1024,512]{1,0:T(8,128)(2,1)}, u32[]{:S(2)}, u32[]{:S(2)}) collective-permute-start(bf16[1024,512]{1,0:T(8,128)(2,1)} %get-tuple-element.1385.kv_ref), channel_id=1, source_target_pairs={{0,8},{8,0},{1,9},{9,1},{2,10},{10,2},{3,11},{11,3},{4,12},{12,4},... | collective-permute-start | bytes 3145736 | tf_op jit(solution)/shard_map/ppermute | solution.py:39
  82.0 31.1 %collective-permute-start.11 = (bf16[512,1024]{1,0:T(8,128)(2,1)}, bf16[512,1024]{1,0:T(8,128)(2,1)}, u32[]{:S(2)}, u32[]{:S(2)}) collective-permute-start(bf16[512,1024]{1,0:T(8,128)(2,1)} %join_weights.6.rest_0_.rest_3_), channel_id=1, source_target_pairs={{0,16},{16,0},{1,17},{17,1},{2,18},{18,2},{3,19},{19,3},{4,20},{20... | collective-permute-start | bytes 3145736 | tf_op jit(solution)/shard_map/ppermute | solution.py:39
  113.0 28.3 %collective-permute-start.16 = (bf16[1280,512]{1,0:T(8,128)(2,1)}, bf16[1280,512]{1,0:T(8,128)(2,1)}, u32[]{:S(2)}, u32[]{:S(2)}) collective-permute-start(bf16[1280,512]{1,0:T(8,128)(2,1)} %collective-permute-done.12.rest_4_.rest_2_), channel_id=1, source_target_pairs={{0,8},{8,0},{1,9},{9,1},{2,10},{10,2},{3,11},{11,3},{4,12},{12,4},... | collective-permute-start | bytes 3932168 | tf_op jit(solution)/shard_map/ppermute | solution.py:39
  141.3 30.6 %collective-permute-start.21 = (bf16[1280,512]{1,0:T(8,128)(2,1)}, bf16[1280,512]{1,0:T(8,128)(2,1)}, u32[]{:S(2)}, u32[]{:S(2)}) collective-permute-start(bf16[1280,512]{1,0:T(8,128)(2,1)} %copy-done.40), channel_id=1, source_target_pairs={{0,16},{16,0},{1,17},{17,1},{2,18},{18,2},{3,19},{19,3},{4,20},{20... | collective-permute-start | bytes 3932168 | tf_op jit(solution)/shard_map/ppermute | solution.py:39
  142.3 29.6 %collective-permute-start.22 = (bf16[1280,512]{1,0:T(8,128)(2,1)}, bf16[1280,512]{1,0:T(8,128)(2,1)}, u32[]{:S(2)}, u32[]{:S(2)}) collective-permute-start(bf16[1280,512]{1,0:T(8,128)(2,1)} %copy-done.40), channel_id=1, source_target_pairs={{0,8},{8,0},{1,9},{9,1},{2,10},{10,2},{3,11},{11,3},{4,12},{12,4},... | collective-permute-start | bytes 3932168 | tf_op jit(solution)/shard_map/ppermute | solution.py:39
  171.9 104.2 %all-gather.13.cloned.1.call-start = ((), (), s32[]{:S(2)}) async-start(), calls=%async_computation.10 | async-start | bytes 4718592 | tf_op jit(solution)/shard_map/all_gather | solution.py:1402
  172.0 42.1 %collective-permute-start.27 = (bf16[512,1792]{1,0:T(8,128)(2,1)S(1)}, bf16[512,1792]{1,0:T(8,128)(2,1)S(1)}, u32[]{:S(2)}, u32[]{:S(2)}) collective-permute-start(bf16[512,1792]{1,0:T(8,128)(2,1)S(1)} %join_weights.8.rest_0_.rest_2_), channel_id=1, source_target_pairs={{0,8},{8,0},{1,9},{9,1},{2,10},{10,2},{3,11},{11,3},{4,12},{12,4},... | collective-permute-start | bytes 5505032 | tf_op jit(solution)/shard_map/ppermute | solution.py:39
  172.4 43.0 %collective-permute-start.28 = (bf16[512,1792]{1,0:T(8,128)(2,1)S(1)}, bf16[512,1792]{1,0:T(8,128)(2,1)S(1)}, u32[]{:S(2)}, u32[]{:S(2)}) collective-permute-start(bf16[512,1792]{1,0:T(8,128)(2,1)S(1)} %join_weights.8.rest_0_.rest_2_), channel_id=1, source_target_pairs={{0,16},{16,0},{1,17},{17,1},{2,18},{18,2},{3,19},{19,3},{4,20},{20... | collective-permute-start | bytes 5505032 | tf_op jit(solution)/shard_map/ppermute | solution.py:39
  229.2 202.9 %reduce-scatter.7.cloned.1.call-start = ((), (), s32[]{:S(2)}) async-start(), calls=%async_computation.5 | async-start | bytes 2621440 | tf_op jit(solution)/shard_map/reduce_scatter | solution.py:1405
  229.3 45.6 %collective-permute-start.31 = (bf16[512,1792]{1,0:T(8,128)(2,1)}, bf16[512,1792]{1,0:T(8,128)(2,1)S(1)}, u32[]{:S(2)}, u32[]{:S(2)}) collective-permute-start(bf16[512,1792]{1,0:T(8,128)(2,1)} %copy-done.27), channel_id=1, source_target_pairs={{0,16},{16,0},{1,17},{17,1},{2,18},{18,2},{3,19},{19,3},{4,20},{20... | collective-permute-start | bytes 5505032 | tf_op jit(solution)/shard_map/ppermute | solution.py:39
  229.6 28.0 %collective-permute-start.32 = (bf16[1280,512]{1,0:T(8,128)(2,1)}, bf16[1280,512]{1,0:T(8,128)(2,1)S(1)}, u32[]{:S(2)}, u32[]{:S(2)}) collective-permute-start(bf16[1280,512]{1,0:T(8,128)(2,1)} %collective-permute-done.21.rest_2_.rest_4_), channel_id=1, source_target_pairs={{0,8},{8,0},{1,9},{9,1},{2,10},{10,2},{3,11},{11,3},{4,12},{12,4},... | collective-permute-start | bytes 3932168 | tf_op jit(solution)/shard_map/ppermute | solution.py:39
  290.2 25.1 %collective-permute-start.33 = (bf16[1024,512]{1,0:T(8,128)(2,1)S(1)}, bf16[1024,512]{1,0:T(8,128)(2,1)S(1)}, u32[]{:S(2)}, u32[]{:S(2)}) collective-permute-start(bf16[1024,512]{1,0:T(8,128)(2,1)S(1)} %get-tuple-element.1180.kv_ref), channel_id=1, source_target_pairs={{0,8},{8,0},{1,9},{9,1},{2,10},{10,2},{3,11},{11,3},{4,12},{12,4},... | collective-permute-start | bytes 3145736 | tf_op jit(solution)/shard_map/ppermute | solution.py:39
  320.3 50.5 %collective-permute-start.35 = (bf16[1024,1024]{1,0:T(8,128)(2,1)}, bf16[1024,1024]{1,0:T(8,128)(2,1)}, u32[]{:S(2)}, u32[]{:S(2)}) collective-permute-start(bf16[1024,1024]{1,0:T(8,128)(2,1)} %grad_in.8), channel_id=1, source_target_pairs={{0,16},{16,0},{1,17},{17,1},{2,18},{18,2},{3,19},{19,3},{4,20},{20... | collective-permute-start | bytes 6291464 | tf_op jit(solution)/shard_map/ppermute | solution.py:39
  390.6 115.2 %all-gather.15.cloned.1.call-start = ((), (), s32[]{:S(2)}) async-start(), calls=%async_computation.11 | async-start | bytes 4718592 | tf_op jit(solution)/shard_map/all_gather | solution.py:1402
  390.6 31.1 %collective-permute-start.36 = (bf16[1280,512]{1,0:T(8,128)(2,1)}, bf16[1280,512]{1,0:T(8,128)(2,1)S(1)}, u32[]{:S(2)}, u32[]{:S(2)}) collective-permute-start(bf16[1280,512]{1,0:T(8,128)(2,1)} %copy-done.109), channel_id=1, source_target_pairs={{0,8},{8,0},{1,9},{9,1},{2,10},{10,2},{3,11},{11,3},{4,12},{12,4},... | collective-permute-start | bytes 3932168 | tf_op jit(solution)/shard_map/ppermute | solution.py:39
  398.8 47.7 %collective-permute-start.38 = (bf16[1024,768]{1,0:T(8,128)(2,1)}, bf16[1024,768]{1,0:T(8,128)(2,1)}, u32[]{:S(2)}, u32[]{:S(2)}) collective-permute-start(bf16[1024,768]{1,0:T(8,128)(2,1)} %grad_in.9), channel_id=1, source_target_pairs={{0,16},{16,0},{1,17},{17,1},{2,18},{18,2},{3,19},{19,3},{4,20},{20... | collective-permute-start | bytes 4718600 | tf_op jit(solution)/shard_map/ppermute | solution.py:39
  422.8 30.4 %collective-permute-start.37 = (bf16[1280,512]{1,0:T(8,128)(2,1)}, bf16[1280,512]{1,0:T(8,128)(2,1)}, u32[]{:S(2)}, u32[]{:S(2)}) collective-permute-start(bf16[1280,512]{1,0:T(8,128)(2,1)} %get-tuple-element.1203), channel_id=1, source_target_pairs={{0,8},{8,0},{1,9},{9,1},{2,10},{10,2},{3,11},{11,3},{4,12},{12,4},... | collective-permute-start | bytes 3932168 | tf_op jit(solution)/shard_map/ppermute | solution.py:39
  453.2 181.7 %reduce-scatter.9.cloned.1.call-start = ((), (), s32[]{:S(2)}) async-start(), calls=%async_computation.6 | async-start | bytes 2621440 | tf_op jit(solution)/shard_map/reduce_scatter | solution.py:1405
  470.0 29.1 %collective-permute-start.47 = (bf16[1280,512]{1,0:T(8,128)(2,1)}, bf16[1280,512]{1,0:T(8,128)(2,1)}, u32[]{:S(2)}, u32[]{:S(2)}) collective-permute-start(bf16[1280,512]{1,0:T(8,128)(2,1)} %get-tuple-element.1298), channel_id=1, source_target_pairs={{0,16},{16,0},{1,17},{17,1},{2,18},{18,2},{3,19},{19,3},{4,20},{20... | collective-permute-start | bytes 3932168 | tf_op jit(solution)/shard_map/ppermute | solution.py:39
  505.8 144.4 %reduce-scatter.11.cloned.1.call-start = ((), (), s32[]{:S(2)}) async-start(), calls=%async_computation.7 | async-start | bytes 2621440 | tf_op jit(solution)/shard_map/reduce_scatter | solution.py:1405
  539.5 47.0 %collective-permute-start.53 = (bf16[1024,1024]{1,0:T(8,128)(2,1)S(1)}, bf16[1024,1024]{1,0:T(8,128)(2,1)S(1)}, u32[]{:S(2)}, u32[]{:S(2)}) collective-permute-start(bf16[1024,1024]{1,0:T(8,128)(2,1)S(1)} %grad_in.12), channel_id=1, source_target_pairs={{0,16},{16,0},{1,17},{17,1},{2,18},{18,2},{3,19},{19,3},{4,20},{20... | collective-permute-start | bytes 6291464 | tf_op jit(solution)/shard_map/ppermute | solution.py:39
  540.3 24.5 %collective-permute-start.52 = (bf16[1024,512]{1,0:T(8,128)(2,1)S(1)}, bf16[1024,512]{1,0:T(8,128)(2,1)}, u32[]{:S(2)}, u32[]{:S(2)}) collective-permute-start(bf16[1024,512]{1,0:T(8,128)(2,1)S(1)} %get-tuple-element.1377), channel_id=1, source_target_pairs={{0,8},{8,0},{1,9},{9,1},{2,10},{10,2},{3,11},{11,3},{4,12},{12,4},... | collective-permute-start | bytes 3145736 | tf_op jit(solution)/shard_map/ppermute | solution.py:39
  564.8 29.1 %collective-permute-start.54 = (bf16[1280,512]{1,0:T(8,128)(2,1)S(1)}, bf16[1280,512]{1,0:T(8,128)(2,1)S(1)}, u32[]{:S(2)}, u32[]{:S(2)}) collective-permute-start(bf16[1280,512]{1,0:T(8,128)(2,1)S(1)} %get-tuple-element.1407), channel_id=1, source_target_pairs={{0,8},{8,0},{1,9},{9,1},{2,10},{10,2},{3,11},{11,3},{4,12},{12,4},... | collective-permute-start | bytes 3932168 | tf_op jit(solution)/shard_map/ppermute | solution.py:39
  603.6 45.6 %collective-permute-start.63 = (bf16[1024,768]{1,0:T(8,128)(2,1)}, bf16[1024,768]{1,0:T(8,128)(2,1)}, u32[]{:S(2)}, u32[]{:S(2)}) collective-permute-start(bf16[1024,768]{1,0:T(8,128)(2,1)} %grad_in.13), channel_id=1, source_target_pairs={{0,16},{16,0},{1,17},{17,1},{2,18},{18,2},{3,19},{19,3},{4,20},{20... | collective-permute-start | bytes 4718600 | tf_op jit(solution)/shard_map/ppermute | solution.py:39
  604.6 33.0 %collective-permute-start.59 = (bf16[1280,512]{1,0:T(8,128)(2,1)}, bf16[1280,512]{1,0:T(8,128)(2,1)}, u32[]{:S(2)}, u32[]{:S(2)}) collective-permute-start(bf16[1280,512]{1,0:T(8,128)(2,1)} %get-tuple-element.1461), channel_id=1, source_target_pairs={{0,8},{8,0},{1,9},{9,1},{2,10},{10,2},{3,11},{11,3},{4,12},{12,4},... | collective-permute-start | bytes 3932168 | tf_op jit(solution)/shard_map/ppermute | solution.py:39
  637.6 31.5 %collective-permute-start.66 = (bf16[512,1024]{1,0:T(8,128)(2,1)}, bf16[512,1024]{1,0:T(8,128)(2,1)}, u32[]{:S(2)}, u32[]{:S(2)}) collective-permute-start(bf16[512,1024]{1,0:T(8,128)(2,1)} %copy-done.110), channel_id=1, source_target_pairs={{0,8},{8,0},{1,9},{9,1},{2,10},{10,2},{3,11},{11,3},{4,12},{12,4},... | collective-permute-start | bytes 3145736 | tf_op jit(solution)/shard_map/ppermute | solution.py:39
  649.2 30.8 %collective-permute-start.70 = (bf16[1280,512]{1,0:T(8,128)(2,1)}, bf16[1280,512]{1,0:T(8,128)(2,1)S(1)}, u32[]{:S(2)}, u32[]{:S(2)}) collective-permute-start(bf16[1280,512]{1,0:T(8,128)(2,1)} %get-tuple-element.1520), channel_id=1, source_target_pairs={{0,16},{16,0},{1,17},{17,1},{2,18},{18,2},{3,19},{19,3},{4,20},{20... | collective-permute-start | bytes 3932168 | tf_op jit(solution)/shard_map/ppermute | solution.py:39
  (177 other events, 1322.9 us)
Sparse Core Ops, SparseCore 0:
  9.6 50.0 all-gather.10
  61.4 46.1 all-gather.8
  172.1 43.2 reduce-scatter.4
  229.3 46.5 all-gather.12
  390.7 41.3 reduce-scatter.6
  453.4 44.6 all-gather.14
  506.0 41.3 reduce-scatter.8
  597.6 41.7 reduce-scatter.10

commit v3 on v2

--- a/solution.py
+++ b/solution.py
@@ -16,7 +16,7 @@
 LANES = 128
 HEADS_TILE = LANES // HEAD_DIM
 MEBI = 1024 * 1024
-PIECES = 4
+PIECES = 2
 VMEM_MEBI = 40
 MORE_MEBI = 40
 F32 = jnp.float32
@@ -81,14 +81,7 @@
 
 
 def sum_over(value, axis):
-    size = lax.axis_size(axis)
-    if size & (size - 1):
-        return value + sum(shift(value, axis, k) for k in range(1, size))
-    step = 1
-    while step < size:
-        value = value + lax.ppermute(value, axis, [(i, i ^ step) for i in range(size)])
-        step *= 2
-    return value
+    return value + sum(shift(value, axis, k) for k in range(1, lax.axis_size(axis)))
 
 
 def width_table(layout):
@@ -438,79 +431,64 @@
     )
 
 
-def project_back(layout, table, lefts, weights, transposed, name):
+def project_back(layout, table, lefts, weights, transposed, away, name):
     rows, count = layout.own_tokens, len(weights)
     per_block = len(weights[0])
     sizes = [left.shape[1] for left in lefts]
     flat = [w for block in weights for w in block]
     n = len(lefts)
-    step = rows // PIECES
+    pieces = PIECES if away else 1
+    step = rows // pieces
 
     def body(table_ref, *rest):
         left_refs, rest = rest[:n], rest[n:]
         w_refs, rest = rest[: len(flat)], rest[len(flat) :]
-        out_refs, rest = rest[: PIECES + 1], rest[PIECES + 1 :]
+        out_refs, rest = rest[:pieces], rest[pieces:]
         left_bufs, rest = rest[:n], rest[n:]
-        w_bufs, (out_buf, sems, w_sems, out_sems) = rest[: len(flat)], rest[len(flat) :]
+        w_bufs, (sems, w_sems) = rest[: len(flat)], rest[len(flat) :]
         core = table_ref[2 * layout.places]
-        copies = []
-        for half, which in enumerate((lax.rem(core + 1, layout.n_c), core)):
-            begin = pl.multiple_of(which * rows, rows)
-            copies.append(
-                [
-                    pltpu.make_async_copy(
-                        ref.at[pl.ds(begin, rows), :], buf.at[half], sems.at[half, i]
-                    )
-                    for i, (ref, buf) in enumerate(zip(left_refs, left_bufs))
-                ]
-            )
+        begin = pl.multiple_of((lax.rem(core + 1, layout.n_c) if away else core) * rows, rows)
+        copies = [
+            pltpu.make_async_copy(ref.at[pl.ds(begin, rows), :], buf, sems.at[i])
+            for i, (ref, buf) in enumerate(zip(left_refs, left_bufs))
+        ]
         w_copies = [
             pltpu.make_async_copy(ref, buf, w_sems.at[i])
             for i, (ref, buf) in enumerate(zip(w_refs, w_bufs))
         ]
-        start_all(copies[0] + w_copies)
-        start_all(copies[1])
-        outs = []
-        for half in range(2):
-            wait_all(copies[half])
-            for b in range(count):
-                if half == 0:
-                    wait_all(w_copies[b * per_block : (b + 1) * per_block])
-                total = None
-                at = 0
-                for i, buf in enumerate(left_bufs):
-                    if per_block == 1:
-                        here = slice(at, at + sizes[i])
-                        w = w_bufs[b][:, here] if transposed else w_bufs[b][here, :]
-                        at += sizes[i]
-                    else:
-                        w = w_bufs[b * per_block + i][...]
-                    term = contract(buf[half], w, 1, 1 if transposed else 0)
-                    total = term if total is None else total + term
-                out_buf[half, :, b * layout.block : (b + 1) * layout.block] = total.astype(BF16)
-            pieces = [out_buf.at[0, i * step : (i + 1) * step] for i in range(PIECES)]
-            pieces = pieces if half == 0 else [out_buf.at[1]]
-            for piece in pieces:
-                at = len(outs)
-                outs.append(pltpu.make_async_copy(piece, out_refs[at], out_sems.at[at]))
-                outs[-1].start()
-        wait_all(outs)
-
-    out = [jax.ShapeDtypeStruct((size, layout.width), BF16) for size in [step] * PIECES + [rows]]
+        start_all(copies + w_copies)
+        wait_all(copies)
+        for b in range(count):
+            wait_all(w_copies[b * per_block : (b + 1) * per_block])
+            total = None
+            at = 0
+            for i, buf in enumerate(left_bufs):
+                if per_block == 1:
+                    here = slice(at, at + sizes[i])
+                    w = w_bufs[b][:, here] if transposed else w_bufs[b][here, :]
+                    at += sizes[i]
+                else:
+                    w = w_bufs[b * per_block + i][...]
+                term = contract(buf[...], w, 1, 1 if transposed else 0)
+                total = term if total is None else total + term
+            for i in range(pieces):
+                out_refs[i][:, b * layout.block : (b + 1) * layout.block] = total[
+                    i * step : (i + 1) * step
+                ].astype(BF16)
+
+    out = [jax.ShapeDtypeStruct((step, layout.width), BF16)] * pieces
     return kernel_call(
         body,
         table,
         [*lefts, *flat],
         [ANY] * n + [HBM] * len(flat),
         out,
-        [ANY] * (PIECES + 1),
-        [pltpu.VMEM((2, rows, size), BF16) for size in sizes]
+        [full(o) for o in out],
+        [pltpu.VMEM((rows, size), BF16) for size in sizes]
         + [pltpu.VMEM(w.shape, BF16) for w in flat]
         + [
-            pltpu.VMEM((2, rows, layout.width), BF16),
-            pltpu.SemaphoreType.DMA((2, n)),
+            pltpu.SemaphoreType.DMA((n,)),
             pltpu.SemaphoreType.DMA((len(flat),)),
-            pltpu.SemaphoreType.DMA((PIECES + 1,)),
         ],
         name,
         mebi=MORE_MEBI,
@@ -857,7 +835,7 @@
 def attend(begins, queries, key_values, starts, before=None):
     tokens, columns = queries.shape
     own = before is None
-    block_q = math.gcd(tokens, 256 if own else 512)
+    block_q = math.gcd(tokens, 512)
     heads, pairs = columns // HEAD_DIM, columns // LANES
     keys = key_values.shape[0]
     steps = tokens // block_q
@@ -1405,10 +1383,13 @@
         return lax.psum_scatter(order.after([summed])[0], Z, scatter_dimension=1, tiled=True)
 
     def to_owner(lefts, weights, transposed, name, awaited=()):
-        *away, own = order.run(
-            lambda *a: project_back(layout, table, a[0], a[1], transposed, name), lefts, weights
+        away = order.run(
+            lambda *a: project_back(layout, table, a[0], a[1], transposed, True, name), lefts, weights
         )
         received = [order.send(piece, C, 1, PIECES) for piece in away]
+        (own,) = order.run(
+            lambda *a: project_back(layout, table, a[0], a[1], transposed, False, name), lefts, weights
+        )
         if awaited:
             order.wait(*awaited)
         return order.run(lambda a, b: merge_cores(layout, table, a, b), own, received)
@@ -1618,7 +1599,7 @@
                 jnp.sum(normed_grad, axis=0),
                 to_both(k.qkv_sum.reshape(3, columns)),
                 jnp.sum(gradient, axis=0),
-                to_both(jnp.sum(k.up_low, axis=0, dtype=F32)),
+                to_both(k.up_sum),
             ]
         )
         return new
@@ -1641,33 +1622,44 @@
             branch = None
             if layer + 1 == last:
                 branch = scatter_features(out_summed)
+        out = ScatterOut(order, layout, table, [k.mixed_low, k.active], grad_features)
+        if layer < last:
+            out.compute()
+            out.begin(layout.n_y - 1, 1)
             grads_of_branch(k, grad_features, k.slope)
             k.up_low = k.hidden_grad
             up = scatter_in(k.up_low)
-        out = ScatterOut(order, layout, table, [k.mixed_low, k.active], grad_features)
         far_gradients(k)
         if layer < last:
             up.compute()
             up.begin()
         own_gradients(k)
-        out.compute()
         if layer < last:
-            arrived(*k.away_pairs)
-            out.begin(layout.n_y - 1, 1)
+            before.swap()
+            place(layer + 1, QKV, before)
+            arrived(*k.away_pairs, *out.received[-1])
+            for a in reversed(range(layout.n_y - 1)):
+                out.begin(a, 1)
         else:
+            out.compute()
             arrived(*k.away_pairs, *up.received)
         join_gradients(k)
+        (k.up_sum,) = order.wait(jnp.sum(order.after([k.up_low])[0], axis=0, dtype=F32))
         qkv = scatter_in(k.qkv_low)
-        awaited = [] if layer == last else [*up.received, *out.received[-1]]
+        if layer < last:
+            qkv.compute()
+        awaited = [] if layer == last else [*up.received, *out.all_received()]
         summed = feature_sum(k, *awaited)
         normed_grad = scatter_features(summed)
         order.wait(summed)
-        for a in reversed(range(layout.n_y - (layer < last))):
-            out.begin(a, 1)
-        qkv.compute()
-        qkv.begin()
-        up.middle()
         if layer == last:
+            for a in reversed(range(1, layout.n_y)):
+                out.begin(a, 1)
+            qkv.compute()
+            qkv.begin()
+            up.middle()
+            out_summed = branch_sum(k)
+            out.begin(0, 1)
             (normed_grad,) = order.wait(normed_grad)
             gradient = norm_backward(k, normed_grad, gradient)
             (low,) = order.wait(gradient.astype(BF16))
@@ -1679,39 +1671,46 @@
             out.finish(1)
             qkv.middle()
             qkv.finish(1)
-            out_summed = branch_sum(k)
-            arrived(*up.near, *qkv.near, *out.near)
+            arrived(*up.near)
+            up.swap()
+            place(layer, UP, up)
+            arrived(*out.near)
+            out.swap()
+            place(layer, OUT, out)
+            arrived(*qkv.near)
         else:
-            for scatter in before:
-                scatter.swap()
-            for group, scatter in zip((UP, QKV, OUT), before):
-                place(layer + 1, group, scatter)
+            qkv.begin()
+            up.middle()
+            up.finish(1)
             if branch is not None:
                 outputs[last] = add_branch(residual, branch, last)
                 (outputs[last],) = order.wait(outputs[last])
-            arrived(*out.all_received())
-            up.finish(1)
             out.middle()
+            arrived(*qkv.received)
             out.finish(1)
+            qkv.middle()
+            qkv.finish(1)
             (normed_grad,) = order.wait(normed_grad)
             gradient = norm_backward(k, normed_grad, gradient)
             (gradient,) = order.wait(gradient)
-            arrived(*qkv.received)
-            qkv.middle()
-            qkv.finish(1)
-        before = (up, qkv, out)
-
-    up, qkv, out = before
+            if layer > 0:
+                up.swap()
+                out.swap()
+                place(layer, UP, up)
+                place(layer, OUT, out)
+        before = qkv
+
     small = sum_over(jnp.stack(order.after(sums)), C)
+    arrived(*qkv.near, *up.near, *out.near)
+    (small,) = order.wait(small)
+    small = sum_over(small, X)
+    qkv.swap()
     up.swap()
+    out.swap()
     place(0, UP, up)
     (small,) = order.wait(small)
-    small = sum_over(small, X)
-    out.swap()
+    small = sum_over(small, Y)
     place(0, OUT, out)
-    (small,) = order.wait(small)
-    small = sum_over(small, Y)
-    qkv.swap()
     place(0, QKV, qkv)
 
     small, gradient, outputs = order.now((small, gradient, outputs))

time: 714 us -> 682 us (0.955)
  waiting for transfers between devices: 228 us -> 201 us
  Pallas kernels: 293 us -> 284 us
    ppermute x9 -> x0, waiting for transfers between devices: 27.3 us -> none  [sum_over(): lax.ppermute(value, axis, [(i, i ^ step) for i in range(size)])]
    ppermute x66 -> x70, starting transfers between devices: 51.5 us -> 63.8 us  [shift(): lax.ppermute(value, axis, [(i, (i + step) % size) for i in range(size)])]
    ppermute x9 -> x0, starting transfers between devices: 9.26 us -> none  [sum_over(): lax.ppermute(value, axis, [(i, i ^ step) for i in range(size)])]
    pallas_call x58 -> x62, Pallas kernels: 293 us -> 284 us  [kernel_call(): pl.pallas_call(body, grid_spec=pltpu.PrefetchScalarGridSpec(num_scalar_pr...]
    ppermute x66 -> x70, waiting for transfers between devices: 192 us -> 188 us  [shift(): lax.ppermute(value, axis, [(i, (i + step) % size) for i in range(size)])]
    unnamed x259 -> x279, local copies, waits for them, and re-layouts: 68.7 us -> 67.4 us
  transfers between devices with their start and end apart: 83 -> 78, of which waited for: 48 -> 44; matrix products, arithmetic and copies ran while one was open for 5% -> 6% of each run, Pallas kernels for 37% -> 38%
where the time goes in v3:
time: 682 us; the launch traced here: 675 us
  Pallas kernels  284 us (42%)
  waiting for transfers between devices  201 us (29%)
  local copies, waits for them, and re-layouts  77.1 us (11%)
  starting transfers between devices  64.1 us (9%)
  other arithmetic  33.4 us (5%)
  between operations  16.3 us (2%)
    pallas_call x62, Pallas kernels, kernel_call(): pl.pallas_call(body, grid_spec=pltpu.PrefetchScalarGridSpec(num_scalar_pr...  284 us
    ppermute x70, waiting for transfers between devices, shift(): lax.ppermute(value, axis, [(i, (i + step) % size) for i in range(size)])  188 us
    unnamed x279, local copies, waits for them, and re-layouts  67.4 us
    ppermute x70, starting transfers between devices, shift(): lax.ppermute(value, axis, [(i, (i + step) % size) for i in range(size)])  63.8 us
  transfers between devices with their start and end apart: 78, of which 44 were waited for; matrix products, arithmetic and copies ran while one was open for 6% of the time, Pallas kernels for 38%

profile of v3, /device:TPU:0, one launch (start us, length us, event | category | flops | bytes accessed | tf_op | source)
XLA Modules:
  0.0 675.4 jit_solution(2620054583769583528)
XLA Ops:
  69.3 10.1 %project_qkv.2 = (bf16[1024,256]{1,0:T(8,128)(2,1)S(1)}, bf16[1024,512]{1,0:T(8,128)(2,1)}) custom-call(s32[25]{0:T(128)S(1)} %concatenate.43.table_ref, bf16[8,512,512]{2,1,0:T(8,128)(2,1)S(1)} %fusion.3.g_ref, bf16[512,768]{1,0:T(8,128)(2,1)S(1)} %copy-done.47, bf16[512,768]{1,0:T(8,128)(2,1)} %collective-permute-done.4.rest_1_.rest_4_, ...), custom_call_target="tpu_custom_call" | custom-call | flops 1 | bytes 1 | tf_op jit(solution)/shard_map/project_qkv/pallas_call | solution.py:133
  81.4 9.0 %attend_own.2 = (bf16[1024,256]{1,0:T(8,128)(2,1)}, f32[1024,256]{1,0:T(8,128)S(1)}, f32[4,1024]{1,0:T(4,128)S(1)}) custom-call(s32[2]{0:T(128)S(1)} %get-tuple-element.1353.begin_ref, bf16[1024,256]{1,0:T(8,128)(2,1)S(1)} %get-tuple-element.1354.q_ref, bf16[1024,512]{1,0:T(8,128)(2,1)} %get-tuple-element.1355.kv_ref, s32[1,1024]{1,0:T(1,128)S(1)} %bitcast.77), custom_call_target="tpu_custom_call" | custom-call | flops 1 | bytes 1 | tf_op jit(solution)/shard_map/attend_own/pallas_call | solution.py:133
  90.4 21.5 %collective-permute-done.14.kv_ref = bf16[1024,512]{1,0:T(8,128)(2,1)} collective-permute-done((bf16[1024,512]{1,0:T(8,128)(2,1)}, bf16[1024,512]{1,0:T(8,128)(2,1)}, u32[]{:S(2)}, u32[]{:S(2)}) %collective-permute-start.14) | collective-permute-done | bytes 1048608 | tf_op jit(solution)/shard_map/ppermute | solution.py:39
  114.5 10.2 %attend_far.2 = (bf16[1024,256]{1,0:T(8,128)(2,1)S(1)}, f32[1024,256]{1,0:T(8,128)S(1)}, f32[4,1024]{1,0:T(4,128)S(1)}) custom-call(s32[2]{0:T(128)S(1)} %get-tuple-element.1335.begin_ref, bf16[1024,256]{1,0:T(8,128)(2,1)S(1)} %get-tuple-element.1354.q_ref, bf16[1024,512]{1,0:T(8,128)(2,1)} %collective-permute-done.14.kv_ref, s32[1,1024]{1,0:T(1,128)S(1)} %bitcast.78, ...), custom_call_target="tpu_custom_call" | custom-call | flops 1 | bytes 1 | tf_op jit(solution)/shard_map/attend_far/pallas_call | solution.py:133
  135.2 5.0 collective-permute-done.16.rest_5_.rest_3_
  145.2 9.7 %project_up.2 = (bf16[1024,1024]{1,0:T(8,128)(2,1)S(1)}, bf16[1024,1024]{1,0:T(8,128)(2,1)S(1)}) custom-call(s32[25]{0:T(128)S(1)} %concatenate.43.table_ref, bf16[8,512,512]{2,1,0:T(8,128)(2,1)S(1)} %copy-done.1, bf16[512,1024]{1,0:T(8,128)(2,1)} %join_weights.6.rest_0_.rest_3_, bf16[512,1024]{1,0:T(8,128)(2,1)} %collective-permute-done.6.rest_1_.rest_5_, ...), custom_call_target="tpu_custom_call" | custom-call | flops 1 | bytes 1 | tf_op jit(solution)/shard_map/project_up/pallas_call | solution.py:133
  170.7 40.0 %collective-permute-done.25.rest_1_.rest_3_ = bf16[512,1792]{1,0:T(8,128)(2,1)S(1)} collective-permute-done((bf16[512,1792]{1,0:T(8,128)(2,1)S(1)}, bf16[512,1792]{1,0:T(8,128)(2,1)S(1)}, u32[]{:S(2)}, u32[]{:S(2)}) %collective-permute-start.25) | collective-permute-done | bytes 1835040 | tf_op jit(solution)/shard_map/ppermute | solution.py:39
  227.4 28.0 %collective-permute-done.31.rest_3_.rest_5_ = bf16[1280,512]{1,0:T(8,128)(2,1)S(1)} collective-permute-done((bf16[1280,512]{1,0:T(8,128)(2,1)}, bf16[1280,512]{1,0:T(8,128)(2,1)S(1)}, u32[]{:S(2)}, u32[]{:S(2)}) %collective-permute-start.31) | collective-permute-done | bytes 1310752 | tf_op jit(solution)/shard_map/ppermute | solution.py:39
  259.0 11.6 %branch_grads.2 = (bf16[1024,256]{1,0:T(8,128)(2,1)S(1)}, bf16[1024,1024]{1,0:T(8,128)(2,1)S(1)}) custom-call(s32[25]{0:T(128)S(1)} %concatenate.43.table_ref, bf16[8,512,512]{2,1,0:T(8,128)(2,1)S(1)} %bitcast.69, bf16[1280,512]{1,0:T(8,128)(2,1)S(1)} %copy-done.41, bf16[1280,512]{1,0:T(8,128)(2,1)} %collective-permute-done.22.rest_1_.rest_3_, ...), custom_call_target="tpu_custom_call" | custom-call | flops 1 | bytes 1 | tf_op jit(solution)/shard_map/branch_grads/pallas_call | solution.py:133
  278.5 9.5 %project_qkv.3 = (bf16[1024,256]{1,0:T(8,128)(2,1)S(1)}, bf16[1024,512]{1,0:T(8,128)(2,1)S(1)}) custom-call(s32[25]{0:T(128)S(1)} %concatenate.43.table_ref, bf16[8,512,512]{2,1,0:T(8,128)(2,1)} %bitcast.63, bf16[512,1792]{1,0:T(8,128)(2,1)S(1)} %join_weights.8.rest_0_.rest_2_, bf16[512,1792]{1,0:T(8,128)(2,1)S(1)} %copy-done.27, ...), custom_call_target="tpu_custom_call" | custom-call | flops 1 | bytes 1 | tf_op jit(solution)/shard_map/project_qkv/pallas_call | solution.py:133
  290.7 10.2 %project_up.3 = (bf16[1024,1024]{1,0:T(8,128)(2,1)S(1)}, bf16[1024,1024]{1,0:T(8,128)(2,1)S(1)}) custom-call(s32[25]{0:T(128)S(1)} %concatenate.43.table_ref, bf16[8,512,512]{2,1,0:T(8,128)(2,1)} %bitcast.64, bf16[512,1792]{1,0:T(8,128)(2,1)S(1)} %copy-done.9, bf16[512,1792]{1,0:T(8,128)(2,1)S(1)} %copy-done.28, bf16[512,1792]{1,0:T(8,128)(2,1)S(1)} %copy-done.31, ...), custom_call_target="tpu_custom_call" | custom-call | flops 1 | bytes 1 | tf_op jit(solution)/shard_map/project_up/pallas_call | solution.py:133
  301.0 7.4 %attend_own.3 = (bf16[1024,256]{1,0:T(8,128)(2,1)}, f32[1024,256]{1,0:T(8,128)S(1)}, f32[4,1024]{1,0:T(4,128)S(1)}) custom-call(s32[2]{0:T(128)S(1)} %get-tuple-element.1353.begin_ref, bf16[1024,256]{1,0:T(8,128)(2,1)S(1)} %get-tuple-element.1145.q_ref, bf16[1024,512]{1,0:T(8,128)(2,1)S(1)} %get-tuple-element.1146.kv_ref, s32[1,1024]{1,0:T(1,128)S(1)} %bitcast.79), custom_call_target="tpu_custom_call" | custom-call | flops 1 | bytes 1 | tf_op jit(solution)/shard_map/attend_own/pallas_call | solution.py:133
  316.6 8.6 %attend_far.3 = (bf16[1024,256]{1,0:T(8,128)(2,1)S(1)}, f32[1024,256]{1,0:T(8,128)S(1)}, f32[4,1024]{1,0:T(4,128)S(1)}) custom-call(s32[2]{0:T(128)S(1)} %get-tuple-element.1335.begin_ref, bf16[1024,256]{1,0:T(8,128)(2,1)S(1)} %get-tuple-element.1145.q_ref, bf16[1024,512]{1,0:T(8,128)(2,1)S(1)} %collective-permute-done.32.kv_ref, s32[1,1024]{1,0:T(1,128)S(1)} %bitcast.80, ...), custom_call_target="tpu_custom_call" | custom-call | flops 1 | bytes 1 | tf_op jit(solution)/shard_map/attend_far/pallas_call | solution.py:133
  325.3 13.6 %attend_backward.4 = (f32[1024,256]{1,0:T(8,128)S(1)}, bf16[1024,512]{1,0:T(8,128)(2,1)}) custom-call(s32[2]{0:T(128)S(1)} %get-tuple-element.1335.begin_ref, bf16[1024,256]{1,0:T(8,128)(2,1)S(1)} %get-tuple-element.1145.q_ref, bf16[1024,512]{1,0:T(8,128)(2,1)S(1)} %collective-permute-done.32.kv_ref, s32[1,1024]{1,0:T(1,128)S(1)} %bitcast.81, ...), custom_call_target="tpu_custom_call" | custom-call | flops 1 | bytes 1 | tf_op jit(solution)/shard_map/attend_backward/pallas_call | solution.py:133
  341.6 9.1 %attend_backward.5 = (f32[1024,256]{1,0:T(8,128)S(1)}, f32[1024,512]{1,0:T(8,128)S(1)}) custom-call(s32[2]{0:T(128)S(1)} %get-tuple-element.1353.begin_ref, bf16[1024,256]{1,0:T(8,128)(2,1)S(1)} %get-tuple-element.1145.q_ref, bf16[1024,512]{1,0:T(8,128)(2,1)S(1)} %get-tuple-element.1146.kv_ref, s32[1,1024]{1,0:T(1,128)S(1)} %bitcast.82, ...), custom_call_target="tpu_custom_call" | custom-call | flops 1 | bytes 1 | tf_op jit(solution)/shard_map/attend_backward/pallas_call | solution.py:133
  366.0 6.2 feature_grads.4
  372.8 5.8 feature_grads.5.own_ref
  390.6 5.6 grad_in.10
  414.0 9.7 %reduce-scatter.7.cloned.1.call-done = bf16[512,512]{1,0:T(8,128)(2,1)} async-done(((bf16[512,2048]{1,0:T(8,128)(2,1)}), bf16[512,512]{1,0:T(8,128)(2,1)}) %reduce-scatter.7.cloned.1.call-update) | async-done | bytes 524304 | tf_op jit(solution)/shard_map/reduce_scatter | solution.py:1383
  446.5 6.7 grad_out.5
  457.9 8.3 %collective-permute-done.45.refs_0_.refs_1_ = bf16[512,1024]{1,0:T(8,128)(2,1)S(1)} collective-permute-done((bf16[512,1024]{1,0:T(8,128)(2,1)}, bf16[512,1024]{1,0:T(8,128)(2,1)S(1)}, u32[]{:S(2)}, u32[]{:S(2)}) %collective-permute-start.45) | collective-permute-done | bytes 1048608 | tf_op jit(solution)/shard_map/ppermute | solution.py:39
  470.9 10.8 %collective-permute-done.47.refs_0_.refs_1_ = bf16[1280,512]{1,0:T(8,128)(2,1)S(1)} collective-permute-done((bf16[1280,512]{1,0:T(8,128)(2,1)S(1)}, bf16[1280,512]{1,0:T(8,128)(2,1)S(1)}, u32[]{:S(2)}, u32[]{:S(2)}) %collective-permute-start.47) | collective-permute-done | bytes 1310752 | tf_op jit(solution)/shard_map/ppermute | solution.py:39
  490.7 5.4 grad_out.6
  499.8 11.3 %branch_grads.3 = (bf16[1024,256]{1,0:T(8,128)(2,1)S(1)}, bf16[1024,1024]{1,0:T(8,128)(2,1)S(1)}) custom-call(s32[25]{0:T(128)S(1)} %concatenate.43.table_ref, bf16[8,512,512]{2,1,0:T(8,128)(2,1)S(1)} %bitcast.73, bf16[1280,512]{1,0:T(8,128)(2,1)S(1)} %copy-done.45, bf16[1280,512]{1,0:T(8,128)(2,1)} %collective-permute-done.13.rest_3_.rest_1_, ...), custom_call_target="tpu_custom_call" | custom-call | flops 1 | bytes 1 | tf_op jit(solution)/shard_map/branch_grads/pallas_call | solution.py:133
  511.2 14.3 %attend_backward.6 = (f32[1024,256]{1,0:T(8,128)S(1)}, bf16[1024,512]{1,0:T(8,128)(2,1)S(1)}) custom-call(s32[2]{0:T(128)S(1)} %get-tuple-element.1335.begin_ref, bf16[1024,256]{1,0:T(8,128)(2,1)S(1)} %copy-done.63, bf16[1024,512]{1,0:T(8,128)(2,1)} %collective-permute-done.14.kv_ref, s32[1,1024]{1,0:T(1,128)S(1)} %bitcast.83, f32[1024,256]{1,0:T(8,128)S(1)} %copy-done.67, ...), custom_call_target="tpu_custom_call" | custom-call | flops 1 | bytes 1 | tf_op jit(solution)/shard_map/attend_backward/pallas_call | solution.py:133
  532.1 10.2 %attend_backward.7 = (f32[1024,256]{1,0:T(8,128)S(1)}, f32[1024,512]{1,0:T(8,128)S(1)}) custom-call(s32[2]{0:T(128)S(1)} %get-tuple-element.1353.begin_ref, bf16[1024,256]{1,0:T(8,128)(2,1)S(1)} %copy-done.63, bf16[1024,512]{1,0:T(8,128)(2,1)} %get-tuple-element.1355.kv_ref, s32[1,1024]{1,0:T(1,128)S(1)} %bitcast.84, f32[1024,256]{1,0:T(8,128)S(1)} %copy-done.67, ...), custom_call_target="tpu_custom_call" | custom-call | flops 1 | bytes 1 | tf_op jit(solution)/shard_map/attend_backward/pallas_call | solution.py:133
  558.2 6.8 %feature_grads.6 = (bf16[256,2048]{1,0:T(8,128)(2,1)S(1)}, bf16[256,2048]{1,0:T(8,128)(2,1)S(1)}) custom-call(s32[25]{0:T(128)S(1)} %concatenate.43.table_ref, bf16[1024,768]{1,0:T(8,128)(2,1)S(1)} %get-tuple-element.1464.right_ref.rest_0_, bf16[1024,1024]{1,0:T(8,128)(2,1)S(1)} %get-tuple-element.1427.right_ref.rest_1_, bf16[512,768]{1,0:T(8,128)(2,1)S(1)} %copy-done.48, ...), custom_call_target="tpu_custom_call" | custom-call | flops 1 | bytes 1 | tf_op jit(solution)/shard_map/feature_grads/pallas_call | solution.py:133
  565.6 6.6 feature_grads.7.own_ref
  572.3 5.8 collective-permute-done.53.rest_0_
  604.6 5.7 grad_out.7
  610.3 8.5 %collective-permute-done.57.rest_0_ = bf16[1024,768]{1,0:T(8,128)(2,1)} collective-permute-done((bf16[1024,768]{1,0:T(8,128)(2,1)}, bf16[1024,768]{1,0:T(8,128)(2,1)}, u32[]{:S(2)}, u32[]{:S(2)}) %collective-permute-start.57) | collective-permute-done | bytes 1572896 | tf_op jit(solution)/shard_map/ppermute | solution.py:39
  620.4 5.2 grad_in.15
  (562 shorter events, 322.6 us)
Async XLA Ops:
  7.2 54.7 %all-gather.11.cloned.1.call-start = ((), (), s32[]{:S(2)}) async-start(), calls=%async_computation.9 | async-start | bytes 4718592 | tf_op jit(solution)/shard_map/all_gather | solution.py:1380
  7.9 126.9 %all-gather.9.cloned.1.call-start = ((), (), s32[]{:S(2)}) async-start(), calls=%async_computation.8 | async-start | bytes 4718592 | tf_op jit(solution)/shard_map/all_gather | solution.py:1380
  13.0 200.1 %reduce-scatter.5.cloned.1.call-start = ((), (), s32[]{:S(2)}) async-start(), calls=%async_computation.4 | async-start | bytes 2621440 | tf_op jit(solution)/shard_map/reduce_scatter | solution.py:1383
  35.4 24.4 %collective-permute-start.6 = (bf16[512,1024]{1,0:T(8,128)(2,1)}, bf16[512,1024]{1,0:T(8,128)(2,1)}, u32[]{:S(2)}, u32[]{:S(2)}) collective-permute-start(bf16[512,1024]{1,0:T(8,128)(2,1)} %join_weights.6.rest_0_.rest_3_), channel_id=1, source_target_pairs={{0,8},{8,0},{1,9},{9,1},{2,10},{10,2},{3,11},{11,3},{4,12},{12,4},... | collective-permute-start | bytes 3145736 | tf_op jit(solution)/shard_map/ppermute | solution.py:39
  59.8 52.1 %collective-permute-start.12 = (bf16[1280,512]{1,0:T(8,128)(2,1)S(1)}, bf16[1280,512]{1,0:T(8,128)(2,1)}, u32[]{:S(2)}, u32[]{:S(2)}) collective-permute-start(bf16[1280,512]{1,0:T(8,128)(2,1)S(1)} %join_weights.7.rest_2_.rest_0_), channel_id=1, source_target_pairs={{0,16},{16,0},{1,17},{17,1},{2,18},{18,2},{3,19},{19,3},{4,20},{20... | collective-permute-start | bytes 3932168 | tf_op jit(solution)/shard_map/ppermute | solution.py:39
  60.7 51.1 %collective-permute-start.13 = (bf16[1280,512]{1,0:T(8,128)(2,1)S(1)}, bf16[1280,512]{1,0:T(8,128)(2,1)}, u32[]{:S(2)}, u32[]{:S(2)}) collective-permute-start(bf16[1280,512]{1,0:T(8,128)(2,1)S(1)} %join_weights.7.rest_2_.rest_0_), channel_id=1, source_target_pairs={{0,8},{8,0},{1,9},{9,1},{2,10},{10,2},{3,11},{11,3},{4,12},{12,4},... | collective-permute-start | bytes 3932168 | tf_op jit(solution)/shard_map/ppermute | solution.py:39
  79.4 32.4 %collective-permute-start.14 = (bf16[1024,512]{1,0:T(8,128)(2,1)}, bf16[1024,512]{1,0:T(8,128)(2,1)}, u32[]{:S(2)}, u32[]{:S(2)}) collective-permute-start(bf16[1024,512]{1,0:T(8,128)(2,1)} %get-tuple-element.1355.kv_ref), channel_id=1, source_target_pairs={{0,8},{8,0},{1,9},{9,1},{2,10},{10,2},{3,11},{11,3},{4,12},{12,4},... | collective-permute-start | bytes 3145736 | tf_op jit(solution)/shard_map/ppermute | solution.py:39
  80.2 31.7 %collective-permute-start.11 = (bf16[512,1024]{1,0:T(8,128)(2,1)}, bf16[512,1024]{1,0:T(8,128)(2,1)}, u32[]{:S(2)}, u32[]{:S(2)}) collective-permute-start(bf16[512,1024]{1,0:T(8,128)(2,1)} %join_weights.6.rest_0_.rest_3_), channel_id=1, source_target_pairs={{0,16},{16,0},{1,17},{17,1},{2,18},{18,2},{3,19},{19,3},{4,20},{20... | collective-permute-start | bytes 3145736 | tf_op jit(solution)/shard_map/ppermute | solution.py:39
  111.9 28.3 %collective-permute-start.16 = (bf16[1280,512]{1,0:T(8,128)(2,1)}, bf16[1280,512]{1,0:T(8,128)(2,1)}, u32[]{:S(2)}, u32[]{:S(2)}) collective-permute-start(bf16[1280,512]{1,0:T(8,128)(2,1)} %collective-permute-done.12.rest_4_.rest_2_), channel_id=1, source_target_pairs={{0,8},{8,0},{1,9},{9,1},{2,10},{10,2},{3,11},{11,3},{4,12},{12,4},... | collective-permute-start | bytes 3932168 | tf_op jit(solution)/shard_map/ppermute | solution.py:39
  140.2 28.3 %collective-permute-start.21 = (bf16[1280,512]{1,0:T(8,128)(2,1)}, bf16[1280,512]{1,0:T(8,128)(2,1)}, u32[]{:S(2)}, u32[]{:S(2)}) collective-permute-start(bf16[1280,512]{1,0:T(8,128)(2,1)} %copy-done.40), channel_id=1, source_target_pairs={{0,16},{16,0},{1,17},{17,1},{2,18},{18,2},{3,19},{19,3},{4,20},{20... | collective-permute-start | bytes 3932168 | tf_op jit(solution)/shard_map/ppermute | solution.py:39
  141.2 27.4 %collective-permute-start.22 = (bf16[1280,512]{1,0:T(8,128)(2,1)}, bf16[1280,512]{1,0:T(8,128)(2,1)}, u32[]{:S(2)}, u32[]{:S(2)}) collective-permute-start(bf16[1280,512]{1,0:T(8,128)(2,1)} %copy-done.40), channel_id=1, source_target_pairs={{0,8},{8,0},{1,9},{9,1},{2,10},{10,2},{3,11},{11,3},{4,12},{12,4},... | collective-permute-start | bytes 3932168 | tf_op jit(solution)/shard_map/ppermute | solution.py:39
  168.6 105.4 %all-gather.13.cloned.1.call-start = ((), (), s32[]{:S(2)}) async-start(), calls=%async_computation.10 | async-start | bytes 4718592 | tf_op jit(solution)/shard_map/all_gather | solution.py:1380
  168.6 42.1 %collective-permute-start.25 = (bf16[512,1792]{1,0:T(8,128)(2,1)S(1)}, bf16[512,1792]{1,0:T(8,128)(2,1)S(1)}, u32[]{:S(2)}, u32[]{:S(2)}) collective-permute-start(bf16[512,1792]{1,0:T(8,128)(2,1)S(1)} %join_weights.8.rest_0_.rest_2_), channel_id=1, source_target_pairs={{0,8},{8,0},{1,9},{9,1},{2,10},{10,2},{3,11},{11,3},{4,12},{12,4},... | collective-permute-start | bytes 5505032 | tf_op jit(solution)/shard_map/ppermute | solution.py:39
  169.3 42.6 %collective-permute-start.26 = (bf16[512,1792]{1,0:T(8,128)(2,1)S(1)}, bf16[512,1792]{1,0:T(8,128)(2,1)S(1)}, u32[]{:S(2)}, u32[]{:S(2)}) collective-permute-start(bf16[512,1792]{1,0:T(8,128)(2,1)S(1)} %join_weights.8.rest_0_.rest_2_), channel_id=1, source_target_pairs={{0,16},{16,0},{1,17},{17,1},{2,18},{18,2},{3,19},{19,3},{4,20},{20... | collective-permute-start | bytes 5505032 | tf_op jit(solution)/shard_map/ppermute | solution.py:39
  226.5 197.2 %reduce-scatter.7.cloned.1.call-start = ((), (), s32[]{:S(2)}) async-start(), calls=%async_computation.5 | async-start | bytes 2621440 | tf_op jit(solution)/shard_map/reduce_scatter | solution.py:1383
  226.6 46.2 %collective-permute-start.30 = (bf16[512,1792]{1,0:T(8,128)(2,1)}, bf16[512,1792]{1,0:T(8,128)(2,1)S(1)}, u32[]{:S(2)}, u32[]{:S(2)}) collective-permute-start(bf16[512,1792]{1,0:T(8,128)(2,1)} %copy-done.26), channel_id=1, source_target_pairs={{0,16},{16,0},{1,17},{17,1},{2,18},{18,2},{3,19},{19,3},{4,20},{20... | collective-permute-start | bytes 5505032 | tf_op jit(solution)/shard_map/ppermute | solution.py:39
  226.8 28.6 %collective-permute-start.31 = (bf16[1280,512]{1,0:T(8,128)(2,1)}, bf16[1280,512]{1,0:T(8,128)(2,1)S(1)}, u32[]{:S(2)}, u32[]{:S(2)}) collective-permute-start(bf16[1280,512]{1,0:T(8,128)(2,1)} %collective-permute-done.21.rest_2_.rest_4_), channel_id=1, source_target_pairs={{0,8},{8,0},{1,9},{9,1},{2,10},{10,2},{3,11},{11,3},{4,12},{12,4},... | collective-permute-start | bytes 3932168 | tf_op jit(solution)/shard_map/ppermute | solution.py:39
  315.1 45.6 %collective-permute-start.34 = (bf16[1024,1024]{1,0:T(8,128)(2,1)}, bf16[1024,1024]{1,0:T(8,128)(2,1)}, u32[]{:S(2)}, u32[]{:S(2)}) collective-permute-start(bf16[1024,1024]{1,0:T(8,128)(2,1)} %grad_in.8), channel_id=1, source_target_pairs={{0,16},{16,0},{1,17},{17,1},{2,18},{18,2},{3,19},{19,3},{4,20},{20... | collective-permute-start | bytes 6291464 | tf_op jit(solution)/shard_map/ppermute | solution.py:39
  381.0 107.4 %all-gather.15.cloned.1.call-start = ((), (), s32[]{:S(2)}) async-start(), calls=%async_computation.11 | async-start | bytes 4718592 | tf_op jit(solution)/shard_map/all_gather | solution.py:1380
  381.1 31.1 %collective-permute-start.39 = (bf16[1280,512]{1,0:T(8,128)(2,1)}, bf16[1280,512]{1,0:T(8,128)(2,1)}, u32[]{:S(2)}, u32[]{:S(2)}) collective-permute-start(bf16[1280,512]{1,0:T(8,128)(2,1)} %copy-done.113), channel_id=1, source_target_pairs={{0,8},{8,0},{1,9},{9,1},{2,10},{10,2},{3,11},{11,3},{4,12},{12,4},... | collective-permute-start | bytes 3932168 | tf_op jit(solution)/shard_map/ppermute | solution.py:39
  401.5 36.7 %collective-permute-start.41 = (bf16[1024,768]{1,0:T(8,128)(2,1)}, bf16[1024,768]{1,0:T(8,128)(2,1)}, u32[]{:S(2)}, u32[]{:S(2)}) collective-permute-start(bf16[1024,768]{1,0:T(8,128)(2,1)} %grad_in.9), channel_id=1, source_target_pairs={{0,16},{16,0},{1,17},{17,1},{2,18},{18,2},{3,19},{19,3},{4,20},{20... | collective-permute-start | bytes 4718600 | tf_op jit(solution)/shard_map/ppermute | solution.py:39
  412.2 30.2 %collective-permute-start.40 = (bf16[1280,512]{1,0:T(8,128)(2,1)}, bf16[1280,512]{1,0:T(8,128)(2,1)}, u32[]{:S(2)}, u32[]{:S(2)}) collective-permute-start(bf16[1280,512]{1,0:T(8,128)(2,1)} %get-tuple-element.1231), channel_id=1, source_target_pairs={{0,8},{8,0},{1,9},{9,1},{2,10},{10,2},{3,11},{11,3},{4,12},{12,4},... | collective-permute-start | bytes 3932168 | tf_op jit(solution)/shard_map/ppermute | solution.py:39
  442.5 154.5 %reduce-scatter.9.cloned.1.call-start = ((), (), s32[]{:S(2)}) async-start(), calls=%async_computation.6 | async-start | bytes 2621440 | tf_op jit(solution)/shard_map/reduce_scatter | solution.py:1383
  453.2 28.4 %collective-permute-start.47 = (bf16[1280,512]{1,0:T(8,128)(2,1)S(1)}, bf16[1280,512]{1,0:T(8,128)(2,1)S(1)}, u32[]{:S(2)}, u32[]{:S(2)}) collective-permute-start(bf16[1280,512]{1,0:T(8,128)(2,1)S(1)} %get-tuple-element.1270), channel_id=1, source_target_pairs={{0,16},{16,0},{1,17},{17,1},{2,18},{18,2},{3,19},{19,3},{4,20},{20... | collective-permute-start | bytes 3932168 | tf_op jit(solution)/shard_map/ppermute | solution.py:39
  488.5 139.1 %reduce-scatter.11.cloned.1.call-start = ((), (), s32[]{:S(2)}) async-start(), calls=%async_computation.7 | async-start | bytes 2621440 | tf_op jit(solution)/shard_map/reduce_scatter | solution.py:1383
  496.1 54.4 %collective-permute-start.51 = (bf16[1280,512]{1,0:T(8,128)(2,1)}, bf16[1280,512]{1,0:T(8,128)(2,1)S(1)}, u32[]{:S(2)}, u32[]{:S(2)}) collective-permute-start(bf16[1280,512]{1,0:T(8,128)(2,1)} %get-tuple-element.1323), channel_id=1, source_target_pairs={{0,8},{8,0},{1,9},{9,1},{2,10},{10,2},{3,11},{11,3},{4,12},{12,4},... | collective-permute-start | bytes 3932168 | tf_op jit(solution)/shard_map/ppermute | solution.py:39
  525.4 25.1 %collective-permute-start.50 = (bf16[1024,512]{1,0:T(8,128)(2,1)S(1)}, bf16[1024,512]{1,0:T(8,128)(2,1)S(1)}, u32[]{:S(2)}, u32[]{:S(2)}) collective-permute-start(bf16[1024,512]{1,0:T(8,128)(2,1)S(1)} %get-tuple-element.1346), channel_id=1, source_target_pairs={{0,8},{8,0},{1,9},{9,1},{2,10},{10,2},{3,11},{11,3},{4,12},{12,4},... | collective-permute-start | bytes 3145736 | tf_op jit(solution)/shard_map/ppermute | solution.py:39
  530.7 47.5 %collective-permute-start.53 = (bf16[1024,1024]{1,0:T(8,128)(2,1)}, bf16[1024,1024]{1,0:T(8,128)(2,1)S(1)}, u32[]{:S(2)}, u32[]{:S(2)}) collective-permute-start(bf16[1024,1024]{1,0:T(8,128)(2,1)} %grad_in.12), channel_id=1, source_target_pairs={{0,16},{16,0},{1,17},{17,1},{2,18},{18,2},{3,19},{19,3},{4,20},{20... | collective-permute-start | bytes 6291464 | tf_op jit(solution)/shard_map/ppermute | solution.py:39
  550.5 30.0 %collective-permute-start.54 = (bf16[1280,512]{1,0:T(8,128)(2,1)}, bf16[1280,512]{1,0:T(8,128)(2,1)S(1)}, u32[]{:S(2)}, u32[]{:S(2)}) collective-permute-start(bf16[1280,512]{1,0:T(8,128)(2,1)} %get-tuple-element.1409), channel_id=1, source_target_pairs={{0,8},{8,0},{1,9},{9,1},{2,10},{10,2},{3,11},{11,3},{4,12},{12,4},... | collective-permute-start | bytes 3932168 | tf_op jit(solution)/shard_map/ppermute | solution.py:39
  584.0 34.8 %collective-permute-start.57 = (bf16[1024,768]{1,0:T(8,128)(2,1)}, bf16[1024,768]{1,0:T(8,128)(2,1)}, u32[]{:S(2)}, u32[]{:S(2)}) collective-permute-start(bf16[1024,768]{1,0:T(8,128)(2,1)} %copy-done.82), channel_id=1, source_target_pairs={{0,16},{16,0},{1,17},{17,1},{2,18},{18,2},{3,19},{19,3},{4,20},{20... | collective-permute-start | bytes 4718600 | tf_op jit(solution)/shard_map/ppermute | solution.py:39
  596.1 30.4 %collective-permute-start.58 = (bf16[512,1024]{1,0:T(8,128)(2,1)}, bf16[512,1024]{1,0:T(8,128)(2,1)}, u32[]{:S(2)}, u32[]{:S(2)}) collective-permute-start(bf16[512,1024]{1,0:T(8,128)(2,1)} %get-tuple-element.1438), channel_id=1, source_target_pairs={{0,8},{8,0},{1,9},{9,1},{2,10},{10,2},{3,11},{11,3},{4,12},{12,4},... | collective-permute-start | bytes 3145736 | tf_op jit(solution)/shard_map/ppermute | solution.py:39
  618.9 28.1 %collective-permute-start.64 = (bf16[1280,512]{1,0:T(8,128)(2,1)}, bf16[1280,512]{1,0:T(8,128)(2,1)S(1)}, u32[]{:S(2)}, u32[]{:S(2)}) collective-permute-start(bf16[1280,512]{1,0:T(8,128)(2,1)} %get-tuple-element.1462), channel_id=1, source_target_pairs={{0,16},{16,0},{1,17},{17,1},{2,18},{18,2},{3,19},{19,3},{4,20},{20... | collective-permute-start | bytes 3932168 | tf_op jit(solution)/shard_map/ppermute | solution.py:39
  (182 other events, 1798.2 us)
Sparse Core Ops, SparseCore 0:
  9.6 50.1 all-gather.10
  61.4 45.7 all-gather.8
  168.7 44.0 reduce-scatter.4
  226.6 44.0 all-gather.12
  381.2 42.4 reduce-scatter.6
  442.6 45.7 all-gather.14
  490.7 42.5 reduce-scatter.8
  584.1 42.1 reduce-scatter.10

commit v4 on v3

--- a/solution.py
+++ b/solution.py
@@ -17,8 +17,8 @@
 HEADS_TILE = LANES // HEAD_DIM
 MEBI = 1024 * 1024
 PIECES = 2
-VMEM_MEBI = 40
-MORE_MEBI = 40
+VMEM_MEBI = 22
+MORE_MEBI = 26
 F32 = jnp.float32
 BF16 = jnp.bfloat16
 ANY = pl.BlockSpec(memory_space=pl.ANY)

time: 682 us -> 678 us (level)
  Pallas kernels: 284 us -> 276 us
    pallas_call x62, Pallas kernels: 284 us -> 276 us  [kernel_call(): pl.pallas_call(body, grid_spec=pltpu.PrefetchScalarGridSpec(num_scalar_pr...]
    unnamed x279 -> x271, local copies, waits for them, and re-layouts: 67.4 us -> 63.7 us
  transfers between devices with their start and end apart: 78 -> 78, of which waited for: 44 -> 43; matrix products, arithmetic and copies ran while one was open for 6% -> 6% of each run, Pallas kernels for 38% -> 37%
where the time goes in v4:
time: 678 us; the launch traced here: 672 us
  Pallas kernels  276 us (41%)
  waiting for transfers between devices  203 us (30%)
  local copies, waits for them, and re-layouts  73.4 us (11%)
  starting transfers between devices  69 us (10%)
  other arithmetic  33.4 us (5%)
  between operations  16.3 us (2%)
    pallas_call x62, Pallas kernels, kernel_call(): pl.pallas_call(body, grid_spec=pltpu.PrefetchScalarGridSpec(num_scalar_pr...  276 us
    ppermute x70, waiting for transfers between devices, shift(): lax.ppermute(value, axis, [(i, (i + step) % size) for i in range(size)])  190 us
    ppermute x70, starting transfers between devices, shift(): lax.ppermute(value, axis, [(i, (i + step) % size) for i in range(size)])  68.7 us
    unnamed x271, local copies, waits for them, and re-layouts  63.7 us
  transfers between devices with their start and end apart: 78, of which 43 were waited for; matrix products, arithmetic and copies ran while one was open for 6% of the time, Pallas kernels for 37%

profile of v4, /device:TPU:0, one launch (start us, length us, event | category | flops | bytes accessed | tf_op | source)
XLA Modules:
  0.0 672.0 jit_solution(17643738691741467890)
XLA Ops:
  69.3 10.1 %project_qkv.2 = (bf16[1024,256]{1,0:T(8,128)(2,1)S(1)}, bf16[1024,512]{1,0:T(8,128)(2,1)}) custom-call(s32[25]{0:T(128)S(1)} %concatenate.43.table_ref, bf16[8,512,512]{2,1,0:T(8,128)(2,1)S(1)} %fusion.3.g_ref, bf16[512,768]{1,0:T(8,128)(2,1)S(1)} %copy-done.47, bf16[512,768]{1,0:T(8,128)(2,1)} %collective-permute-done.4.rest_1_.rest_4_, ...), custom_call_target="tpu_custom_call" | custom-call | flops 1 | bytes 1 | tf_op jit(solution)/shard_map/project_qkv/pallas_call | solution.py:133
  81.4 9.0 %attend_own.2 = (bf16[1024,256]{1,0:T(8,128)(2,1)}, f32[1024,256]{1,0:T(8,128)S(1)}, f32[4,1024]{1,0:T(4,128)S(1)}) custom-call(s32[2]{0:T(128)S(1)} %get-tuple-element.1353.begin_ref, bf16[1024,256]{1,0:T(8,128)(2,1)S(1)} %get-tuple-element.1354.q_ref, bf16[1024,512]{1,0:T(8,128)(2,1)} %get-tuple-element.1355.kv_ref, s32[1,1024]{1,0:T(1,128)S(1)} %bitcast.77), custom_call_target="tpu_custom_call" | custom-call | flops 1 | bytes 1 | tf_op jit(solution)/shard_map/attend_own/pallas_call | solution.py:133
  90.4 21.5 %collective-permute-done.14.kv_ref = bf16[1024,512]{1,0:T(8,128)(2,1)} collective-permute-done((bf16[1024,512]{1,0:T(8,128)(2,1)}, bf16[1024,512]{1,0:T(8,128)(2,1)}, u32[]{:S(2)}, u32[]{:S(2)}) %collective-permute-start.14) | collective-permute-done | bytes 1048608 | tf_op jit(solution)/shard_map/ppermute | solution.py:39
  114.5 10.2 %attend_far.2 = (bf16[1024,256]{1,0:T(8,128)(2,1)S(1)}, f32[1024,256]{1,0:T(8,128)S(1)}, f32[4,1024]{1,0:T(4,128)S(1)}) custom-call(s32[2]{0:T(128)S(1)} %get-tuple-element.1335.begin_ref, bf16[1024,256]{1,0:T(8,128)(2,1)S(1)} %get-tuple-element.1354.q_ref, bf16[1024,512]{1,0:T(8,128)(2,1)} %collective-permute-done.14.kv_ref, s32[1,1024]{1,0:T(1,128)S(1)} %bitcast.78, ...), custom_call_target="tpu_custom_call" | custom-call | flops 1 | bytes 1 | tf_op jit(solution)/shard_map/attend_far/pallas_call | solution.py:133
  135.2 5.0 collective-permute-done.16.rest_5_.rest_3_
  145.2 9.7 %project_up.2 = (bf16[1024,1024]{1,0:T(8,128)(2,1)S(1)}, bf16[1024,1024]{1,0:T(8,128)(2,1)S(1)}) custom-call(s32[25]{0:T(128)S(1)} %concatenate.43.table_ref, bf16[8,512,512]{2,1,0:T(8,128)(2,1)S(1)} %copy-done.1, bf16[512,1024]{1,0:T(8,128)(2,1)} %join_weights.6.rest_0_.rest_3_, bf16[512,1024]{1,0:T(8,128)(2,1)} %collective-permute-done.6.rest_1_.rest_5_, ...), custom_call_target="tpu_custom_call" | custom-call | flops 1 | bytes 1 | tf_op jit(solution)/shard_map/project_up/pallas_call | solution.py:133
  170.7 40.0 %collective-permute-done.25.rest_1_.rest_3_ = bf16[512,1792]{1,0:T(8,128)(2,1)S(1)} collective-permute-done((bf16[512,1792]{1,0:T(8,128)(2,1)S(1)}, bf16[512,1792]{1,0:T(8,128)(2,1)S(1)}, u32[]{:S(2)}, u32[]{:S(2)}) %collective-permute-start.25) | collective-permute-done | bytes 1835040 | tf_op jit(solution)/shard_map/ppermute | solution.py:39
  227.4 28.0 %collective-permute-done.31.rest_3_.rest_5_ = bf16[1280,512]{1,0:T(8,128)(2,1)S(1)} collective-permute-done((bf16[1280,512]{1,0:T(8,128)(2,1)}, bf16[1280,512]{1,0:T(8,128)(2,1)S(1)}, u32[]{:S(2)}, u32[]{:S(2)}) %collective-permute-start.31) | collective-permute-done | bytes 1310752 | tf_op jit(solution)/shard_map/ppermute | solution.py:39
  259.0 11.6 %branch_grads.2 = (bf16[1024,256]{1,0:T(8,128)(2,1)S(1)}, bf16[1024,1024]{1,0:T(8,128)(2,1)S(1)}) custom-call(s32[25]{0:T(128)S(1)} %concatenate.43.table_ref, bf16[8,512,512]{2,1,0:T(8,128)(2,1)S(1)} %bitcast.69, bf16[1280,512]{1,0:T(8,128)(2,1)S(1)} %copy-done.41, bf16[1280,512]{1,0:T(8,128)(2,1)} %collective-permute-done.22.rest_1_.rest_3_, ...), custom_call_target="tpu_custom_call" | custom-call | flops 1 | bytes 1 | tf_op jit(solution)/shard_map/branch_grads/pallas_call | solution.py:133
  280.6 8.8 %project_qkv.3 = (bf16[1024,256]{1,0:T(8,128)(2,1)S(1)}, bf16[1024,512]{1,0:T(8,128)(2,1)S(1)}) custom-call(s32[25]{0:T(128)S(1)} %concatenate.43.table_ref, bf16[8,512,512]{2,1,0:T(8,128)(2,1)S(1)} %bitcast.63, bf16[512,1792]{1,0:T(8,128)(2,1)S(1)} %join_weights.8.rest_0_.rest_2_, bf16[512,1792]{1,0:T(8,128)(2,1)S(1)} %copy-done.27, ...), custom_call_target="tpu_custom_call" | custom-call | flops 1 | bytes 1 | tf_op jit(solution)/shard_map/project_qkv/pallas_call | solution.py:133
  292.2 9.8 %project_up.3 = (bf16[1024,1024]{1,0:T(8,128)(2,1)S(1)}, bf16[1024,1024]{1,0:T(8,128)(2,1)S(1)}) custom-call(s32[25]{0:T(128)S(1)} %concatenate.43.table_ref, bf16[8,512,512]{2,1,0:T(8,128)(2,1)S(1)} %bitcast.64, bf16[512,1792]{1,0:T(8,128)(2,1)S(1)} %copy-done.10, bf16[512,1792]{1,0:T(8,128)(2,1)S(1)} %copy-done.28, bf16[512,1792]{1,0:T(8,128)(2,1)S(1)} %copy-done.31, ...), custom_call_target="tpu_custom_call" | custom-call | flops 1 | bytes 1 | tf_op jit(solution)/shard_map/project_up/pallas_call | solution.py:133
  302.0 7.4 %attend_own.3 = (bf16[1024,256]{1,0:T(8,128)(2,1)}, f32[1024,256]{1,0:T(8,128)S(1)}, f32[4,1024]{1,0:T(4,128)S(1)}) custom-call(s32[2]{0:T(128)S(1)} %get-tuple-element.1353.begin_ref, bf16[1024,256]{1,0:T(8,128)(2,1)S(1)} %get-tuple-element.1145.q_ref, bf16[1024,512]{1,0:T(8,128)(2,1)S(1)} %get-tuple-element.1146.kv_ref, s32[1,1024]{1,0:T(1,128)S(1)} %bitcast.79), custom_call_target="tpu_custom_call" | custom-call | flops 1 | bytes 1 | tf_op jit(solution)/shard_map/attend_own/pallas_call | solution.py:133
  317.2 8.6 %attend_far.3 = (bf16[1024,256]{1,0:T(8,128)(2,1)S(1)}, f32[1024,256]{1,0:T(8,128)S(1)}, f32[4,1024]{1,0:T(4,128)S(1)}) custom-call(s32[2]{0:T(128)S(1)} %get-tuple-element.1335.begin_ref, bf16[1024,256]{1,0:T(8,128)(2,1)S(1)} %get-tuple-element.1145.q_ref, bf16[1024,512]{1,0:T(8,128)(2,1)S(1)} %collective-permute-done.32.kv_ref, s32[1,1024]{1,0:T(1,128)S(1)} %bitcast.80, ...), custom_call_target="tpu_custom_call" | custom-call | flops 1 | bytes 1 | tf_op jit(solution)/shard_map/attend_far/pallas_call | solution.py:133
  325.9 12.7 %attend_backward.4 = (f32[1024,256]{1,0:T(8,128)S(1)}, bf16[1024,512]{1,0:T(8,128)(2,1)S(1)}) custom-call(s32[2]{0:T(128)S(1)} %get-tuple-element.1335.begin_ref, bf16[1024,256]{1,0:T(8,128)(2,1)S(1)} %get-tuple-element.1145.q_ref, bf16[1024,512]{1,0:T(8,128)(2,1)S(1)} %collective-permute-done.32.kv_ref, s32[1,1024]{1,0:T(1,128)S(1)} %bitcast.81, ...), custom_call_target="tpu_custom_call" | custom-call | flops 1 | bytes 1 | tf_op jit(solution)/shard_map/attend_backward/pallas_call | solution.py:133
  340.1 9.1 %attend_backward.5 = (f32[1024,256]{1,0:T(8,128)S(1)}, f32[1024,512]{1,0:T(8,128)S(1)}) custom-call(s32[2]{0:T(128)S(1)} %get-tuple-element.1353.begin_ref, bf16[1024,256]{1,0:T(8,128)(2,1)S(1)} %get-tuple-element.1145.q_ref, bf16[1024,512]{1,0:T(8,128)(2,1)S(1)} %get-tuple-element.1146.kv_ref, s32[1,1024]{1,0:T(1,128)S(1)} %bitcast.82, ...), custom_call_target="tpu_custom_call" | custom-call | flops 1 | bytes 1 | tf_op jit(solution)/shard_map/attend_backward/pallas_call | solution.py:133
  353.6 6.4 collective-permute-done.33.rest_0_
  362.7 6.2 feature_grads.4
  369.5 5.8 feature_grads.5.own_ref
  410.7 10.5 %reduce-scatter.7.cloned.1.call-done = bf16[512,512]{1,0:T(8,128)(2,1)} async-done(((bf16[512,2048]{1,0:T(8,128)(2,1)}), bf16[512,512]{1,0:T(8,128)(2,1)}) %reduce-scatter.7.cloned.1.call-update) | async-done | bytes 524304 | tf_op jit(solution)/shard_map/reduce_scatter | solution.py:1383
  443.3 6.5 grad_out.5
  455.5 7.4 %collective-permute-done.45.refs_0_.refs_1_ = bf16[512,1024]{1,0:T(8,128)(2,1)S(1)} collective-permute-done((bf16[512,1024]{1,0:T(8,128)(2,1)}, bf16[512,1024]{1,0:T(8,128)(2,1)S(1)}, u32[]{:S(2)}, u32[]{:S(2)}) %collective-permute-start.45) | collective-permute-done | bytes 1048608 | tf_op jit(solution)/shard_map/ppermute | solution.py:39
  467.6 10.8 %collective-permute-done.47.refs_0_.refs_1_ = bf16[1280,512]{1,0:T(8,128)(2,1)S(1)} collective-permute-done((bf16[1280,512]{1,0:T(8,128)(2,1)S(1)}, bf16[1280,512]{1,0:T(8,128)(2,1)S(1)}, u32[]{:S(2)}, u32[]{:S(2)}) %collective-permute-start.47) | collective-permute-done | bytes 1310752 | tf_op jit(solution)/shard_map/ppermute | solution.py:39
  496.0 11.3 %branch_grads.3 = (bf16[1024,256]{1,0:T(8,128)(2,1)S(1)}, bf16[1024,1024]{1,0:T(8,128)(2,1)S(1)}) custom-call(s32[25]{0:T(128)S(1)} %concatenate.43.table_ref, bf16[8,512,512]{2,1,0:T(8,128)(2,1)S(1)} %bitcast.73, bf16[1280,512]{1,0:T(8,128)(2,1)S(1)} %copy-done.45, bf16[1280,512]{1,0:T(8,128)(2,1)} %collective-permute-done.13.rest_3_.rest_1_, ...), custom_call_target="tpu_custom_call" | custom-call | flops 1 | bytes 1 | tf_op jit(solution)/shard_map/branch_grads/pallas_call | solution.py:133
  507.3 14.3 %attend_backward.6 = (f32[1024,256]{1,0:T(8,128)S(1)}, bf16[1024,512]{1,0:T(8,128)(2,1)S(1)}) custom-call(s32[2]{0:T(128)S(1)} %get-tuple-element.1335.begin_ref, bf16[1024,256]{1,0:T(8,128)(2,1)S(1)} %copy-done.63, bf16[1024,512]{1,0:T(8,128)(2,1)} %collective-permute-done.14.kv_ref, s32[1,1024]{1,0:T(1,128)S(1)} %bitcast.83, f32[1024,256]{1,0:T(8,128)S(1)} %copy-done.67, ...), custom_call_target="tpu_custom_call" | custom-call | flops 1 | bytes 1 | tf_op jit(solution)/shard_map/attend_backward/pallas_call | solution.py:133
  527.5 10.2 %attend_backward.7 = (f32[1024,256]{1,0:T(8,128)S(1)}, f32[1024,512]{1,0:T(8,128)S(1)}) custom-call(s32[2]{0:T(128)S(1)} %get-tuple-element.1353.begin_ref, bf16[1024,256]{1,0:T(8,128)(2,1)S(1)} %copy-done.63, bf16[1024,512]{1,0:T(8,128)(2,1)} %get-tuple-element.1355.kv_ref, s32[1,1024]{1,0:T(1,128)S(1)} %bitcast.84, f32[1024,256]{1,0:T(8,128)S(1)} %copy-done.67, ...), custom_call_target="tpu_custom_call" | custom-call | flops 1 | bytes 1 | tf_op jit(solution)/shard_map/attend_backward/pallas_call | solution.py:133
  541.9 4.8 collective-permute-done.50.rest_0_
  554.7 6.8 %feature_grads.6 = (bf16[256,2048]{1,0:T(8,128)(2,1)S(1)}, bf16[256,2048]{1,0:T(8,128)(2,1)S(1)}) custom-call(s32[25]{0:T(128)S(1)} %concatenate.43.table_ref, bf16[1024,768]{1,0:T(8,128)(2,1)S(1)} %get-tuple-element.1464.right_ref.rest_0_, bf16[1024,1024]{1,0:T(8,128)(2,1)S(1)} %get-tuple-element.1427.right_ref.rest_1_, bf16[512,768]{1,0:T(8,128)(2,1)S(1)} %copy-done.48, ...), custom_call_target="tpu_custom_call" | custom-call | flops 1 | bytes 1 | tf_op jit(solution)/shard_map/feature_grads/pallas_call | solution.py:133
  562.1 6.6 feature_grads.7.own_ref
  568.7 4.8 collective-permute-done.53.rest_0_
  601.2 5.7 grad_out.7
  607.0 7.9 %collective-permute-done.57.rest_0_ = bf16[1024,768]{1,0:T(8,128)(2,1)} collective-permute-done((bf16[1024,768]{1,0:T(8,128)(2,1)}, bf16[1024,768]{1,0:T(8,128)(2,1)}, u32[]{:S(2)}, u32[]{:S(2)}) %collective-permute-start.57) | collective-permute-done | bytes 1572896 | tf_op jit(solution)/shard_map/ppermute | solution.py:39
  616.3 5.2 grad_in.15
  (554 shorter events, 322.9 us)
Async XLA Ops:
  7.2 54.7 %all-gather.11.cloned.1.call-start = ((), (), s32[]{:S(2)}) async-start(), calls=%async_computation.9 | async-start | bytes 4718592 | tf_op jit(solution)/shard_map/all_gather | solution.py:1380
  7.9 126.9 %all-gather.9.cloned.1.call-start = ((), (), s32[]{:S(2)}) async-start(), calls=%async_computation.8 | async-start | bytes 4718592 | tf_op jit(solution)/shard_map/all_gather | solution.py:1380
  13.0 200.1 %reduce-scatter.5.cloned.1.call-start = ((), (), s32[]{:S(2)}) async-start(), calls=%async_computation.4 | async-start | bytes 2621440 | tf_op jit(solution)/shard_map/reduce_scatter | solution.py:1383
  35.4 24.4 %collective-permute-start.6 = (bf16[512,1024]{1,0:T(8,128)(2,1)}, bf16[512,1024]{1,0:T(8,128)(2,1)}, u32[]{:S(2)}, u32[]{:S(2)}) collective-permute-start(bf16[512,1024]{1,0:T(8,128)(2,1)} %join_weights.6.rest_0_.rest_3_), channel_id=1, source_target_pairs={{0,8},{8,0},{1,9},{9,1},{2,10},{10,2},{3,11},{11,3},{4,12},{12,4},... | collective-permute-start | bytes 3145736 | tf_op jit(solution)/shard_map/ppermute | solution.py:39
  59.8 52.1 %collective-permute-start.12 = (bf16[1280,512]{1,0:T(8,128)(2,1)S(1)}, bf16[1280,512]{1,0:T(8,128)(2,1)}, u32[]{:S(2)}, u32[]{:S(2)}) collective-permute-start(bf16[1280,512]{1,0:T(8,128)(2,1)S(1)} %join_weights.7.rest_2_.rest_0_), channel_id=1, source_target_pairs={{0,16},{16,0},{1,17},{17,1},{2,18},{18,2},{3,19},{19,3},{4,20},{20... | collective-permute-start | bytes 3932168 | tf_op jit(solution)/shard_map/ppermute | solution.py:39
  60.7 51.1 %collective-permute-start.13 = (bf16[1280,512]{1,0:T(8,128)(2,1)S(1)}, bf16[1280,512]{1,0:T(8,128)(2,1)}, u32[]{:S(2)}, u32[]{:S(2)}) collective-permute-start(bf16[1280,512]{1,0:T(8,128)(2,1)S(1)} %join_weights.7.rest_2_.rest_0_), channel_id=1, source_target_pairs={{0,8},{8,0},{1,9},{9,1},{2,10},{10,2},{3,11},{11,3},{4,12},{12,4},... | collective-permute-start | bytes 3932168 | tf_op jit(solution)/shard_map/ppermute | solution.py:39
  79.4 32.4 %collective-permute-start.14 = (bf16[1024,512]{1,0:T(8,128)(2,1)}, bf16[1024,512]{1,0:T(8,128)(2,1)}, u32[]{:S(2)}, u32[]{:S(2)}) collective-permute-start(bf16[1024,512]{1,0:T(8,128)(2,1)} %get-tuple-element.1355.kv_ref), channel_id=1, source_target_pairs={{0,8},{8,0},{1,9},{9,1},{2,10},{10,2},{3,11},{11,3},{4,12},{12,4},... | collective-permute-start | bytes 3145736 | tf_op jit(solution)/shard_map/ppermute | solution.py:39
  80.2 31.7 %collective-permute-start.11 = (bf16[512,1024]{1,0:T(8,128)(2,1)}, bf16[512,1024]{1,0:T(8,128)(2,1)}, u32[]{:S(2)}, u32[]{:S(2)}) collective-permute-start(bf16[512,1024]{1,0:T(8,128)(2,1)} %join_weights.6.rest_0_.rest_3_), channel_id=1, source_target_pairs={{0,16},{16,0},{1,17},{17,1},{2,18},{18,2},{3,19},{19,3},{4,20},{20... | collective-permute-start | bytes 3145736 | tf_op jit(solution)/shard_map/ppermute | solution.py:39
  111.9 28.3 %collective-permute-start.16 = (bf16[1280,512]{1,0:T(8,128)(2,1)}, bf16[1280,512]{1,0:T(8,128)(2,1)}, u32[]{:S(2)}, u32[]{:S(2)}) collective-permute-start(bf16[1280,512]{1,0:T(8,128)(2,1)} %collective-permute-done.12.rest_4_.rest_2_), channel_id=1, source_target_pairs={{0,8},{8,0},{1,9},{9,1},{2,10},{10,2},{3,11},{11,3},{4,12},{12,4},... | collective-permute-start | bytes 3932168 | tf_op jit(solution)/shard_map/ppermute | solution.py:39
  140.2 28.3 %collective-permute-start.21 = (bf16[1280,512]{1,0:T(8,128)(2,1)}, bf16[1280,512]{1,0:T(8,128)(2,1)}, u32[]{:S(2)}, u32[]{:S(2)}) collective-permute-start(bf16[1280,512]{1,0:T(8,128)(2,1)} %copy-done.40), channel_id=1, source_target_pairs={{0,16},{16,0},{1,17},{17,1},{2,18},{18,2},{3,19},{19,3},{4,20},{20... | collective-permute-start | bytes 3932168 | tf_op jit(solution)/shard_map/ppermute | solution.py:39
  141.2 27.4 %collective-permute-start.22 = (bf16[1280,512]{1,0:T(8,128)(2,1)}, bf16[1280,512]{1,0:T(8,128)(2,1)}, u32[]{:S(2)}, u32[]{:S(2)}) collective-permute-start(bf16[1280,512]{1,0:T(8,128)(2,1)} %copy-done.40), channel_id=1, source_target_pairs={{0,8},{8,0},{1,9},{9,1},{2,10},{10,2},{3,11},{11,3},{4,12},{12,4},... | collective-permute-start | bytes 3932168 | tf_op jit(solution)/shard_map/ppermute | solution.py:39
  168.6 105.4 %all-gather.13.cloned.1.call-start = ((), (), s32[]{:S(2)}) async-start(), calls=%async_computation.10 | async-start | bytes 4718592 | tf_op jit(solution)/shard_map/all_gather | solution.py:1380
  168.6 42.1 %collective-permute-start.25 = (bf16[512,1792]{1,0:T(8,128)(2,1)S(1)}, bf16[512,1792]{1,0:T(8,128)(2,1)S(1)}, u32[]{:S(2)}, u32[]{:S(2)}) collective-permute-start(bf16[512,1792]{1,0:T(8,128)(2,1)S(1)} %join_weights.8.rest_0_.rest_2_), channel_id=1, source_target_pairs={{0,8},{8,0},{1,9},{9,1},{2,10},{10,2},{3,11},{11,3},{4,12},{12,4},... | collective-permute-start | bytes 5505032 | tf_op jit(solution)/shard_map/ppermute | solution.py:39
  169.3 42.6 %collective-permute-start.26 = (bf16[512,1792]{1,0:T(8,128)(2,1)S(1)}, bf16[512,1792]{1,0:T(8,128)(2,1)S(1)}, u32[]{:S(2)}, u32[]{:S(2)}) collective-permute-start(bf16[512,1792]{1,0:T(8,128)(2,1)S(1)} %join_weights.8.rest_0_.rest_2_), channel_id=1, source_target_pairs={{0,16},{16,0},{1,17},{17,1},{2,18},{18,2},{3,19},{19,3},{4,20},{20... | collective-permute-start | bytes 5505032 | tf_op jit(solution)/shard_map/ppermute | solution.py:39
  226.5 194.7 %reduce-scatter.7.cloned.1.call-start = ((), (), s32[]{:S(2)}) async-start(), calls=%async_computation.5 | async-start | bytes 2621440 | tf_op jit(solution)/shard_map/reduce_scatter | solution.py:1383
  226.6 46.1 %collective-permute-start.30 = (bf16[512,1792]{1,0:T(8,128)(2,1)}, bf16[512,1792]{1,0:T(8,128)(2,1)S(1)}, u32[]{:S(2)}, u32[]{:S(2)}) collective-permute-start(bf16[512,1792]{1,0:T(8,128)(2,1)} %copy-done.26), channel_id=1, source_target_pairs={{0,16},{16,0},{1,17},{17,1},{2,18},{18,2},{3,19},{19,3},{4,20},{20... | collective-permute-start | bytes 5505032 | tf_op jit(solution)/shard_map/ppermute | solution.py:39
  226.8 28.6 %collective-permute-start.31 = (bf16[1280,512]{1,0:T(8,128)(2,1)}, bf16[1280,512]{1,0:T(8,128)(2,1)S(1)}, u32[]{:S(2)}, u32[]{:S(2)}) collective-permute-start(bf16[1280,512]{1,0:T(8,128)(2,1)} %collective-permute-done.21.rest_2_.rest_4_), channel_id=1, source_target_pairs={{0,8},{8,0},{1,9},{9,1},{2,10},{10,2},{3,11},{11,3},{4,12},{12,4},... | collective-permute-start | bytes 3932168 | tf_op jit(solution)/shard_map/ppermute | solution.py:39
  315.7 44.4 %collective-permute-start.34 = (bf16[1024,1024]{1,0:T(8,128)(2,1)S(1)}, bf16[1024,1024]{1,0:T(8,128)(2,1)S(1)}, u32[]{:S(2)}, u32[]{:S(2)}) collective-permute-start(bf16[1024,1024]{1,0:T(8,128)(2,1)S(1)} %grad_in.8), channel_id=1, source_target_pairs={{0,16},{16,0},{1,17},{17,1},{2,18},{18,2},{3,19},{19,3},{4,20},{20... | collective-permute-start | bytes 6291464 | tf_op jit(solution)/shard_map/ppermute | solution.py:39
  377.8 108.2 %all-gather.15.cloned.1.call-start = ((), (), s32[]{:S(2)}) async-start(), calls=%async_computation.11 | async-start | bytes 4718592 | tf_op jit(solution)/shard_map/all_gather | solution.py:1380
  377.8 31.1 %collective-permute-start.39 = (bf16[1280,512]{1,0:T(8,128)(2,1)}, bf16[1280,512]{1,0:T(8,128)(2,1)}, u32[]{:S(2)}, u32[]{:S(2)}) collective-permute-start(bf16[1280,512]{1,0:T(8,128)(2,1)} %copy-done.109), channel_id=1, source_target_pairs={{0,8},{8,0},{1,9},{9,1},{2,10},{10,2},{3,11},{11,3},{4,12},{12,4},... | collective-permute-start | bytes 3932168 | tf_op jit(solution)/shard_map/ppermute | solution.py:39
  396.1 38.4 %collective-permute-start.41 = (bf16[1024,768]{1,0:T(8,128)(2,1)}, bf16[1024,768]{1,0:T(8,128)(2,1)}, u32[]{:S(2)}, u32[]{:S(2)}) collective-permute-start(bf16[1024,768]{1,0:T(8,128)(2,1)} %grad_in.9), channel_id=1, source_target_pairs={{0,16},{16,0},{1,17},{17,1},{2,18},{18,2},{3,19},{19,3},{4,20},{20... | collective-permute-start | bytes 4718600 | tf_op jit(solution)/shard_map/ppermute | solution.py:39
  409.0 30.2 %collective-permute-start.40 = (bf16[1280,512]{1,0:T(8,128)(2,1)}, bf16[1280,512]{1,0:T(8,128)(2,1)}, u32[]{:S(2)}, u32[]{:S(2)}) collective-permute-start(bf16[1280,512]{1,0:T(8,128)(2,1)} %get-tuple-element.1231), channel_id=1, source_target_pairs={{0,8},{8,0},{1,9},{9,1},{2,10},{10,2},{3,11},{11,3},{4,12},{12,4},... | collective-permute-start | bytes 3932168 | tf_op jit(solution)/shard_map/ppermute | solution.py:39
  439.2 154.3 %reduce-scatter.9.cloned.1.call-start = ((), (), s32[]{:S(2)}) async-start(), calls=%async_computation.6 | async-start | bytes 2621440 | tf_op jit(solution)/shard_map/reduce_scatter | solution.py:1383
  449.8 28.6 %collective-permute-start.47 = (bf16[1280,512]{1,0:T(8,128)(2,1)S(1)}, bf16[1280,512]{1,0:T(8,128)(2,1)S(1)}, u32[]{:S(2)}, u32[]{:S(2)}) collective-permute-start(bf16[1280,512]{1,0:T(8,128)(2,1)S(1)} %get-tuple-element.1270), channel_id=1, source_target_pairs={{0,16},{16,0},{1,17},{17,1},{2,18},{18,2},{3,19},{19,3},{4,20},{20... | collective-permute-start | bytes 3932168 | tf_op jit(solution)/shard_map/ppermute | solution.py:39
  486.0 138.4 %reduce-scatter.11.cloned.1.call-start = ((), (), s32[]{:S(2)}) async-start(), calls=%async_computation.7 | async-start | bytes 2621440 | tf_op jit(solution)/shard_map/reduce_scatter | solution.py:1383
  492.8 53.9 %collective-permute-start.51 = (bf16[1280,512]{1,0:T(8,128)(2,1)S(1)}, bf16[1280,512]{1,0:T(8,128)(2,1)S(1)}, u32[]{:S(2)}, u32[]{:S(2)}) collective-permute-start(bf16[1280,512]{1,0:T(8,128)(2,1)S(1)} %get-tuple-element.1323), channel_id=1, source_target_pairs={{0,8},{8,0},{1,9},{9,1},{2,10},{10,2},{3,11},{11,3},{4,12},{12,4},... | collective-permute-start | bytes 3932168 | tf_op jit(solution)/shard_map/ppermute | solution.py:39
  521.6 25.1 %collective-permute-start.50 = (bf16[1024,512]{1,0:T(8,128)(2,1)S(1)}, bf16[1024,512]{1,0:T(8,128)(2,1)S(1)}, u32[]{:S(2)}, u32[]{:S(2)}) collective-permute-start(bf16[1024,512]{1,0:T(8,128)(2,1)S(1)} %get-tuple-element.1346), channel_id=1, source_target_pairs={{0,8},{8,0},{1,9},{9,1},{2,10},{10,2},{3,11},{11,3},{4,12},{12,4},... | collective-permute-start | bytes 3145736 | tf_op jit(solution)/shard_map/ppermute | solution.py:39
  526.0 47.5 %collective-permute-start.53 = (bf16[1024,1024]{1,0:T(8,128)(2,1)S(1)}, bf16[1024,1024]{1,0:T(8,128)(2,1)S(1)}, u32[]{:S(2)}, u32[]{:S(2)}) collective-permute-start(bf16[1024,1024]{1,0:T(8,128)(2,1)S(1)} %grad_in.12), channel_id=1, source_target_pairs={{0,16},{16,0},{1,17},{17,1},{2,18},{18,2},{3,19},{19,3},{4,20},{20... | collective-permute-start | bytes 6291464 | tf_op jit(solution)/shard_map/ppermute | solution.py:39
  546.7 29.8 %collective-permute-start.54 = (bf16[1280,512]{1,0:T(8,128)(2,1)S(1)}, bf16[1280,512]{1,0:T(8,128)(2,1)S(1)}, u32[]{:S(2)}, u32[]{:S(2)}) collective-permute-start(bf16[1280,512]{1,0:T(8,128)(2,1)S(1)} %get-tuple-element.1409), channel_id=1, source_target_pairs={{0,8},{8,0},{1,9},{9,1},{2,10},{10,2},{3,11},{11,3},{4,12},{12,4},... | collective-permute-start | bytes 3932168 | tf_op jit(solution)/shard_map/ppermute | solution.py:39
  580.1 34.8 %collective-permute-start.57 = (bf16[1024,768]{1,0:T(8,128)(2,1)}, bf16[1024,768]{1,0:T(8,128)(2,1)}, u32[]{:S(2)}, u32[]{:S(2)}) collective-permute-start(bf16[1024,768]{1,0:T(8,128)(2,1)} %copy-done.80), channel_id=1, source_target_pairs={{0,16},{16,0},{1,17},{17,1},{2,18},{18,2},{3,19},{19,3},{4,20},{20... | collective-permute-start | bytes 4718600 | tf_op jit(solution)/shard_map/ppermute | solution.py:39
  592.2 30.4 %collective-permute-start.58 = (bf16[512,1024]{1,0:T(8,128)(2,1)}, bf16[512,1024]{1,0:T(8,128)(2,1)}, u32[]{:S(2)}, u32[]{:S(2)}) collective-permute-start(bf16[512,1024]{1,0:T(8,128)(2,1)} %get-tuple-element.1438), channel_id=1, source_target_pairs={{0,8},{8,0},{1,9},{9,1},{2,10},{10,2},{3,11},{11,3},{4,12},{12,4},... | collective-permute-start | bytes 3145736 | tf_op jit(solution)/shard_map/ppermute | solution.py:39
  614.9 28.1 %collective-permute-start.64 = (bf16[1280,512]{1,0:T(8,128)(2,1)}, bf16[1280,512]{1,0:T(8,128)(2,1)S(1)}, u32[]{:S(2)}, u32[]{:S(2)}) collective-permute-start(bf16[1280,512]{1,0:T(8,128)(2,1)} %get-tuple-element.1462), channel_id=1, source_target_pairs={{0,16},{16,0},{1,17},{17,1},{2,18},{18,2},{3,19},{19,3},{4,20},{20... | collective-permute-start | bytes 3932168 | tf_op jit(solution)/shard_map/ppermute | solution.py:39
  (178 other events, 1757.0 us)
Sparse Core Ops, SparseCore 0:
  9.6 50.1 all-gather.10
  61.4 45.7 all-gather.8
  168.7 44.0 reduce-scatter.4
  226.6 44.0 all-gather.12
  377.9 43.2 reduce-scatter.6
  439.4 46.5 all-gather.14
  488.3 42.5 reduce-scatter.8
  580.2 42.5 reduce-scatter.10
